TPU v7x, 32 devices: a whole 2x2x4 slice. The times are simulated.
32 devices in a mesh: seq: 8 (over z, x), batch: 4 (over y, core).
Axes of the slice: x: 2, y: 2, z: 4, core: 2. Of those that a mesh axis runs over, the one named last changes fastest.
Arguments:
- tokens: bfloat16 [4, 4096, 768], P('batch', 'seq'), may hold values from -6 to 6
- global_states: bfloat16 [4, 128, 768], P('batch'), may hold values from -6 to 6
- token_seg: int32 [4, 4096], P('batch', 'seq'), may hold values from 0 to 2, as said below
- global_seg: int32 [4, 128], P('batch'), may hold values from 0 to 2, as said below
- attn_gain: float32 [768], replicated, may hold values from 0.1 to 1.9
- attn_shift: float32 [768], replicated, may hold values from -4 to 4
- glob_gain: float32 [768], replicated, may hold values from 0.1 to 1.9
- glob_shift: float32 [768], replicated, may hold values from -4 to 4
- w_qkv: bfloat16 [768, 2304], replicated, may hold values from -0.21875 to 0.21875
- w_out: bfloat16 [768, 768], replicated, may hold values from -2.5 to 2.5
- ffn_gain: float32 [768], replicated, may hold values from 0.1 to 1.9
- ffn_shift: float32 [768], replicated, may hold values from -4 to 4
- w_up: bfloat16 [768, 3072], replicated, may hold values from -0.21875 to 0.21875
- up_bias: float32 [3072], replicated, may hold values from -6 to 6
- w_down: bfloat16 [3072, 768], replicated, may hold values from -0.109375 to 0.109375
- down_bias: float32 [768], replicated, may hold values from -4 to 4
- out_cotangent: bfloat16 [4, 4096, 768], P('batch', 'seq'), may hold values from -6 to 6
- global_cotangent: bfloat16 [4, 128, 768], P('batch'), may hold values from -6 to 6
Outputs:
- staggered_out: bfloat16 [4, 4096, 768], P('batch', 'seq')
- global_out: bfloat16 [4, 128, 768], P('batch')
- token_grad: bfloat16 [4, 4096, 768], P('batch', 'seq')
- global_grad: bfloat16 [4, 128, 768], P('batch')
- grad_attn_gain: float32 [768], P('seq')
- grad_attn_shift: float32 [768], P('seq')
- grad_glob_gain: float32 [768], P('seq')
- grad_glob_shift: float32 [768], P('seq')
- grad_w_qkv: float32 [768, 2304], P('seq', 'batch')
- grad_w_out: float32 [768, 768], P('seq', 'batch')
- grad_ffn_gain: float32 [768], P('seq')
- grad_ffn_shift: float32 [768], P('seq')
- grad_w_up: float32 [768, 3072], P('seq', 'batch')
- grad_up_bias: float32 [3072], P('seq')
- grad_w_down: float32 [3072, 768], P('seq', 'batch')
- grad_down_bias: float32 [768], P('seq')
Inputs may be any that keep to these rules, and one draw needn't show every extreme that they name: `token_seg`: in input order each row holds three documents with ids 0, 1, 2 in turn; document 1 begins within the row's first 256 tokens and ends within its last 256; entry p holds the id of input position (p + 256) mod 4096. `global_seg`: the document that each global slot serves.
All inputs are finite; a program needn't handle non-finite values.
Results may differ from a plain program's by a relative error of at most 0.014.
Values may be sent and summed in bfloat16 or wider, within the bound.
A program may use at most 192 MiB of HBM per device.

v0:
```python
import jax
import jax.numpy as jnp
from jax import lax
from jax.sharding import PartitionSpec as P

HEADS = 12
HEAD_DIM = 64
BLOCK = 512


EPS = 1e-05
NEGATIVE = -1e30


def from_behind(block, axis, distance):
    devices = range(lax.axis_size(axis))
    route = [((i - distance) % len(devices), i) for i in devices]
    return lax.ppermute(block, axis, route)


def norm_rows(source, scaling, offset):
    center = jnp.mean(source, axis=-1, keepdims=True)
    spread = source - center
    variance = jnp.mean(spread * spread, axis=-1, keepdims=True)
    return spread * lax.rsqrt(variance + EPS) * scaling + offset


def norm_back(source, scaling, offset, upstream):
    _, pullback = jax.vjp(norm_rows, source, scaling, offset)
    return pullback(upstream)


def project(former, latter):
    return jnp.einsum("rsd,de->rse", former, latter, preferred_element_type=jnp.float32)


def project_back(former, latter):
    return jnp.einsum("rse,de->rsd", former, latter, preferred_element_type=jnp.float32)


def outer_sum(former, latter):
    return jnp.einsum("rsd,rse->de", former, latter, preferred_element_type=jnp.float32)


def gelu_exact(hidden):
    return jax.nn.gelu(hidden, approximate=False)


def ffn_forward(state, ffn_gain, ffn_shift, w_up, up_bias, w_down, down_bias):
    normed = norm_rows(state, ffn_gain, ffn_shift).astype(jnp.bfloat16)
    hidden = project(normed, w_up) + up_bias
    active = gelu_exact(hidden).astype(jnp.bfloat16)
    result = state + project(active, w_down) + down_bias
    return (result, (normed, hidden, active))


def ffn_backward(state, stored, upstream, ffn_gain, ffn_shift, w_up, w_down):
    normed, hidden, active = stored
    upstream_low = upstream.astype(jnp.bfloat16)
    grad_down = outer_sum(active, upstream_low)
    grad_down_bias = jnp.sum(upstream, axis=(0, 1))
    grad_active = project_back(upstream_low, w_down)
    _, gelu_pull = jax.vjp(gelu_exact, hidden)
    grad_hidden = gelu_pull(grad_active)[0].astype(jnp.bfloat16)
    grad_up = outer_sum(normed, grad_hidden)
    grad_up_bias = jnp.sum(grad_hidden.astype(jnp.float32), axis=(0, 1))
    grad_normed = project_back(grad_hidden, w_up)
    grad_state, grad_gain, grad_shift = norm_back(state, ffn_gain, ffn_shift, grad_normed)
    return (
        upstream + grad_state,
        (grad_gain, grad_shift, grad_up, grad_up_bias, grad_down, grad_down_bias),
    )


def local_scores(queries, keys_near, seg_near, keys_far, seg_far):
    scaling = HEAD_DIM ** (-0.5)
    near_scores = (
        jnp.einsum("rnqhd,rnkhd->rnhqk", queries, keys_near, preferred_element_type=jnp.float32)
        * scaling
    )
    far_scores = (
        jnp.einsum("rnqhd,rghd->rnhqg", queries, keys_far, preferred_element_type=jnp.float32)
        * scaling
    )
    near_open = (seg_near[:, :, :, None] == seg_near[:, :, None, :])[:, :, None]
    far_open = (seg_near[:, :, :, None] == seg_far[:, None, None, :])[:, :, None]
    return (jnp.where(near_open, near_scores, NEGATIVE), jnp.where(far_open, far_scores, NEGATIVE))


def local_forward(queries, keys_near, values_near, seg_near, keys_far, values_far, seg_far):
    near_scores, far_scores = local_scores(queries, keys_near, seg_near, keys_far, seg_far)
    maxima = jnp.maximum(jnp.max(near_scores, axis=-1), jnp.max(far_scores, axis=-1))
    near_exp = jnp.exp(near_scores - maxima[..., None])
    far_exp = jnp.exp(far_scores - maxima[..., None])
    totals = jnp.sum(near_exp, axis=-1) + jnp.sum(far_exp, axis=-1)
    near_weights = (near_exp / totals[..., None]).astype(jnp.bfloat16)
    far_weights = (far_exp / totals[..., None]).astype(jnp.bfloat16)
    mixed_out = jnp.einsum(
        "rnhqk,rnkhd->rnqhd", near_weights, values_near, preferred_element_type=jnp.float32
    )
    mixed_out = mixed_out + jnp.einsum(
        "rnhqg,rghd->rnqhd", far_weights, values_far, preferred_element_type=jnp.float32
    )
    return (mixed_out, maxima + jnp.log(totals))


def local_backward(
    queries, keys_near, values_near, seg_near, keys_far, values_far, seg_far, logsum, upstream
):
    scaling = HEAD_DIM ** (-0.5)
    near_scores, far_scores = local_scores(queries, keys_near, seg_near, keys_far, seg_far)
    near_weights = jnp.exp(near_scores - logsum[..., None])
    far_weights = jnp.exp(far_scores - logsum[..., None])
    near_grad = jnp.einsum(
        "rnqhd,rnkhd->rnhqk", upstream, values_near, preferred_element_type=jnp.float32
    )
    far_grad = jnp.einsum(
        "rnqhd,rghd->rnhqg", upstream, values_far, preferred_element_type=jnp.float32
    )
    row_inner = jnp.sum(near_weights * near_grad, axis=-1) + jnp.sum(
        far_weights * far_grad, axis=-1
    )
    near_score_grad = (near_weights * (near_grad - row_inner[..., None])).astype(jnp.bfloat16)
    far_score_grad = (far_weights * (far_grad - row_inner[..., None])).astype(jnp.bfloat16)
    grad_queries = jnp.einsum(
        "rnhqk,rnkhd->rnqhd", near_score_grad, keys_near, preferred_element_type=jnp.float32
    )
    grad_queries = scaling * (
        grad_queries
        + jnp.einsum(
            "rnhqg,rghd->rnqhd", far_score_grad, keys_far, preferred_element_type=jnp.float32
        )
    )
    grad_keys = scaling * jnp.einsum(
        "rnhqk,rnqhd->rnkhd", near_score_grad, queries, preferred_element_type=jnp.float32
    )
    grad_values = jnp.einsum(
        "rnhqk,rnqhd->rnkhd",
        near_weights.astype(jnp.bfloat16),
        upstream,
        preferred_element_type=jnp.float32,
    )
    grad_keys_far = scaling * jnp.einsum(
        "rnhqg,rnqhd->rghd", far_score_grad, queries, preferred_element_type=jnp.float32
    )
    grad_values_far = jnp.einsum(
        "rnhqg,rnqhd->rghd",
        far_weights.astype(jnp.bfloat16),
        upstream,
        preferred_element_type=jnp.float32,
    )
    return (grad_queries, grad_keys, grad_values, grad_keys_far, grad_values_far)


def global_scores(glob_queries, glob_keys, glob_seg, key_rows, seg_tokens):
    scaling = HEAD_DIM ** (-0.5)
    remote_scores = (
        jnp.einsum("rghd,rshd->rhgs", glob_queries, key_rows, preferred_element_type=jnp.float32)
        * scaling
    )
    own_scores = (
        jnp.einsum("rghd,rjhd->rhgj", glob_queries, glob_keys, preferred_element_type=jnp.float32)
        * scaling
    )
    remote_open = glob_seg[:, None, :, None] == seg_tokens[:, None, None, :]
    own_open = glob_seg[:, None, :, None] == glob_seg[:, None, None, :]
    return (
        jnp.where(remote_open, remote_scores, NEGATIVE),
        jnp.where(own_open, own_scores, NEGATIVE),
    )


def local(
    tokens,
    global_states,
    token_seg,
    global_seg,
    attn_gain,
    attn_shift,
    glob_gain,
    glob_shift,
    w_qkv,
    w_out,
    ffn_gain,
    ffn_shift,
    w_up,
    up_bias,
    w_down,
    down_bias,
    out_cotangent,
    global_cotangent,
):
    row_count, tok_count, model_width = tokens.shape
    glob_count = global_states.shape[1]
    half_block = BLOCK // 2
    block_count = tok_count // BLOCK
    seq_devices = lax.axis_size("seq")
    scaling = HEAD_DIM ** (-0.5)
    low_type = jnp.bfloat16
    arrived = from_behind(tokens[:, :half_block], "seq", -1)
    sectioned = jnp.concatenate([tokens[:, half_block:], arrived], axis=1).astype(jnp.float32)
    glob_state = global_states.astype(jnp.float32)
    normed = norm_rows(sectioned, attn_gain, attn_shift).astype(low_type)
    glob_normed = norm_rows(glob_state, glob_gain, glob_shift).astype(low_type)
    projected = (
        project(normed, w_qkv).astype(low_type).reshape(row_count, tok_count, 3, HEADS, HEAD_DIM)
    )
    glob_proj = (
        project(glob_normed, w_qkv)
        .astype(low_type)
        .reshape(row_count, glob_count, 3, HEADS, HEAD_DIM)
    )
    queries = projected[:, :, 0]
    key_rows = projected[:, :, 1]
    value_rows = projected[:, :, 2]
    glob_queries = glob_proj[:, :, 0]
    glob_keys = glob_proj[:, :, 1]
    glob_values = glob_proj[:, :, 2]
    block_shape = (row_count, block_count, BLOCK, HEADS, HEAD_DIM)
    block_queries = queries.reshape(block_shape)
    block_keys = key_rows.reshape(block_shape)
    block_values = value_rows.reshape(block_shape)
    block_seg = token_seg.reshape(row_count, block_count, BLOCK)
    local_out, local_logsum = local_forward(
        block_queries, block_keys, block_values, block_seg, glob_keys, glob_values, global_seg
    )
    remote_scores, own_scores = global_scores(
        glob_queries, glob_keys, global_seg, key_rows, token_seg
    )
    maxima = jnp.maximum(
        lax.pmax(jnp.max(remote_scores, axis=-1), "seq"), jnp.max(own_scores, axis=-1)
    )
    remote_total = jnp.sum(jnp.exp(remote_scores - maxima[..., None]), axis=-1)
    totals = lax.psum(remote_total, "seq") + jnp.sum(
        jnp.exp(own_scores - maxima[..., None]), axis=-1
    )
    remote_weights = (jnp.exp(remote_scores - maxima[..., None]) / totals[..., None]).astype(
        low_type
    )
    own_weights = (jnp.exp(own_scores - maxima[..., None]) / totals[..., None]).astype(low_type)
    remote_part = jnp.einsum(
        "rhgs,rshd->rghd", remote_weights, value_rows, preferred_element_type=jnp.float32
    )
    glob_out = lax.psum(remote_part, "seq")
    glob_out = glob_out + jnp.einsum(
        "rhgj,rjhd->rghd", own_weights, glob_values, preferred_element_type=jnp.float32
    )
    glob_logsum = maxima + jnp.log(totals)
    attended = local_out.reshape(row_count, tok_count, model_width).astype(low_type)
    glob_attended = glob_out.reshape(row_count, glob_count, model_width).astype(low_type)
    attn_sum = sectioned + project(attended, w_out)
    glob_sum = glob_state + project(glob_attended, w_out)
    result, stored = ffn_forward(attn_sum, ffn_gain, ffn_shift, w_up, up_bias, w_down, down_bias)
    glob_result, glob_stored = ffn_forward(
        glob_sum, ffn_gain, ffn_shift, w_up, up_bias, w_down, down_bias
    )
    grad_attn_sum, tok_ffn = ffn_backward(
        attn_sum, stored, out_cotangent.astype(jnp.float32), ffn_gain, ffn_shift, w_up, w_down
    )
    grad_glob_sum, glob_ffn = ffn_backward(
        glob_sum,
        glob_stored,
        global_cotangent.astype(jnp.float32),
        ffn_gain,
        ffn_shift,
        w_up,
        w_down,
    )
    branch_low = grad_attn_sum.astype(low_type)
    glob_branch_low = grad_glob_sum.astype(low_type)
    grad_out_all = (
        outer_sum(attended, branch_low) + outer_sum(glob_attended, glob_branch_low) / seq_devices
    )
    upstream_mix = project_back(branch_low, w_out).astype(low_type).reshape(block_shape)
    glob_upstream = (
        project_back(glob_branch_low, w_out)
        .astype(low_type)
        .reshape(row_count, glob_count, HEADS, HEAD_DIM)
    )
    remote_exact = jnp.exp(remote_scores - glob_logsum[..., None])
    own_exact = jnp.exp(own_scores - glob_logsum[..., None])
    remote_grad = jnp.einsum(
        "rghd,rshd->rhgs", glob_upstream, value_rows, preferred_element_type=jnp.float32
    )
    own_grad = jnp.einsum(
        "rghd,rjhd->rhgj", glob_upstream, glob_values, preferred_element_type=jnp.float32
    )
    row_inner = lax.psum(jnp.sum(remote_exact * remote_grad, axis=-1), "seq")
    row_inner = row_inner + jnp.sum(own_exact * own_grad, axis=-1)
    remote_score_grad = (remote_exact * (remote_grad - row_inner[..., None])).astype(low_type)
    own_score_grad = (own_exact * (own_grad - row_inner[..., None])).astype(low_type)
    remote_queries = scaling * jnp.einsum(
        "rhgs,rshd->rghd", remote_score_grad, key_rows, preferred_element_type=jnp.float32
    )
    tok_keys_extra = scaling * jnp.einsum(
        "rhgs,rghd->rshd", remote_score_grad, glob_queries, preferred_element_type=jnp.float32
    )
    tok_values_extra = jnp.einsum(
        "rhgs,rghd->rshd",
        remote_exact.astype(low_type),
        glob_upstream,
        preferred_element_type=jnp.float32,
    )
    own_queries = scaling * jnp.einsum(
        "rhgj,rjhd->rghd", own_score_grad, glob_keys, preferred_element_type=jnp.float32
    )
    own_keys = scaling * jnp.einsum(
        "rhgj,rghd->rjhd", own_score_grad, glob_queries, preferred_element_type=jnp.float32
    )
    own_values = jnp.einsum(
        "rhgj,rghd->rjhd",
        own_exact.astype(low_type),
        glob_upstream,
        preferred_element_type=jnp.float32,
    )
    grad_queries, grad_keys, grad_values, grad_keys_far, grad_values_far = local_backward(
        block_queries,
        block_keys,
        block_values,
        block_seg,
        glob_keys,
        glob_values,
        global_seg,
        local_logsum,
        upstream_mix,
    )
    far_grads = lax.psum((remote_queries, grad_keys_far, grad_values_far), "seq")
    head_shape = (row_count, tok_count, HEADS, HEAD_DIM)
    grad_projected = jnp.stack(
        [
            grad_queries.reshape(head_shape),
            grad_keys.reshape(head_shape) + tok_keys_extra,
            grad_values.reshape(head_shape) + tok_values_extra,
        ],
        axis=2,
    )
    grad_projected = grad_projected.reshape(row_count, tok_count, 3 * model_width).astype(low_type)
    glob_grad_projected = jnp.stack(
        [far_grads[0] + own_queries, far_grads[1] + own_keys, far_grads[2] + own_values], axis=2
    )
    glob_grad_projected = glob_grad_projected.reshape(
        row_count, glob_count, 3 * model_width
    ).astype(low_type)
    grad_qkv_all = (
        outer_sum(normed, grad_projected)
        + outer_sum(glob_normed, glob_grad_projected) / seq_devices
    )
    grad_normed = project_back(grad_projected, w_qkv)
    glob_grad_normed = project_back(glob_grad_projected, w_qkv)
    grad_sectioned, attn_gain_grad, attn_shift_grad = norm_back(
        sectioned, attn_gain, attn_shift, grad_normed
    )
    grad_sectioned = grad_sectioned + grad_attn_sum
    glob_grad_state, glob_gain_grad, glob_shift_grad = norm_back(
        glob_state, glob_gain, glob_shift, glob_grad_normed
    )
    global_grad = (glob_grad_state + grad_glob_sum).astype(low_type)
    grad_low = grad_sectioned.astype(low_type)
    returned = from_behind(grad_low[:, tok_count - half_block :], "seq", 1)
    token_grad = jnp.concatenate([returned, grad_low[:, : tok_count - half_block]], axis=1)
    ffn_gain_all = tok_ffn[0] + glob_ffn[0] / seq_devices
    ffn_shift_all = tok_ffn[1] + glob_ffn[1] / seq_devices
    up_all = tok_ffn[2] + glob_ffn[2] / seq_devices
    up_bias_all = tok_ffn[3] + glob_ffn[3] / seq_devices
    down_all = tok_ffn[4] + glob_ffn[4] / seq_devices
    down_bias_all = tok_ffn[5] + glob_ffn[5] / seq_devices
    glob_gain_all = glob_gain_grad / seq_devices
    glob_shift_all = glob_shift_grad / seq_devices
    mat_sums = (
        lax.psum_scatter(
            grad_qkv_all.astype(jnp.bfloat16), "batch", scatter_dimension=1, tiled=True
        ).astype(jnp.float32),
        lax.psum_scatter(
            grad_out_all.astype(jnp.bfloat16), "batch", scatter_dimension=1, tiled=True
        ).astype(jnp.float32),
        lax.psum_scatter(
            up_all.astype(jnp.bfloat16), "batch", scatter_dimension=1, tiled=True
        ).astype(jnp.float32),
        lax.psum_scatter(
            down_all.astype(jnp.bfloat16), "batch", scatter_dimension=1, tiled=True
        ).astype(jnp.float32),
    )
    vec_sums = (
        lax.psum(attn_gain_grad.astype(jnp.bfloat16), "batch").astype(jnp.float32),
        lax.psum(attn_shift_grad.astype(jnp.bfloat16), "batch").astype(jnp.float32),
        lax.psum(glob_gain_all.astype(jnp.bfloat16), "batch").astype(jnp.float32),
        lax.psum(glob_shift_all.astype(jnp.bfloat16), "batch").astype(jnp.float32),
        lax.psum(ffn_gain_all.astype(jnp.bfloat16), "batch").astype(jnp.float32),
        lax.psum(ffn_shift_all.astype(jnp.bfloat16), "batch").astype(jnp.float32),
        lax.psum(up_bias_all.astype(jnp.bfloat16), "batch").astype(jnp.float32),
        lax.psum(down_bias_all.astype(jnp.bfloat16), "batch").astype(jnp.float32),
    )
    shares = (
        lax.psum_scatter(vec_sums[0], "seq", scatter_dimension=0, tiled=True),
        lax.psum_scatter(vec_sums[1], "seq", scatter_dimension=0, tiled=True),
        lax.psum_scatter(vec_sums[2], "seq", scatter_dimension=0, tiled=True),
        lax.psum_scatter(vec_sums[3], "seq", scatter_dimension=0, tiled=True),
        lax.psum_scatter(mat_sums[0], "seq", scatter_dimension=0, tiled=True),
        lax.psum_scatter(mat_sums[1], "seq", scatter_dimension=0, tiled=True),
        lax.psum_scatter(vec_sums[4], "seq", scatter_dimension=0, tiled=True),
        lax.psum_scatter(vec_sums[5], "seq", scatter_dimension=0, tiled=True),
        lax.psum_scatter(mat_sums[2], "seq", scatter_dimension=0, tiled=True),
        lax.psum_scatter(vec_sums[6], "seq", scatter_dimension=0, tiled=True),
        lax.psum_scatter(mat_sums[3], "seq", scatter_dimension=0, tiled=True),
        lax.psum_scatter(vec_sums[7], "seq", scatter_dimension=0, tiled=True),
    )
    matrices = (shares[4], shares[5], shares[8], shares[10])
    vectors = (
        shares[0],
        shares[1],
        shares[2],
        shares[3],
        shares[6],
        shares[7],
        shares[9],
        shares[11],
    )
    return (
        result.astype(low_type),
        glob_result.astype(low_type),
        token_grad,
        global_grad,
        vectors[0],
        vectors[1],
        vectors[2],
        vectors[3],
        matrices[0],
        matrices[1],
        vectors[4],
        vectors[5],
        matrices[2],
        vectors[6],
        matrices[3],
        vectors[7],
    )


def solution(mesh):
    placed = (
        P("batch", "seq", None),
        P("batch", None, None),
        P("batch", "seq"),
        P("batch", None),
        P(),
        P(),
        P(),
        P(),
        P(),
        P(),
        P(),
        P(),
        P(),
        P(),
        P(),
        P(),
        P("batch", "seq", None),
        P("batch", None, None),
    )
    return jax.shard_map(
        local,
        mesh=mesh,
        in_specs=placed,
        out_specs=(
            P("batch", "seq", None),
            P("batch", None, None),
            P("batch", "seq", None),
            P("batch", None, None),
            P("seq"),
            P("seq"),
            P("seq"),
            P("seq"),
            P("seq", "batch"),
            P("seq", "batch"),
            P("seq"),
            P("seq"),
            P("seq", "batch"),
            P("seq"),
            P("seq", "batch"),
            P("seq"),
        ),
        check_vma=False,
    )
```

profile of v0, /device:TPU:2, one launch (start us, length us, event | category | flops | bytes accessed | tf_op | source)
XLA Modules:
  0.0 836.3 jit_solution(921198629861173681)
XLA Ops:
  54.9 21.7 %multiply_convert_fusion.1 = (bf16[512,3072]{1,0:T(8,128)(2,1)}, f32[512,3072]{1,0:T(8,128)}, f32[512,3072]{1,0:T(8,128)}) fusion(f32[3072]{0:T(1024)S(1)} %copy-done.103, bf16[768,3072]{1,0:T(8,128)(2,1)S(1)} %bitcast.412, f32[512,768]{1,0:T(8,128)S(1)} %get-tuple-element.120, f32[768]{0:T(1024)S(1)} %copy-done.98, f32[768]{0:T(1024)S(1)} %copy-done.64, ...), kind=kOutput, calls=%fused_computation.17 | convolution fusion | flops 2521694208 | bytes 22042624 | tf_op jit(solution)/shard_map/rsd,de->rse/dot_general | solution.py:34
  76.6 9.5 %convert_reduce_fusion = (f32[3072]{0:T(1024)}, bf16[512,3072]{1,0:T(8,128)(2,1)}) fusion(f32[512,3072]{1,0:T(8,128)} %get-tuple-element.103, bf16[3072,768]{1,0:T(8,128)(2,1)S(1)} %bitcast.418, bf16[1,512,768]{2,1,0:T(8,128)(2,1)S(1)} %copy-done.42, f32[512,3072]{1,0:T(8,128)} %get-tuple-element.121, f32[3072]{0:T(1024)S(1)} %copy-done.103), kind=kOutput, calls=%fused_computation.14 | convolution fusion | flops 2442654720 | bytes 21258240 | tf_op jit(solution)/shard_map/rse,de->rsd/dot_general | solution.py:38
  106.3 10.5 %multiply_reduce_fusion = (f32[12,512]{1,0:T(8,128)}, f32[12,512,512]{1,2,0:T(8,128)}) fusion(f32[12,512]{1,0:T(8,128)S(1)} %copy-done.54, f32[12,512,512]{1,2,0:T(8,128)} %copy-done.1, pred[512,512]{0,1:T(8,128)(4,1)S(1)} %copy-done.26, bf16[512,12,64]{0,2,1:T(8,128)(2,1)S(1)} %bitcast.393, bf16[1,512,3,12,64]{1,4,3,2,0:T(8,128)(2,1)S(1)} %bitcast.386), kind=kOutput, calls=%fused_computation.1 | convolution fusion | flops 418375680 | bytes 27058176 | tf_op jit(solution)/shard_map/rnqhd,rnkhd->rnhqk/dot_general | solution.py:114
  120.0 22.4 %pmax.7 = f32[1,12,128]{2,1,0:T(8,128)S(1)} all-reduce(f32[1,12,128]{2,1,0:T(8,128)S(1)} %bitcast.430), channel_id=1, replica_groups=mesh['seq'=8,'batch'=4] {'seq'}, use_global_device_ids=true, to_apply=%region_11.12 | all-reduce | flops 1536 | bytes 12288 | tf_op jit(solution)/shard_map/pmax | solution.py:231
  148.2 19.4 %psum.98 = f32[1,12,128]{2,1,0:T(8,128)} all-reduce(f32[1,12,128]{2,1,0:T(8,128)} %bitcast.432), channel_id=1, replica_groups=mesh['seq'=8,'batch'=4] {'seq'}, use_global_device_ids=true, to_apply=%region_14.15 | all-reduce | flops 1536 | bytes 12288 | tf_op jit(solution)/shard_map/psum | solution.py:234
  173.7 10.8 %multiply_convert_fusion = bf16[12,512,512]{1,2,0:T(8,128)(2,1)S(1)} fusion(f32[12,512,512]{1,2,0:T(8,128)} %get-tuple-element.136, f32[12,512]{1,0:T(8,128)S(1)} %add.325, f32[12,512]{1,0:T(8,128)} %get-tuple-element.94, f32[12,512,512]{1,2,0:T(8,128)} %copy-done.1, pred[512,512]{0,1:T(8,128)(4,1)} %broadcast_compare_fusion), kind=kLoop, calls=%fused_computation | loop fusion | flops 18874368 | bytes 31768576 | tf_op jit(solution)/shard_map/convert_element_type | solution.py:123
  192.8 48.9 %all-reduce.14.cloned.1.call-done = f32[1,128,12,64]{1,3,2,0:T(8,128)} async-done(((f32[1,128,12,64]{1,3,2,0:T(8,128)}), f32[1,128,12,64]{1,3,2,0:T(8,128)}) %all-reduce.14.cloned.1.call-update) | async-done | bytes 393232 | tf_op jit(solution)/shard_map/psum | solution.py:244
  244.3 8.2 multiply_convert_fusion.3
  270.0 19.3 %psum.100 = f32[1,12,128]{2,1,0:T(8,128)} all-reduce(f32[1,12,128]{2,1,0:T(8,128)S(1)} %bitcast.431), channel_id=1, replica_groups=mesh['seq'=8,'batch'=4] {'seq'}, use_global_device_ids=true, to_apply=%region_26.27 | all-reduce | flops 1536 | bytes 12288 | tf_op jit(solution)/shard_map/psum | solution.py:288
  299.3 6.5 fusion.99
  311.4 8.7 %fusion.59 = bf16[1,512,1,12,64]{1,4,3,2,0:T(8,128)(2,1)S(1)} fusion(f32[12,64,512]{2,1,0:T(8,128)} %fusion.32, bf16[512,12,64]{0,2,1:T(8,128)(2,1)} %bitcast.391, f32[12,512]{1,0:T(8,128)} %get-tuple-element.94, f32[12,512,512]{1,2,0:T(8,128)} %copy-done.1, pred[512,512]{0,1:T(8,128)(4,1)} %broadcast_compare_fusion), kind=kOutput, calls=%fused_computation.123 | convolution fusion | flops 416022528 | bytes 16015360 | tf_op jit(solution)/shard_map/rnhqk,rnqhd->rnkhd/dot_general | solution.py:137
  324.1 6.2 fusion.142
  330.3 46.8 %all-reduce.16.cloned.1.call-done = (f32[1,128,12,64]{1,3,2,0:T(8,128)}, f32[1,128,12,64]{1,3,2,0:T(8,128)}, f32[1,128,12,64]{1,3,2,0:T(8,128)}) async-done(((f32[1,128,12,64]{1,3,2,0:T(8,128)}, f32[1,128,12,64]{1,3,2,0:T(8,128)}, f32[1,128,12,64]{1,3,2,0:T(8,128)}), (f32[1,128,12,64]{1,3,2,0:T(8,128)}, f32[1,128,12,64]{1,3,2,0:T(8,128)}, f32[1,128,12,64]{1,3,2,0:T(8,128)})) %all-reduce.16.cloned.1.call-update) | async-done | bytes 1179664 | tf_op jit(solution)/shard_map/psum | solution.py:327
  381.7 6.1 add_convert_fusion.2
  408.6 39.0 %reduce-scatter.13.cloned.1.call-done = bf16[768,576]{0,1:T(8,128)(2,1)} async-done(((bf16[768,2304]{0,1:T(8,128)(2,1)}), bf16[768,576]{0,1:T(8,128)(2,1)}) %reduce-scatter.13.cloned.1.call-update) | async-done | bytes 884752 | tf_op jit(solution)/shard_map/reduce_scatter | solution.py:370
  450.1 47.7 %reduce-scatter.17.cloned.1.call-done = bf16[768,768]{1,0:T(8,128)(2,1)} async-done(((bf16[768,3072]{1,0:T(8,128)(2,1)}), bf16[768,768]{1,0:T(8,128)(2,1)}) %reduce-scatter.17.cloned.1.call-update) | async-done | bytes 1179664 | tf_op jit(solution)/shard_map/reduce_scatter | solution.py:376
  502.9 45.4 %reduce-scatter.21.cloned.1.call-done = bf16[3072,192]{0,1:T(8,128)(2,1)} async-done(((bf16[3072,768]{0,1:T(8,128)(2,1)}), bf16[3072,192]{0,1:T(8,128)(2,1)}) %reduce-scatter.21.cloned.1.call-update) | async-done | bytes 1179664 | tf_op jit(solution)/shard_map/reduce_scatter | solution.py:379
  551.3 7.2 fusion.56
  575.5 6.7 collective-permute-done.1
  594.8 10.9 %all-reduce.10 = (bf16[768]{0:T(1024)(128)(2,1)}, bf16[768]{0:T(1024)(128)(2,1)}, bf16[768]{0:T(1024)(128)(2,1)}, bf16[768]{0:T(1024)(128)(2,1)}, bf16[768]{0:T(...) all-reduce(bf16[768]{0:T(1024)(128)(2,1)} %get-tuple-element.66, ...), channel_id=1, replica_groups=mesh['seq'=8,'batch'=4] {'batch'}, use_global_device_ids=true, to_apply=%region_36.37 | all-reduce | flops 8448 | bytes 33792 | tf_op jit(solution)/shard_map/psum | solution.py:384
  605.7 36.5 %all-reduce.8 = (f32[768]{0:T(1024)}, f32[768]{0:T(1024)}, f32[768]{0:T(1024)}, f32[768]{0:T(1024)}, f32[768]{0:T(1024)}, /*index=5*/f32[768]{0:T(1024)}, f32[3072]{0:T(1024)S(1)}, f32[768]{0:T(1024)S(1)}) all-reduce(bf16[768]{0:T(1024)(128)(2,1)} %get-tuple-element.86, ...), channel_id=2, replica_groups=mesh['seq'=8,'batch'=4] {'seq'}, use_global_device_ids=true, to_apply=%region_37.38.clone | all-reduce | flops 8448 | bytes 50688
  650.9 34.2 %reduce-scatter.25.cloned.1.call-done = f32[96,576]{1,0:T(8,128)} async-done(((f32[768,576]{1,0:T(8,128)}), f32[96,576]{1,0:T(8,128)}) %reduce-scatter.25.cloned.1.call-update) | async-done | bytes 221200
  685.1 72.0 %reduce-scatter.19.cloned.1.call-done = f32[96,768]{1,0:T(8,128)} async-done(((f32[768,768]{1,0:T(8,128)}), f32[96,768]{1,0:T(8,128)}) %reduce-scatter.19.cloned.1.call-update) | async-done | bytes 294928 | tf_op jit(solution)/shard_map/reduce_scatter | solution.py:402
  757.2 72.1 %reduce-scatter.23.cloned.1.call-done = f32[384,192]{0,1:T(8,128)} async-done(((f32[3072,192]{0,1:T(8,128)}), f32[384,192]{0,1:T(8,128)}) %reduce-scatter.23.cloned.1.call-update) | async-done | bytes 294928 | tf_op jit(solution)/shard_map/reduce_scatter | solution.py:404
  (378 shorter events, 202.4 us)
Async XLA Ops:
  7.2 234.6 %all-reduce.14.cloned.1.call-start = ((), (), s32[]{:S(2)}) async-start(), calls=%async_computation.8 | async-start | bytes 786432 | tf_op jit(solution)/shard_map/psum | solution.py:244
  9.6 12.5 %collective-permute-start = (bf16[1,256,768]{2,1,0:T(8,128)(2,1)}, bf16[1,256,768]{2,1,0:T(8,128)(2,1)}, u32[]{:S(2)}, u32[]{:S(2)}) collective-permute-start(bf16[1,256,768]{2,1,0:T(8,128)(2,1)} %get-tuple-element.109), channel_id=1, source_target_pairs={{4,0},{8,4},{12,8},{16,12},{20,16},{24,20},{28,24},{0,28},{5,1},{9... | collective-permute-start | bytes 1179656 | tf_op jit(solution)/shard_map/ppermute | solution.py:18
  52.2 24.4 %slice-start.6 = ((s8[4718592]{0:T(1024)(128)(4,1)}), s8[4194304]{0:T(1024)(128)(4,1)S(1)}, s32[]{:S(2)}) async-start(s8[4718592]{0:T(1024)(128)(4,1)} %bitcast.417), calls=%async_computation.24 | async-start | bytes 8388608
  52.2 33.8 %slice-start.2 = ((s8[4718592]{0:T(1024)(128)(4,1)}), s8[4194304]{0:T(1024)(128)(4,1)S(1)}, s32[]{:S(2)}) async-start(s8[4718592]{0:T(1024)(128)(4,1)} %bitcast.413), calls=%async_computation.20 | async-start | bytes 8388608
  54.4 37.2 %copy-start.27 = (f32[512,768]{1,0:T(8,128)}, f32[512,768]{1,0:T(8,128)S(1)}, u32[]{:S(2)}) copy-start(f32[512,768]{1,0:T(8,128)S(1)} %get-tuple-element.120) | copy-start | bytes 4718596
  54.4 37.1 %copy-start.77 = (f32[512]{0:T(512)}, f32[512]{0:T(512)S(1)}, u32[]{:S(2)}) copy-start(f32[512]{0:T(512)S(1)} %broadcast_multiply_fusion) | copy-start | bytes 6148
  54.8 36.8 %copy-start.94 = (f32[512]{0:T(512)}, f32[512]{0:T(512)S(1)}, u32[]{:S(2)}) copy-start(f32[512]{0:T(512)S(1)} %fusion.130) | copy-start | bytes 6148
  54.8 21.7 %slice-start.7 = ((s8[4718592]{0:T(1024)(128)(4,1)}), s8[524288]{0:T(1024)(128)(4,1)S(1)}, s32[]{:S(2)}) async-start(s8[4718592]{0:T(1024)(128)(4,1)} %bitcast.417), calls=%async_computation.25 | async-start | bytes 1048576
  54.8 21.7 %copy-start.42 = (bf16[1,512,768]{2,1,0:T(8,128)(2,1)S(1)}, bf16[1,512,768]{2,1,0:T(8,128)(2,1)}, u32[]{:S(2)}) copy-start(bf16[1,512,768]{2,1,0:T(8,128)(2,1)} %param.34) | copy-start | bytes 2359300
  54.9 31.2 %slice-start.3 = ((s8[4718592]{0:T(1024)(128)(4,1)}), s8[524288]{0:T(1024)(128)(4,1)S(1)}, s32[]{:S(2)}) async-start(s8[4718592]{0:T(1024)(128)(4,1)} %bitcast.413), calls=%async_computation.21 | async-start | bytes 1048576
  172.8 204.3 %all-reduce.16.cloned.1.call-start = ((), (), s32[]{:S(2)}) async-start(), calls=%async_computation.17 | async-start | bytes 2359296 | tf_op jit(solution)/shard_map/psum | solution.py:327
  241.8 13.2 %slice-start.4 = ((s8[4718592]{0:T(1024)(128)(4,1)}), s8[4194304]{0:T(1024)(128)(4,1)S(1)}, s32[]{:S(2)}) async-start(s8[4718592]{0:T(1024)(128)(4,1)} %bitcast.415), calls=%async_computation.22 | async-start | bytes 8388608
  244.0 13.3 %copy-start.13 = (f32[1,128,768]{2,1,0:T(8,128)}, f32[1,128,768]{2,1,0:T(8,128)S(1)}, u32[]{:S(2)}) copy-start(f32[1,128,768]{2,1,0:T(8,128)S(1)} %get-tuple-element.127) | copy-start | bytes 1179652
  244.1 13.3 %copy-start.91 = (f32[128]{0:T(128)}, f32[128]{0:T(128)S(1)}, u32[]{:S(2)}) copy-start(f32[128]{0:T(128)S(1)} %broadcast_multiply_fusion.2) | copy-start | bytes 1540
  297.0 109.4 %reduce-scatter.15.cloned.1.call-start = ((), (), s32[]{:S(2)}) async-start(), calls=%async_computation.10 | async-start | bytes 1474560 | tf_op jit(solution)/shard_map/reduce_scatter | solution.py:373
  311.3 136.2 %reduce-scatter.13.cloned.1.call-start = ((), (), s32[]{:S(2)}) async-start(), calls=%async_computation.9 | async-start | bytes 4423680 | tf_op jit(solution)/shard_map/reduce_scatter | solution.py:370
  387.8 110.0 %reduce-scatter.17.cloned.1.call-start = ((), (), s32[]{:S(2)}) async-start(), calls=%async_computation.11 | async-start | bytes 5898240 | tf_op jit(solution)/shard_map/reduce_scatter | solution.py:376
  397.7 150.5 %reduce-scatter.21.cloned.1.call-start = ((), (), s32[]{:S(2)}) async-start(), calls=%async_computation.13 | async-start | bytes 5898240 | tf_op jit(solution)/shard_map/reduce_scatter | solution.py:379
  406.4 244.5 %reduce-scatter.27.cloned.1.call-start = ((), (), s32[]{:S(2)}) async-start(), calls=%async_computation.16 | async-start | bytes 884736
  408.5 276.6 %reduce-scatter.25.cloned.1.call-start = ((), (), s32[]{:S(2)}) async-start(), calls=%async_computation.15 | async-start | bytes 2211840
  450.1 50.9 %copy-start.106 = (u32[32]{0:T(128)S(1)}, u32[32]{0:T(128)}, u32[]{:S(2)}) copy-start(u32[32]{0:T(128)} %constant.34) | copy-start | bytes 388
  450.1 307.1 %reduce-scatter.19.cloned.1.call-start = ((), (), s32[]{:S(2)}) async-start(), calls=%async_computation.12 | async-start | bytes 2654208 | tf_op jit(solution)/shard_map/reduce_scatter | solution.py:402
  500.7 328.5 %reduce-scatter.23.cloned.1.call-start = ((), (), s32[]{:S(2)}) async-start(), calls=%async_computation.14 | async-start | bytes 2654208 | tf_op jit(solution)/shard_map/reduce_scatter | solution.py:404
  569.9 12.3 %collective-permute-start.1 = (bf16[1,256,768]{2,1,0:T(8,128)(2,1)S(1)}, bf16[1,256,768]{2,1,0:T(8,128)(2,1)S(1)}, u32[]{:S(2)}, u32[]{:S(2)}) collective-permute-start(bf16[1,256,768]{2,1,0:T(8,128)(2,1)S(1)} %get-tuple-element.106), channel_id=1, source_target_pairs={{28,0},{0,4},{4,8},{8,12},{12,16},{16,20},{20,24},{24,28},{29,1},{... | collective-permute-start | bytes 1179656 | tf_op jit(solution)/shard_map/ppermute | solution.py:18
  (105 other events, 487.6 us)
Sparse Core Ops, SparseCore 0:
  172.9 68.7 all-reduce.13
  297.1 79.9 all-reduce.15
  379.7 24.7 reduce-scatter.14
  407.1 40.4 reduce-scatter.12
  449.9 47.8 reduce-scatter.16
  500.4 47.8 reduce-scatter.20
  552.1 63.2 reduce-scatter.26
  619.9 65.2 reduce-scatter.24
  689.2 67.9 reduce-scatter.18
  761.1 68.1 reduce-scatter.22
where the time goes:
time: 844 us; the launch traced here: 836 us
  waiting for transfers between devices  413 us (49%)
  matrix products  194 us (23%)
  blocking collectives  108 us (13%)
  other arithmetic  60.9 us (7%)
  local copies, waits for them, and re-layouts  39.8 us (5%)
  between operations  17.1 us (2%)
    reduce_scatter x1, waiting for transfers between devices, local(): lax.psum_scatter(mat_sums[3], 'seq', scatter_dimension=0, tiled=True)  72.1 us
    reduce_scatter x1, waiting for transfers between devices, local(): lax.psum_scatter(mat_sums[2], 'seq', scatter_dimension=0, tiled=True)  72 us
    dot_general x8, matrix products, project(): jnp.einsum('rsd,de->rse', former, latter, preferred_element_type=jnp.floa...  49.8 us
    psum x1, waiting for transfers between devices, local(): glob_out = lax.psum(remote_part, 'seq')  48.9 us
    reduce_scatter x1, waiting for transfers between devices, local(): lax.psum_scatter(up_all.astype(jnp.bfloat16), 'batch', scatter_dimension=...  47.7 us
    psum x1, waiting for transfers between devices, local(): lax.psum((remote_queries, grad_keys_far, grad_values_far), 'seq')  46.8 us
    reduce_scatter x1, waiting for transfers between devices, local(): lax.psum_scatter(down_all.astype(jnp.bfloat16), 'batch', scatter_dimensio...  45.4 us
    reduce_scatter x1, waiting for transfers between devices, local(): lax.psum_scatter(grad_qkv_all.astype(jnp.bfloat16), 'batch', scatter_dime...  39 us
  transfers between devices with their start and end apart: 12, of which 9 were waited for; matrix products, arithmetic and copies ran while one was open for 17% of the time, Pallas kernels for 0%

commit v1 on v0

--- a/solution.py
+++ b/solution.py
@@ -1,6 +1,10 @@
+import functools
+
 import jax
 import jax.numpy as jnp
 from jax import lax
+from jax.experimental import pallas as pl
+from jax.experimental.pallas import tpu as pltpu
 from jax.sharding import PartitionSpec as P
 
 HEADS = 12
@@ -170,7 +174,7 @@
     )
 
 
-def local(
+def general(
     tokens,
     global_states,
     token_seg,
@@ -435,6 +439,870 @@
     )
 
 
+MESH = pl.DeviceIdType.MESH
+BF = jnp.bfloat16
+F32 = jnp.float32
+
+
+def dot_nn(left, right):
+    return lax.dot_general(left, right, (((1,), (0,)), ((), ())), preferred_element_type=F32)
+
+
+def dot_nt(left, right):
+    return lax.dot_general(left, right, (((1,), (1,)), ((), ())), preferred_element_type=F32)
+
+
+def lanes_of(shape):
+    return lax.broadcasted_iota(jnp.int32, shape, len(shape) - 1)
+
+
+def two_parts(value):
+    high = value.astype(BF)
+    return high, (value - high.astype(F32)).astype(BF)
+
+
+def norm_stats(value):
+    center = jnp.mean(value, axis=-1, keepdims=True)
+    spread = value - center
+    variance = jnp.mean(spread * spread, axis=-1, keepdims=True)
+    return spread, lax.rsqrt(variance + EPS)
+
+
+def norm_pull(value, gain, upstream):
+    spread, scale = norm_stats(value)
+    unit = spread * scale
+    scaled = upstream * gain
+    first = jnp.mean(scaled, axis=-1, keepdims=True)
+    second = jnp.mean(scaled * unit, axis=-1, keepdims=True)
+    grad = scale * (scaled - first - unit * second)
+    return (
+        grad,
+        jnp.sum(upstream * unit, axis=0, keepdims=True),
+        jnp.sum(upstream, axis=0, keepdims=True),
+    )
+
+
+def gelu_pair(hidden):
+    size = jnp.abs(hidden) * 0.7071067811865476
+    step = 1.0 / (1.0 + 0.3275911 * size)
+    bell = jnp.exp(-(size * size))
+    series = 1.061405429 * 0.5
+    for term in (-1.453152027, 1.421413741, -0.284496736, 0.254829592):
+        series = series * step + term * 0.5
+    tail = series * step * bell
+    mass = jnp.where(hidden < 0.0, tail, 1.0 - tail)
+    return hidden * mass, mass + hidden * (bell * 0.3989422804014327)
+
+
+def layer_kernel(
+    tokens, gstates, tseg, gseg, attn_gain, attn_shift, glob_gain, glob_shift, w_qkv, w_out,
+    ffn_gain, ffn_shift, w_up, up_bias, w_down, down_bias, cotan, gcotan,
+    o_out, o_gout, o_tgrad, o_ggrad, o_qkv, o_wout, o_up, o_down, o_vec, o_ub,
+    sec, nrm, proj, kvt, probs, att_t, att, x2, n2, n2t, ct, ct_t, acc, gn2, gatt, qaug, kaug,
+    wq, wo, wus, wds,
+    lse_t, rl_t, og_t, msg1, rcv1, cx, rcv2, rcv3, vec, rvec, rll,
+    gd, r0d, r1d, r2d, r3d, r4d, gu, r0u, r1u, r2u, r3u, r4u, r0q, r1qx, r1qy, r2q, r3q, r4q,
+    loc, wsem, hs, hr, m1s, m1r, m2s, m2r, m3s, m3r, gos, gor, ggs_s, ggs_r, vs, vr,
+    d0s, d0r, d1s, d1r, d2s, d2r, d3s, d3r, d4s, d4r,
+    u0s, u0r, u1s, u1r, u2s, u2r, u3s, u3r, u4s, u4r,
+    q0s, q0r, q1s, q1r, q2s, q2r, q3s, q3r, q4s, q4r,
+    hs2, hr2, osem,
+):
+    tok, width = tokens.shape
+    glob = gstates.shape[0]
+    rows = tok + glob
+    n_seq = lax.axis_size("seq")
+    slots = glob // n_seq
+    wide = tok + slots
+    half = tok // 2
+    pairs = HEADS // 2
+    chunk = wus.shape[2]
+    n_chunk = up_bias.shape[1] // chunk
+    tail = 128
+
+    s = lax.axis_index("seq")
+    b = lax.axis_index("batch")
+    x, zl, zh = s % 2, (s // 2) % 2, s // 4
+    c, y = b % 2, b // 2
+    dev_c, dev_y = (s, b + 1 - 2 * c), (s, b + 2 - 4 * y)
+    dev_x, dev_1, dev_2 = (s + 1 - 2 * x, b), (s + 2 - 4 * zl, b), (s + 4 - 8 * zh, b)
+
+    def flip(k):
+        other = s
+        if k & 1:
+            other = other + 1 - 2 * x
+        if k & 2:
+            other = other + 2 - 4 * zl
+        if k & 4:
+            other = other + 4 - 8 * zh
+        return other
+
+    def remote(src, dst, ss, rs, dev):
+        return pltpu.make_async_remote_copy(
+            src_ref=src, dst_ref=dst, send_sem=ss, recv_sem=rs, device_id=dev, device_id_type=MESH
+        )
+
+    peers = tuple(range(1, n_seq))
+
+    my_slots = pl.multiple_of(s * slots, slots)
+    loads = [
+        (tokens.at[pl.ds(half, half)], sec.at[pl.ds(0, half)]),
+        (gstates, sec.at[pl.ds(tok, glob)]),
+        (w_qkv, wq),
+        (cotan, ct.at[pl.ds(0, tok)]),
+        (gcotan.at[pl.ds(my_slots, slots)], ct.at[pl.ds(tok, slots)]),
+        (w_out, wo),
+    ]
+    loads = [pltpu.make_async_copy(a, d, loc.at[i]) for i, (a, d) in enumerate(loads)]
+    for load in loads:
+        load.start()
+
+    def stream(i, slot):
+        at = pl.multiple_of(i * chunk, chunk)
+        return (
+            pltpu.make_async_copy(w_up.at[:, pl.ds(at, chunk)], wus.at[slot], wsem.at[0, slot]),
+            pltpu.make_async_copy(w_down.at[pl.ds(at, chunk)], wds.at[slot], wsem.at[1, slot]),
+        )
+
+    for i in range(2):
+        for copy in stream(i, i):
+            copy.start()
+
+    bar = pltpu.get_barrier_semaphore()
+    for k in peers:
+        pl.semaphore_signal(bar, inc=1, device_id=(flip(k), b), device_id_type=MESH)
+    pl.semaphore_signal(bar, inc=1, device_id=dev_c, device_id_type=MESH)
+    pl.semaphore_signal(bar, inc=1, device_id=dev_y, device_id_type=MESH)
+    pl.semaphore_wait(bar, len(peers) + 2)
+    halo = remote(
+        tokens.at[pl.ds(0, half)], sec.at[pl.ds(half, half)], hs.at[0], hr.at[0],
+        (lax.rem(s + n_seq - 1, n_seq), b),
+    )
+    halo.start()
+
+    seg_row = jnp.concatenate([tseg[...], gseg[...]], axis=1)
+    which = lax.broadcasted_iota(jnp.int32, (128, rows), 0)
+    col = lanes_of((128, rows))
+    is_glob = col >= tok
+    same = which == seg_row
+    q_t = jnp.where(which < 3, jnp.where(same, 1.0, 0.0), jnp.where((which == 3) & is_glob, 1.0, 0.0))
+    far = jnp.where(s == 0, 0.0, NEGATIVE)
+    k_t = jnp.where(which < 3, jnp.where(same, 0.0, NEGATIVE), jnp.where((which == 3) & is_glob, far, 0.0))
+    qaug[...] = jnp.transpose(q_t).astype(BF)
+    kaug[...] = jnp.transpose(k_t).astype(BF)
+
+    def norm_to(first, count, gain, shift):
+        for r in range(first, first + count, 128):
+            spread, scale = norm_stats(sec[pl.ds(r, 128), :].astype(F32))
+            nrm[pl.ds(r, 128), :] = (spread * scale * gain[...] + shift[...]).astype(BF)
+
+    def project_rows(first, count):
+        def step(i, carry):
+            at = pl.multiple_of(i * width, width)
+            proj[pl.ds(first, count), pl.ds(at, width)] = dot_nn(
+                nrm[pl.ds(first, count), :], wq[:, pl.ds(at, width)]
+            ).astype(BF)
+            return carry
+
+        lax.fori_loop(0, 3, step, 0)
+
+    loads[1].wait()
+    norm_to(tok, glob, glob_gain, glob_shift)
+    loads[0].wait()
+    norm_to(0, half, attn_gain, attn_shift)
+    loads[2].wait()
+    project_rows(tok, glob)
+    project_rows(0, half)
+    loads[3].wait()
+    loads[4].wait()
+    ct_t[:, pl.ds(0, wide)] = jnp.transpose(ct[...])
+    halo.wait()
+    norm_to(half, half, attn_gain, attn_shift)
+    project_rows(half, half)
+
+    kvt[...] = jnp.transpose(proj[:, pl.ds(2 * width, width)])
+    lane_p = lanes_of((1, 128))
+    even = jnp.where(lane_p < HEAD_DIM, HEAD_DIM ** (-0.5), 0.0).astype(BF)
+    odd = jnp.where(lane_p < HEAD_DIM, 0.0, HEAD_DIM ** (-0.5)).astype(BF)
+    even_one = jnp.where(lane_p < HEAD_DIM, 1.0, 0.0).astype(BF)
+    odd_one = jnp.where(lane_p < HEAD_DIM, 0.0, 1.0).astype(BF)
+    first_head = lax.broadcasted_iota(jnp.int32, (128, 128), 0) < HEAD_DIM
+    lse_t[...] = jnp.zeros_like(lse_t)
+    rl_t[...] = jnp.zeros_like(rl_t)
+
+    def glob_forward(p, carry):
+        at = pl.multiple_of(p * 128, 128)
+        keys = jnp.concatenate([proj[:, pl.ds(width + at, 128)], kaug[...]], axis=1)
+        qg = proj[pl.ds(tok, glob), pl.ds(at, 128)]
+        qa = qaug[pl.ds(tok, glob), :]
+        queries = jnp.concatenate(
+            [jnp.concatenate([qg * even, qa], axis=1), jnp.concatenate([qg * odd, qa], axis=1)], axis=0
+        )
+        scores = dot_nt(keys, queries)
+        top = jnp.max(scores, axis=0, keepdims=True)
+        raised = jnp.exp(scores - top)
+        total = jnp.sum(raised, axis=0, keepdims=True)
+        weights = (raised * (1.0 / total)).astype(BF)
+        probs[p, :, pl.ds(2 * tok, 2 * glob)] = weights
+        mixed = dot_nn(kvt[pl.ds(at, 128), :], weights)
+        og_t[pl.ds(at, 128), :] = jnp.where(first_head, mixed[:, :glob], mixed[:, glob:])
+        logsum = top + jnp.log(total)
+        lse_t[pl.ds(2 * p, 1), :] = logsum[:, :glob]
+        lse_t[pl.ds(2 * p + 1, 1), :] = logsum[:, glob:]
+        return carry
+
+    lax.fori_loop(0, pairs, glob_forward, 0)
+
+    lse = jnp.transpose(lse_t[...])
+    in_heads = lanes_of((glob, 128)) < HEADS
+    lse = jnp.where(in_heads, lse, 0.0)
+    part_a, rest = two_parts(lse)
+    rest = lse - part_a.astype(F32)
+    part_b = rest.astype(BF)
+    part_c = rest - part_b.astype(F32)
+    packed = part_a.astype(F32) + pltpu.roll(part_b.astype(F32), 16, 1) + pltpu.roll(part_c, 32, 1)
+    msg1[:, pl.ds(0, width)] = jnp.transpose(og_t[...]).astype(BF)
+    msg1[:, pl.ds(width, 128)] = packed.astype(BF)
+    sends1 = []
+    for k in peers:
+        other = flip(k)
+        at = pl.multiple_of(other * slots, slots)
+        copy = remote(msg1.at[pl.ds(at, slots)], rcv1.at[k], m1s.at[k], m1r.at[k], (other, b))
+        copy.start()
+        sends1.append(copy)
+    rcv1[0] = msg1[pl.ds(my_slots, slots), :]
+
+    def local_forward_pair(p, carry):
+        at = pl.multiple_of(p * 128, 128)
+        keys = jnp.concatenate([proj[:, pl.ds(width + at, 128)], kaug[...]], axis=1)
+        qp = proj[pl.ds(0, tok), pl.ds(at, 128)]
+        for e, mask in ((0, even), (1, odd)):
+            queries = jnp.concatenate([qp * mask, qaug[pl.ds(0, tok), :]], axis=1)
+            scores = dot_nt(keys, queries)
+            top = jnp.max(scores, axis=0, keepdims=True)
+            raised = jnp.exp(scores - top)
+            inverse = 1.0 / jnp.sum(raised, axis=0, keepdims=True)
+            weights = raised.astype(BF)
+            probs[p, :, pl.ds(e * tok, tok)] = weights
+            rl_t[pl.ds(2 * p + e, 1), :] = inverse
+            here = pl.multiple_of(at + e * HEAD_DIM, HEAD_DIM)
+            mixed = dot_nn(kvt[pl.ds(here, HEAD_DIM), :], weights)
+            att_t[pl.ds(here, HEAD_DIM), pl.ds(0, tok)] = (mixed * inverse).astype(BF)
+        return carry
+
+    lax.fori_loop(0, pairs, local_forward_pair, 0)
+    att[pl.ds(0, tok), :] = jnp.transpose(att_t[:, pl.ds(0, tok)])
+
+    head_of = lanes_of((128, width)) // HEAD_DIM
+    spread_heads = jnp.where(head_of == lax.broadcasted_iota(jnp.int32, (128, width), 0), 1.0, 0.0).astype(BF)
+    for copy in sends1:
+        copy.wait()
+    logs = []
+    for k in range(n_seq):
+        packed = rcv1[k, :, pl.ds(width, 128)].astype(F32)
+        logs.append(packed + pltpu.roll(packed, 112, 1) + pltpu.roll(packed, 96, 1))
+    high = functools.reduce(jnp.maximum, logs)
+    raised = [jnp.exp(one - high) for one in logs]
+    total = functools.reduce(jnp.add, raised)
+    in_heads = lanes_of((slots, 128)) < HEADS
+    shares = jnp.concatenate([jnp.where(in_heads, one / total, 0.0) for one in raised], axis=0)
+    share_a, share_b = two_parts(shares)
+    shares = dot_nn(share_a, spread_heads) + dot_nn(share_b, spread_heads)
+    cx[...] = shares
+    mixed = jnp.zeros((slots, width), F32)
+    for k in range(n_seq):
+        mixed = mixed + shares[k * slots : (k + 1) * slots] * rcv1[k, :, pl.ds(0, width)].astype(F32)
+    att[pl.ds(tok, slots), :] = mixed.astype(BF)
+    att_t[:, pl.ds(tok, tail)] = jnp.transpose(
+        jnp.concatenate([mixed, jnp.zeros((tail - slots, width), F32)], axis=0)
+    ).astype(BF)
+
+    loads[5].wait()
+    x2[...] = dot_nn(att[...], wo[...])
+    x2[pl.ds(0, tok), :] += sec[pl.ds(0, tok), :].astype(F32)
+    x2[pl.ds(tok, slots), :] += sec[pl.ds(pl.multiple_of(tok + my_slots, slots), slots), :].astype(F32)
+
+    def second_norm(first, count):
+        spread, scale = norm_stats(x2[pl.ds(first, count), :])
+        n2[pl.ds(first, count), :] = (spread * scale * ffn_gain[...] + ffn_shift[...]).astype(BF)
+
+    for r in range(0, tok, 128):
+        second_norm(r, 128)
+    second_norm(tok, slots)
+    n2t[:, pl.ds(0, wide)] = jnp.transpose(n2[...])
+
+    def d_core(i):
+        return remote(gd.at[i, :, 1 - c], r0d.at[i], d0s.at[i], d0r.at[i], dev_c)
+
+    def d_y(i):
+        return remote(r0d.at[i, 1 - y], r1d.at[i], d1s.at[i], d1r.at[i], dev_y)
+
+    def d_x(z):
+        return remote(r1d.at[2 * z + 1 - x], r2d.at[z], d2s.at[z], d2r.at[z], dev_x)
+
+    def d_1(h):
+        return remote(r2d.at[2 * h + 1 - zl], r3d.at[h], d3s.at[h], d3r.at[h], dev_1)
+
+    def d_2():
+        return remote(r3d.at[1 - zh], r4d, d4s.at[0], d4r.at[0], dev_2)
+
+    def do_d_y(i):
+        d_core(i).wait_recv()
+        r0d[i] = r0d[i] + gd[i, :, c]
+        d_y(i).start()
+
+    def do_d_x(z):
+        for o in range(2):
+            d_y(2 * z + o).wait_recv()
+            r1d[2 * z + o] = r1d[2 * z + o] + r0d[2 * z + o, y]
+        d_x(z).start()
+
+    def do_d_1(h):
+        for o in range(2):
+            d_x(2 * h + o).wait_recv()
+            r2d[2 * h + o] = r2d[2 * h + o] + r1d[2 * (2 * h + o) + x]
+        d_1(h).start()
+
+    def do_d_2():
+        for h in range(2):
+            d_1(h).wait_recv()
+            r3d[h] = r3d[h] + r2d[2 * h + zl]
+        d_2().start()
+
+    def u_core(yy, j):
+        return remote(gu.at[yy, 1 - c, j], r0u.at[yy, j], u0s.at[yy * 2 + j], u0r.at[yy * 2 + j], dev_c)
+
+    def u_x(yy, j):
+        return remote(r0u.at[yy, j, :, :, 1 - x], r1u.at[yy, j], u1s.at[yy * 2 + j], u1r.at[yy * 2 + j], dev_x)
+
+    def u_y(j):
+        return remote(r1u.at[1 - y, j], r2u.at[j], u2s.at[j], u2r.at[j], dev_y)
+
+    def u_1():
+        return remote(r2u.at[:, :, 1 - zl], r3u, u3s.at[0], u3r.at[0], dev_1)
+
+    def u_2():
+        return remote(r3u.at[:, 1 - zh], r4u, u4s.at[0], u4r.at[0], dev_2)
+
+    def do_u_x(yy, j):
+        u_core(yy, j).wait_recv()
+        r0u[yy, j] = r0u[yy, j] + gu[yy, c, j]
+        u_x(yy, j).start()
+
+    def do_u_y(j):
+        for yy in range(2):
+            u_x(yy, j).wait_recv()
+            r1u[yy, j] = r1u[yy, j] + r0u[yy, j, :, :, x]
+        u_y(j).start()
+
+    def do_u_1():
+        for j in range(2):
+            u_y(j).wait_recv()
+            r2u[j] = r2u[j] + r1u[y, j]
+        u_1().start()
+
+    def do_u_2():
+        u_1().wait_recv()
+        r3u[...] = r3u[...] + r2u[:, :, zl]
+        u_2().start()
+
+    acc[...] = jnp.zeros_like(acc)
+    gn2[...] = jnp.zeros_like(gn2)
+
+    def ffn_step(i, carry):
+        slot = lax.rem(i, 2)
+        for copy in stream(i, slot):
+            copy.wait()
+        at = pl.multiple_of(i * chunk, chunk)
+        hidden = dot_nn(n2[...], wus[slot]) + up_bias[:, pl.ds(at, chunk)]
+        active, slope = gelu_pair(hidden)
+        active = active.astype(BF)
+        gd[i] = dot_nn(ct_t[:, pl.ds(0, wide)], active).astype(BF).reshape(gd.shape[1:])
+        d_core(i).start()
+        grad_hidden = (slope * dot_nt(ct[...], wds[slot])).astype(BF)
+        gu[i // 4, (i // 2) % 2, i % 2] = (
+            dot_nn(n2t[:, pl.ds(0, wide)], grad_hidden).astype(BF).reshape(gu.shape[3:])
+        )
+
+        @pl.when((i // 2) % 2 != c)
+        def _():
+            u_core(i // 4, i % 2).start()
+
+        rll[pl.ds(i, 1), :] = jnp.sum(grad_hidden.astype(F32), axis=0, keepdims=True)
+        acc[...] += dot_nn(active, wds[slot])
+        gn2[...] += dot_nt(grad_hidden, wus[slot])
+
+        @pl.when(i + 2 < n_chunk)
+        def _():
+            for copy in stream(i + 2, slot):
+                copy.start()
+
+        @pl.when(i >= 2)
+        def _():
+            do_d_y(i - 2)
+
+        @pl.when((i >= 2) & (((i - 2) // 2) % 2 == c))
+        def _():
+            do_u_x((i - 2) // 4, i % 2)
+
+        return carry
+
+    lax.fori_loop(0, n_chunk, ffn_step, 0)
+
+    vec[...] = jnp.zeros_like(vec)
+    for i in range(n_chunk):
+        vec[pl.ds(8 + i // 2, 1), pl.ds((i % 2) * chunk, chunk)] = rll[pl.ds(i, 1), :]
+
+    def second_pull(first, count):
+        grad, gain_term, shift_term = norm_pull(
+            x2[pl.ds(first, count), :], ffn_gain[...], gn2[pl.ds(first, count), :]
+        )
+        upstream = ct[pl.ds(first, count), :].astype(F32)
+        total = upstream + grad
+        acc[pl.ds(first, count), :] += x2[pl.ds(first, count), :] + down_bias[...]
+        x2[pl.ds(first, count), :] = total
+        n2[pl.ds(first, count), :] = total.astype(BF)
+        vec[pl.ds(4, 1), :] += gain_term
+        vec[pl.ds(5, 1), :] += shift_term
+        vec[pl.ds(6, 1), :] += jnp.sum(upstream, axis=0, keepdims=True)
+
+    for r in range(0, tok, 128):
+        second_pull(r, 128)
+    second_pull(tok, slots)
+    do_d_y(n_chunk - 2)
+    do_d_y(n_chunk - 1)
+
+    @pl.when(c == 1)
+    def _():
+        do_u_x(1, 0)
+        do_u_x(1, 1)
+
+    gatt[...] = dot_nt(n2[...], wo[...]).astype(BF)
+
+    slot_grad = gatt[pl.ds(tok, slots), :].astype(F32)
+    slot_att = att[pl.ds(tok, slots), :].astype(F32)
+    head_sel = lanes_of((1, 128)) < HEADS
+
+    def inner_aug(upstream, values):
+        high, low = two_parts(upstream.astype(F32) * values)
+        inner = dot_nt(high, spread_heads) + dot_nt(low, spread_heads)
+        high, low = two_parts(jnp.where(head_sel, inner, 0.0))
+        return (high.astype(F32) + pltpu.roll(low.astype(F32), 16, 1)).astype(BF)
+
+    scaled = jnp.concatenate(
+        [(cx[pl.ds(k * slots, slots), :] * slot_grad).astype(BF) for k in range(n_seq)], axis=0
+    )
+    msg1[:, pl.ds(0, width)] = scaled
+    msg1[:, pl.ds(width, 128)] = inner_aug(scaled, jnp.concatenate([slot_att] * n_seq, axis=0))
+    sends2 = []
+    for k in peers:
+        copy = remote(
+            msg1.at[pl.ds(k * slots, slots)], rcv2.at[pl.ds(my_slots, slots)], m2s.at[k], m2r.at[k],
+            (flip(k), b),
+        )
+        copy.start()
+        sends2.append(copy)
+    rcv2[pl.ds(my_slots, slots), :] = msg1[pl.ds(0, slots), :]
+
+    n2t[:, pl.ds(0, tok)] = jnp.transpose(nrm[pl.ds(0, tok), :])
+    mine = nrm[pl.ds(pl.multiple_of(tok + my_slots, slots), slots), :].astype(F32)
+    n2t[:, pl.ds(tok, tail)] = jnp.transpose(
+        jnp.concatenate([mine, jnp.zeros((tail - slots, width), F32)], axis=0)
+    ).astype(BF)
+
+    outs = nrm
+    outs[pl.ds(0, wide), :] = acc[...].astype(BF)
+    out_copy = pltpu.make_async_copy(outs.at[pl.ds(0, tok)], o_out, osem.at[0])
+    out_copy.start()
+    own_out = pltpu.make_async_copy(
+        outs.at[pl.ds(tok, slots)], o_gout.at[pl.ds(my_slots, slots)], osem.at[1]
+    )
+    own_out.start()
+    sends_o = []
+    for k in peers:
+        copy = remote(
+            outs.at[pl.ds(tok, slots)], o_gout.at[pl.ds(my_slots, slots)], gos.at[k], gor.at[k], (flip(k), b)
+        )
+        copy.start()
+        sends_o.append(copy)
+
+    scale_c = jnp.transpose(
+        jnp.concatenate([rl_t[...], jnp.zeros((128 - rl_t.shape[0], tok), F32)], axis=0)
+    )
+    scale_a, scale_b = two_parts(scale_c)
+    for r in range(0, tok, 128):
+        wider = dot_nn(scale_a[r : r + 128], spread_heads) + dot_nn(scale_b[r : r + 128], spread_heads)
+        scaled = (gatt[pl.ds(r, 128), :].astype(F32) * wider).astype(BF)
+        gatt[pl.ds(r, 128), :] = scaled
+        qaug[pl.ds(r, 128), :] = inner_aug(scaled, att[pl.ds(r, 128), :].astype(F32))
+    kvt[...] = jnp.transpose(proj[:, pl.ds(width, width)])
+    for i in range(4):
+        do_d_x(i)
+    do_u_y(0)
+    do_u_y(1)
+    for copy in sends2:
+        copy.wait()
+
+    minus = jnp.where(lanes_of((rows, 128)) < 32, -1.0, 0.0).astype(BF)
+
+    def chosen(head):
+        lane = lanes_of((1, 128))
+        return jnp.where((lane == head) | (lane == head + 16), 1.0, 0.0).astype(BF)
+
+    def attention_back(p, carry):
+        at = pl.multiple_of(p * 128, 128)
+        qp = proj[pl.ds(0, tok), pl.ds(at, 128)]
+        qg = proj[pl.ds(tok, glob), pl.ds(at, 128)]
+        gp = gatt[pl.ds(0, tok), pl.ds(at, 128)]
+        gg = rcv2[:, pl.ds(at, 128)]
+        dg = rcv2[:, pl.ds(width, 128)]
+        values = jnp.concatenate([proj[:, pl.ds(2 * width + at, 128)], minus], axis=1)
+        ups = jnp.concatenate([gp * even_one, gp * odd_one, gg * even_one, gg * odd_one], axis=0)
+        dd = qaug[pl.ds(0, tok), :]
+        sel_e, sel_o = chosen(2 * p), chosen(2 * p + 1)
+        inner = jnp.concatenate([dd * sel_e, dd * sel_o, dg * sel_e, dg * sel_o], axis=0)
+        qs = jnp.concatenate([qp * even, qp * odd, qg * even, qg * odd], axis=0)
+        grad_v = dot_nn(probs[p], ups)
+        for first, count in ((0, tok), (tok, tok), (2 * tok, 2 * glob)):
+            right = jnp.concatenate([ups[first : first + count], inner[first : first + count]], axis=1)
+            grad_w = dot_nt(values, right)
+            here = probs[p, :, pl.ds(first, count)].astype(F32)
+            probs[p, :, pl.ds(first, count)] = (here * grad_w).astype(BF)
+        grad_k = dot_nn(probs[p], qs)
+        factor = HEAD_DIM ** (-0.5)
+        low = dot_nn(kvt[pl.ds(at, HEAD_DIM), :], probs[p, :, pl.ds(0, tok)])
+        upper = dot_nn(
+            kvt[pl.ds(pl.multiple_of(at + HEAD_DIM, HEAD_DIM), HEAD_DIM), :], probs[p, :, pl.ds(tok, tok)]
+        )
+        grad_q = jnp.concatenate([low, upper], axis=0) * factor
+        own = dot_nn(kvt[pl.ds(at, 128), :], probs[p, :, pl.ds(2 * tok, 2 * glob)])
+        own = jnp.where(first_head, own[:, :glob], own[:, glob:]) * factor
+        proj[pl.ds(0, tok), pl.ds(at, 128)] = jnp.transpose(grad_q).astype(BF)
+        proj[pl.ds(tok, glob), pl.ds(at, 128)] = jnp.transpose(own).astype(BF)
+        proj[:, pl.ds(width + at, 128)] = grad_k.astype(BF)
+        proj[:, pl.ds(2 * width + at, 128)] = grad_v.astype(BF)
+
+        @pl.when(p == 2)
+        def _():
+            do_d_1(0)
+            do_d_1(1)
+
+        @pl.when(p == 3)
+        def _():
+            do_u_1()
+
+        @pl.when(p == 4)
+        def _():
+            do_d_2()
+
+        @pl.when(p == 5)
+        def _():
+            do_u_2()
+
+        return carry
+
+    lax.fori_loop(0, pairs, attention_back, 0)
+
+    sends3 = []
+    for k in peers:
+        other = flip(k)
+        at = pl.multiple_of(tok + other * slots, slots)
+        copy = remote(proj.at[pl.ds(at, slots)], rcv3.at[k - 1], m3s.at[k], m3r.at[k], (other, b))
+        copy.start()
+        sends3.append(copy)
+
+    total3 = proj[pl.ds(pl.multiple_of(tok + my_slots, slots), slots), :].astype(F32)
+    for copy in sends3:
+        copy.wait()
+    for k in peers:
+        total3 = total3 + rcv3[k - 1].astype(F32)
+    proj[pl.ds(tok, slots), :] = total3.astype(BF)
+
+    for yy in range(2):
+        for j in range(2):
+            u_core(yy, j).wait_send()
+
+    def q_block(yy, cc):
+        bb = 2 * yy + cc
+        odd_b = cc == 1
+        at = pl.multiple_of(bb * 576 - 64 * cc, 128)
+        window = proj[pl.ds(0, wide), pl.ds(at, 640)].astype(F32)
+        window = jnp.where(odd_b, pltpu.roll(window, 576, 1), window).astype(BF)
+        at = pl.multiple_of(bb * 192 - 64 * cc, 128)
+        branch = n2[:, pl.ds(at, 256)].astype(F32)
+        branch = jnp.where(odd_b, branch, pltpu.roll(branch, 64, 1)).astype(BF)
+        first = dot_nn(n2t[:, pl.ds(0, wide)], window[:, :384])
+        second = dot_nn(n2t[:, pl.ds(0, wide)], window[:, 384:])
+        third = dot_nn(att_t[:, pl.ds(0, wide)], branch)
+        middle = jnp.where(lanes_of((width, 128)) < 64, second[:, 128:], third[:, :128])
+        return first, jnp.concatenate([second[:, :128], middle, third[:, 128:]], axis=1)
+
+    def q_core(yy, j):
+        return remote(gu.at[yy, 1 - c, j], r0q.at[yy, j], q0s.at[yy * 2 + j], q0r.at[yy * 2 + j], dev_c)
+
+    def q_first(yy, carry):
+        for j, block in enumerate(q_block(yy, 1 - c)):
+            gu[yy, 1 - c, j] = block.astype(BF).reshape(gu.shape[3:])
+            q_core(yy, j).start()
+        return carry
+
+    lax.fori_loop(0, 2, q_first, 0)
+
+    gn2[...] = dot_nt(proj[pl.ds(0, wide), :], wq[...])
+
+    def q_x0(yy):
+        return remote(r0q.at[yy, 0, :, :, 1 - x], r1qx.at[yy], q1s.at[yy], q1r.at[yy], dev_x)
+
+    def q_y0():
+        return remote(r1qx.at[1 - y], r2q.at[0], q2s.at[0], q2r.at[0], dev_y)
+
+    def q_y1():
+        return remote(r0q.at[1 - y, 1], r1qy, q1s.at[2], q1r.at[2], dev_y)
+
+    def q_x1():
+        return remote(r1qy.at[:, :, 1 - x], r2q.at[1], q2s.at[1], q2r.at[1], dev_x)
+
+    def q_1():
+        return remote(r2q.at[:, :, 1 - zl], r3q, q3s.at[0], q3r.at[0], dev_1)
+
+    def q_2():
+        return remote(r3q.at[:, 1 - zh], r4q, q4s.at[0], q4r.at[0], dev_2)
+
+    def q_second(yy, carry):
+        first, second = q_block(yy, c)
+        q_core(yy, 0).wait_recv()
+        r0q[yy, 0] = (r0q[yy, 0].astype(F32) + first.reshape(gu.shape[3:])).astype(BF)
+        q_x0(yy).start()
+        q_core(yy, 1).wait_recv()
+        r0q[yy, 1] = (r0q[yy, 1].astype(F32) + second.reshape(gu.shape[3:])).astype(BF)
+        return carry
+
+    lax.fori_loop(0, 2, q_second, 0)
+    q_y1().start()
+
+    def first_pull(first):
+        grad, gain_term, shift_term = norm_pull(
+            sec[pl.ds(first, 128), :].astype(F32), attn_gain[...], gn2[pl.ds(first, 128), :]
+        )
+        n2[pl.ds(first, 128), :] = (grad + x2[pl.ds(first, 128), :]).astype(BF)
+        vec[pl.ds(0, 1), :] += gain_term
+        vec[pl.ds(1, 1), :] += shift_term
+
+    for r in range(half, tok, 128):
+        first_pull(r)
+    back = remote(
+        n2.at[pl.ds(half, half)], o_tgrad.at[pl.ds(0, half)], hs2.at[0], hr2.at[0],
+        (lax.rem(s + 1, n_seq), b),
+    )
+    back.start()
+    for r in range(0, half, 128):
+        first_pull(r)
+    keep = pltpu.make_async_copy(n2.at[pl.ds(0, half)], o_tgrad.at[pl.ds(half, half)], osem.at[2])
+    keep.start()
+
+    grad, gain_term, shift_term = norm_pull(
+        sec[pl.ds(pl.multiple_of(tok + my_slots, slots), slots), :].astype(F32),
+        glob_gain[...],
+        gn2[pl.ds(tok, slots), :],
+    )
+    vec[pl.ds(2, 1), :] += gain_term
+    vec[pl.ds(3, 1), :] += shift_term
+    n2[pl.ds(tok, slots), :] = (grad + x2[pl.ds(tok, slots), :]).astype(BF)
+    own_grad = pltpu.make_async_copy(
+        n2.at[pl.ds(tok, slots)], o_ggrad.at[pl.ds(my_slots, slots)], osem.at[3]
+    )
+    own_grad.start()
+    sends_g = []
+    for k in peers:
+        copy = remote(
+            n2.at[pl.ds(tok, slots)], o_ggrad.at[pl.ds(my_slots, slots)], ggs_s.at[k], ggs_r.at[k],
+            (flip(k), b),
+        )
+        copy.start()
+        sends_g.append(copy)
+
+    def vec_step(k, dev):
+        return remote(vec, rvec.at[k], vs.at[k], vr.at[k], dev)
+
+    def vec_add(k, dev):
+        vec_step(k, dev).wait()
+        vec[...] += rvec[k]
+
+    vec_step(0, dev_c).start()
+    d_2().wait_recv()
+    o_down[...] = jnp.transpose(r4d[...].astype(F32) + r3d[zh].astype(F32))
+    u_2().wait_recv()
+    last = r4u[...].astype(F32) + r3u[:, zh].astype(F32)
+    o_up[:, pl.ds(0, 384)] = last[0]
+    o_up[:, pl.ds(384, 384)] = last[1]
+    vec_add(0, dev_c)
+    vec_step(1, dev_y).start()
+    for yy in range(2):
+        q_x0(yy).wait_recv()
+        r1qx[yy] = r1qx[yy] + r0q[yy, 0, :, :, x]
+    q_y0().start()
+    vec_add(1, dev_y)
+    vec_step(2, dev_x).start()
+    q_y1().wait_recv()
+    r1qy[...] = r1qy[...] + r0q[y, 1]
+    q_x1().start()
+    vec_add(2, dev_x)
+    vec_step(3, dev_1).start()
+    q_y0().wait_recv()
+    r2q[0] = r2q[0] + r1qx[y]
+    q_x1().wait_recv()
+    r2q[1] = r2q[1] + r1qy[:, :, x]
+    q_1().start()
+    vec_add(3, dev_1)
+    vec_step(4, dev_2).start()
+    q_1().wait_recv()
+    r3q[...] = r3q[...] + r2q[:, :, zl]
+    q_2().start()
+    vec_add(4, dev_2)
+    share = vec.shape[1] // n_seq
+    turned = pltpu.roll(vec[pl.ds(0, 8), :], lax.rem(vec.shape[1] - share * s, vec.shape[1]), 1)
+    o_vec[...] = turned[:, :share]
+    o_ub[...] = vec[pl.ds(8 + s // 2, 1), pl.ds(pl.multiple_of((s % 2) * chunk, chunk), chunk)]
+    q_2().wait_recv()
+    last = r4q[...].astype(F32) + r3q[:, zh].astype(F32)
+    o_qkv[:, pl.ds(0, 384)] = last[0]
+    o_qkv[:, pl.ds(384, 192)] = last[1][:, :192]
+    o_wout[...] = last[1][:, 192:]
+
+    for i in range(8):
+        d_core(i).wait_send()
+        d_y(i).wait_send()
+    for i in range(4):
+        d_x(i).wait_send()
+    for i in range(2):
+        d_1(i).wait_send()
+    d_2().wait_send()
+    for yy in range(2):
+        for j in range(2):
+            u_x(yy, j).wait_send()
+            q_core(yy, j).wait_send()
+        u_y(yy).wait_send()
+        q_x0(yy).wait_send()
+    u_1().wait_send()
+    u_2().wait_send()
+    q_y0().wait_send()
+    q_y1().wait_send()
+    q_x1().wait_send()
+    q_1().wait_send()
+    q_2().wait_send()
+    back.wait()
+    keep.wait()
+    own_grad.wait()
+    out_copy.wait()
+    own_out.wait()
+    for copy in sends_o + sends_g:
+        copy.wait()
+
+
+def fits(tokens, global_states, w_qkv, w_up):
+    return (
+        lax.axis_size("seq") == 8
+        and lax.axis_size("batch") == 4
+        and tokens.shape == (1, BLOCK, HEADS * HEAD_DIM)
+        and global_states.shape == (1, 128, HEADS * HEAD_DIM)
+        and w_qkv.shape == (HEADS * HEAD_DIM, 3 * HEADS * HEAD_DIM)
+        and w_up.shape == (HEADS * HEAD_DIM, 3072)
+    )
+
+
+def fused(
+    tokens, global_states, token_seg, global_seg, attn_gain, attn_shift, glob_gain, glob_shift, w_qkv, w_out,
+    ffn_gain, ffn_shift, w_up, up_bias, w_down, down_bias, out_cotangent, global_cotangent,
+):
+    tok, width = tokens.shape[1:]
+    glob = global_states.shape[1]
+    hidden = w_up.shape[1]
+    n_seq, n_batch = lax.axis_size("seq"), lax.axis_size("batch")
+    rows, slots = tok + glob, glob // n_seq
+    wide = tok + slots
+    chunk, part, side = hidden // n_seq, width // n_seq, width // n_batch
+    pairs = HEADS // 2
+    dma = pltpu.SemaphoreType.DMA
+
+    def any_space():
+        return pl.BlockSpec(memory_space=pl.ANY)
+
+    def vmem():
+        return pl.BlockSpec(memory_space=pltpu.VMEM)
+
+    def low(*shape):
+        return pltpu.VMEM(shape, BF)
+
+    def full(*shape):
+        return pltpu.VMEM(shape, F32)
+
+    scratch = [
+        low(rows, width), low(rows, width), low(rows, 3 * width), low(width, rows),
+        low(pairs, rows, 2 * tok + 2 * glob), low(width, tok + 128), low(wide, width), full(wide, width),
+        low(wide, width), low(width, tok + 128), low(wide, width), low(width, tok + 128),
+        full(wide, width), full(wide, width), low(wide, width), low(rows, 128), low(rows, 128),
+        low(width, 3 * width), low(width, width), low(2, width, chunk), low(2, chunk, width),
+        full(128, glob), full(16, tok), full(width, glob), low(glob, width + 128),
+        low(n_seq, slots, width + 128), full(glob, width), low(glob, width + 128),
+        low(n_seq - 1, slots, 3 * width),
+        full(16, width), full(5, 16, width), full(8, chunk),
+        low(8, 2, 2, side, chunk), low(8, 2, side, chunk), low(8, side, chunk), low(4, side, chunk),
+        low(2, side, chunk), low(side, chunk),
+        low(2, 2, 2, 2, 2, 2, part, chunk), low(2, 2, 2, 2, 2, part, chunk), low(2, 2, 2, 2, part, chunk),
+        low(2, 2, 2, part, chunk), low(2, 2, part, chunk), low(2, part, chunk),
+        low(2, 2, 2, 2, 2, part, chunk), low(2, 2, 2, part, chunk), low(2, 2, 2, part, chunk),
+        low(2, 2, 2, part, chunk), low(2, 2, part, chunk), low(2, part, chunk),
+        dma((8,)), dma((2, 2)), dma((1,)), dma((1,)),
+        *[dma((8,)) for _ in range(10)], dma((5,)), dma((5,)),
+        dma((8,)), dma((8,)), dma((8,)), dma((8,)), dma((4,)), dma((4,)), dma((2,)), dma((2,)), dma((1,)), dma((1,)),
+        dma((4,)), dma((4,)), dma((4,)), dma((4,)), dma((2,)), dma((2,)), dma((1,)), dma((1,)), dma((1,)), dma((1,)),
+        dma((4,)), dma((4,)), dma((3,)), dma((3,)), dma((2,)), dma((2,)), dma((1,)), dma((1,)), dma((1,)), dma((1,)),
+        dma((1,)), dma((1,)), dma((4,)),
+    ]
+
+    def row(vector):
+        return vector.reshape(1, -1)
+
+    results = pl.pallas_call(
+        layer_kernel,
+        out_shape=[
+            jax.ShapeDtypeStruct((tok, width), BF),
+            jax.ShapeDtypeStruct((glob, width), BF),
+            jax.ShapeDtypeStruct((tok, width), BF),
+            jax.ShapeDtypeStruct((glob, width), BF),
+            jax.ShapeDtypeStruct((part, 3 * side), F32),
+            jax.ShapeDtypeStruct((part, side), F32),
+            jax.ShapeDtypeStruct((part, 2 * chunk), F32),
+            jax.ShapeDtypeStruct((chunk, side), F32),
+            jax.ShapeDtypeStruct((8, part), F32),
+            jax.ShapeDtypeStruct((1, chunk), F32),
+        ],
+        in_specs=[any_space(), any_space(), vmem(), vmem(), vmem(), vmem(), vmem(), vmem(), any_space(), any_space(),
+                  vmem(), vmem(), any_space(), vmem(), any_space(), vmem(), any_space(), any_space()],
+        out_specs=[any_space()] * 4 + [vmem()] * 6,
+        scratch_shapes=scratch,
+        compiler_params=pltpu.CompilerParams(
+            collective_id=0, has_side_effects=True, vmem_limit_bytes=64 * 1024 * 1024
+        ),
+        name="layer",
+    )(
+        tokens[0], global_states[0], token_seg, global_seg, row(attn_gain), row(attn_shift), row(glob_gain),
+        row(glob_shift), w_qkv, w_out, row(ffn_gain), row(ffn_shift), w_up, row(up_bias), w_down, row(down_bias),
+        out_cotangent[0], global_cotangent[0],
+    )
+    out, gout, tgrad, ggrad, g_qkv, g_out, g_up, g_down, g_vec, g_ub = results
+    return (
+        out[None], gout[None], tgrad[None], ggrad[None], g_vec[0], g_vec[1], g_vec[2], g_vec[3], g_qkv, g_out,
+        g_vec[4], g_vec[5], g_up, g_ub[0], g_down, g_vec[6],
+    )
+
+
+def local(tokens, global_states, token_seg, global_seg, *rest):
+    w_qkv, w_up = rest[4], rest[8]
+    way = fused if fits(tokens, global_states, w_qkv, w_up) else general
+    return way(tokens, global_states, token_seg, global_seg, *rest)
+
+
 def solution(mesh):
     placed = (
         P("batch", "seq", None),

time: 844 us -> 212 us (0.25)
  waiting for transfers between devices: 413 us -> 0 us
  matrix products: 194 us -> 0 us
  Pallas kernels: 0 us -> 187 us
  blocking collectives: 108 us -> 0 us
  other arithmetic: 60.9 us -> 1.27 us
  local copies, waits for them, and re-layouts: 39.8 us -> 21.6 us
  between operations: 17.1 us -> 0.69 us
    reduce_scatter x6 -> x0, waiting for transfers between devices: 276 us -> none  [the longest x1 72.1 us: local(): lax.psum_scatter(mat_sums[3], 'seq', scatter_dimension=0, tiled=True)]
    dot_general x48 -> x0, matrix products: 194 us -> none  [the longest x8 49.8 us: project(): jnp.einsum('rsd,de->rse', former, latter, preferred_element_type=jnp.floa...]
    pallas_call x0 -> x1, Pallas kernels: none -> 187 us  [fused(): pl.pallas_call(layer_kernel, out_shape=[jax.ShapeDtypeStruct((tok, width)...]
    psum x2 -> x0, waiting for transfers between devices: 95.7 us -> none  [the longest x1 48.9 us: local(): glob_out = lax.psum(remote_part, 'seq')]
    psum x3 -> x0, blocking collectives: 49.6 us -> none  [the longest x1 19.4 us: local(): lax.psum(remote_total, 'seq')]
    unnamed x1 -> x0, blocking collectives: 36.5 us -> none
    unnamed x12 -> x0, waiting for transfers between devices: 34.4 us -> none
    reduce_sum x18 -> x0, other arithmetic: 25.4 us -> none  [the longest x4 7.13 us: norm_rows(): return spread * lax.rsqrt(variance + EPS) * scaling + offset]
  transfers between devices with their start and end apart: 12 -> 0, of which waited for: 9 -> 0; matrix products, arithmetic and copies ran while one was open for 17% -> 0% of each run, Pallas kernels for 0% -> 0%
where the time goes in v1:
time: 212 us; the launch traced here: 210 us
  Pallas kernels  187 us (88%)
  local copies, waits for them, and re-layouts  21.6 us (10%)
    pallas_call x1, Pallas kernels, fused(): pl.pallas_call(layer_kernel, out_shape=[jax.ShapeDtypeStruct((tok, width)...  187 us
    unnamed x14, local copies, waits for them, and re-layouts  11.3 us
    reshape x7, local copies, waits for them, and re-layouts, row(): return vector.reshape(1, -1)  8.87 us

profile of v1, /device:TPU:2, one launch (start us, length us, event | category | flops | bytes accessed | tf_op | source)
XLA Modules:
  0.0 210.2 jit_solution(3242779231598060389)
XLA Ops:
  0.6 1.3 reshape.56.attn_gain
  1.9 1.3 reshape.57.attn_shift
  3.2 1.3 reshape.58.glob_gain
  4.4 1.3 reshape.59.glob_shift
  5.7 1.3 reshape.60.ffn_gain
  7.0 1.3 reshape.61.ffn_shift
  8.2 1.3 reshape.63.down_bias
  9.5 186.6 %layer.1 = (bf16[512,768]{1,0:T(8,128)(2,1)}, bf16[128,768]{1,0:T(8,128)(2,1)}, bf16[512,768]{1,0:T(8,128)(2,1)}, bf16[128,768]{1,0:T(8,128)(2,1)}, f32[96,576]{...) custom-call(bf16[512,768]{1,0:T(8,128)(2,1)} %bitcast.23, ...), custom_call_target="tpu_custom_call" | custom-call | tf_op jit(solution)/shard_map/layer/pallas_call | solution.py:1266
  196.1 0.0 copy-start.1
  196.1 0.0 copy-start.2
  196.1 0.0 copy-start
  196.2 1.5 slice_bitcast_fusion
  197.6 1.9 copy.34
  199.5 1.3 reduce
  200.8 2.1 copy.42
  202.8 1.6 copy.43
  204.4 2.1 copy.44
  206.5 1.6 copy.45
  208.1 0.0 copy-done.1
  208.1 0.7 copy.46
  208.8 0.0 copy-done.2
  208.8 0.6 copy.47
  209.5 0.0 copy-done
  209.5 0.7 copy.48
Async XLA Ops:
  196.1 12.0 %copy-start.1 = (f32[96,576]{1,0:T(8,128)S(1)}, f32[96,576]{1,0:T(8,128)}, u32[]{:S(2)}) copy-start(f32[96,576]{1,0:T(8,128)} %get-tuple-element.83) | copy-start | bytes 663556
  196.1 12.7 %copy-start.2 = (f32[96,192]{1,0:T(8,128)S(1)}, f32[96,192]{1,0:T(8,128)}, u32[]{:S(2)}) copy-start(f32[96,192]{1,0:T(8,128)} %get-tuple-element.84) | copy-start | bytes 221188
  196.1 13.3 %copy-start = (f32[96,768]{1,0:T(8,128)S(1)}, f32[96,768]{1,0:T(8,128)}, u32[]{:S(2)}) copy-start(f32[96,768]{1,0:T(8,128)} %get-tuple-element.87) | copy-start | bytes 884740

commit v2 on v1

--- a/solution.py
+++ b/solution.py
@@ -500,13 +500,13 @@
     o_out, o_gout, o_tgrad, o_ggrad, o_qkv, o_wout, o_up, o_down, o_vec, o_ub,
     sec, nrm, proj, kvt, probs, att_t, att, x2, n2, n2t, ct, ct_t, acc, gn2, gatt, qaug, kaug,
     wq, wo, wus, wds,
-    lse_t, rl_t, og_t, msg1, rcv1, cx, rcv2, rcv3, vec, rvec, rll,
-    gd, r0d, r1d, r2d, r3d, r4d, gu, r0u, r1u, r2u, r3u, r4u, r0q, r1qx, r1qy, r2q, r3q, r4q,
+    lse_t, rl_t, cx, msg1, rcv1, rcv2, rcv3, vec, vmsg, vrcv, vsum, rll,
+    gd, r0d, r1d, r2d, r3d, r4d, gu, r0u, r1u, r2u, r3u, r4u, r0q, r1q, r2q, r3q, r4q, both, ymsg, yrcv,
     loc, wsem, hs, hr, m1s, m1r, m2s, m2r, m3s, m3r, gos, gor, ggs_s, ggs_r, vs, vr,
     d0s, d0r, d1s, d1r, d2s, d2r, d3s, d3r, d4s, d4r,
     u0s, u0r, u1s, u1r, u2s, u2r, u3s, u3r, u4s, u4r,
     q0s, q0r, q1s, q1r, q2s, q2r, q3s, q3r, q4s, q4r,
-    hs2, hr2, osem,
+    fs, fr, hs2, hr2, osem,
 ):
     tok, width = tokens.shape
     glob = gstates.shape[0]
@@ -517,7 +517,7 @@
     half = tok // 2
     pairs = HEADS // 2
     chunk = wus.shape[2]
-    n_chunk = up_bias.shape[1] // chunk
+    n_chunk = up_bias.shape[0] // chunk
     tail = 128
 
     s = lax.axis_index("seq")
@@ -543,6 +543,13 @@
         )
 
     peers = tuple(range(1, n_seq))
+
+    def as_row(vector):
+        return vector[...].reshape(1, vector.shape[0])
+
+    attn_gain, attn_shift, glob_gain, glob_shift, ffn_gain, ffn_shift, down_bias = (
+        as_row(v) for v in (attn_gain, attn_shift, glob_gain, glob_shift, ffn_gain, ffn_shift, down_bias)
+    )
 
     my_slots = pl.multiple_of(s * slots, slots)
     loads = [
@@ -594,7 +601,7 @@
     def norm_to(first, count, gain, shift):
         for r in range(first, first + count, 128):
             spread, scale = norm_stats(sec[pl.ds(r, 128), :].astype(F32))
-            nrm[pl.ds(r, 128), :] = (spread * scale * gain[...] + shift[...]).astype(BF)
+            nrm[pl.ds(r, 128), :] = (spread * scale * gain + shift).astype(BF)
 
     def project_rows(first, count):
         def step(i, carry):
@@ -645,7 +652,7 @@
         weights = (raised * (1.0 / total)).astype(BF)
         probs[p, :, pl.ds(2 * tok, 2 * glob)] = weights
         mixed = dot_nn(kvt[pl.ds(at, 128), :], weights)
-        og_t[pl.ds(at, 128), :] = jnp.where(first_head, mixed[:, :glob], mixed[:, glob:])
+        cx[:, pl.ds(at, 128)] = jnp.transpose(jnp.where(first_head, mixed[:, :glob], mixed[:, glob:]))
         logsum = top + jnp.log(total)
         lse_t[pl.ds(2 * p, 1), :] = logsum[:, :glob]
         lse_t[pl.ds(2 * p + 1, 1), :] = logsum[:, glob:]
@@ -661,7 +668,7 @@
     part_b = rest.astype(BF)
     part_c = rest - part_b.astype(F32)
     packed = part_a.astype(F32) + pltpu.roll(part_b.astype(F32), 16, 1) + pltpu.roll(part_c, 32, 1)
-    msg1[:, pl.ds(0, width)] = jnp.transpose(og_t[...]).astype(BF)
+    msg1[:, pl.ds(0, width)] = cx[...].astype(BF)
     msg1[:, pl.ds(width, 128)] = packed.astype(BF)
     sends1 = []
     for k in peers:
@@ -724,7 +731,7 @@
 
     def second_norm(first, count):
         spread, scale = norm_stats(x2[pl.ds(first, count), :])
-        n2[pl.ds(first, count), :] = (spread * scale * ffn_gain[...] + ffn_shift[...]).astype(BF)
+        n2[pl.ds(first, count), :] = (spread * scale * ffn_gain + ffn_shift).astype(BF)
 
     for r in range(0, tok, 128):
         second_norm(r, 128)
@@ -806,6 +813,8 @@
         r3u[...] = r3u[...] + r2u[:, :, zl]
         u_2().start()
 
+    for i in range(n_chunk):
+        rll[pl.ds(i, 1), :] = up_bias[pl.ds(i * chunk, chunk)].reshape(1, chunk)
     acc[...] = jnp.zeros_like(acc)
     gn2[...] = jnp.zeros_like(gn2)
 
@@ -814,7 +823,7 @@
         for copy in stream(i, slot):
             copy.wait()
         at = pl.multiple_of(i * chunk, chunk)
-        hidden = dot_nn(n2[...], wus[slot]) + up_bias[:, pl.ds(at, chunk)]
+        hidden = dot_nn(n2[...], wus[slot]) + rll[pl.ds(i, 1), :]
         active, slope = gelu_pair(hidden)
         active = active.astype(BF)
         gd[i] = dot_nn(ct_t[:, pl.ds(0, wide)], active).astype(BF).reshape(gd.shape[1:])
@@ -855,11 +864,11 @@
 
     def second_pull(first, count):
         grad, gain_term, shift_term = norm_pull(
-            x2[pl.ds(first, count), :], ffn_gain[...], gn2[pl.ds(first, count), :]
+            x2[pl.ds(first, count), :], ffn_gain, gn2[pl.ds(first, count), :]
         )
         upstream = ct[pl.ds(first, count), :].astype(F32)
         total = upstream + grad
-        acc[pl.ds(first, count), :] += x2[pl.ds(first, count), :] + down_bias[...]
+        acc[pl.ds(first, count), :] += x2[pl.ds(first, count), :] + down_bias
         x2[pl.ds(first, count), :] = total
         n2[pl.ds(first, count), :] = total.astype(BF)
         vec[pl.ds(4, 1), :] += gain_term
@@ -942,6 +951,118 @@
     do_u_y(1)
     for copy in sends2:
         copy.wait()
+
+    def chunk_at(p):
+        return gu.at[p // 4, lax.rem(p // 2, 2), lax.rem(p, 2)]
+
+    def put_chunk(p, value):
+        gu[p // 4, lax.rem(p // 2, 2), lax.rem(p, 2)] = value.astype(BF).reshape(gu.shape[3:])
+
+    def q_core(p):
+        i = p // 2
+        return remote(chunk_at(p), r0q.at[i], q0s.at[i], q0r.at[i], dev_c)
+
+    def q_a(i, first):
+        src, dev = (r0q.at[i, :, :, 1 - x], dev_x) if first == "x" else (r0q.at[i, :, :, :, 1 - y], dev_y)
+        return remote(src, r1q.at[i], q1s.at[i], q1r.at[i], dev)
+
+    def q_b(i, first):
+        side_bit, dev = (y, dev_y) if first == "x" else (x, dev_x)
+        return remote(r1q.at[i, :, :, 1 - side_bit], r2q.at[i], q2s.at[i], q2r.at[i], dev)
+
+    def q_1(i):
+        return remote(r2q.at[i, :, 1 - zl], r3q.at[i], q3s.at[i], q3r.at[i], dev_1)
+
+    def q_2(i):
+        return remote(r3q.at[i, 1 - zh], r4q.at[i], q4s.at[i], q4r.at[i], dev_2)
+
+    def by_order(i, act):
+        if isinstance(i, int):
+            act("x" if i % 2 else "y")
+            return
+
+        @pl.when(lax.rem(i, 2) == 1)
+        def _():
+            act("x")
+
+        @pl.when(lax.rem(i, 2) == 0)
+        def _():
+            act("y")
+
+    def do_q_a(p):
+        i = p // 2
+        q_core(p).wait_recv()
+        r0q[i] = r0q[i] + chunk_at(p)[...].reshape(r0q.shape[1:])
+        by_order(i, lambda first: q_a(i, first).start())
+
+    def do_q_b(i):
+        def act(first):
+            q_a(i, first).wait_recv()
+            if first == "x":
+                r1q[i] = r1q[i] + r0q[i, :, :, x]
+            else:
+                r1q[i] = r1q[i] + r0q[i, :, :, :, y]
+            q_b(i, first).start()
+
+        by_order(i, act)
+
+    def do_q_1(i):
+        def act(first):
+            q_b(i, first).wait_recv()
+            r2q[i] = r2q[i] + r1q[i, :, :, y if first == "x" else x]
+
+        by_order(i, act)
+        q_1(i).start()
+
+    def do_q_2(i):
+        q_1(i).wait_recv()
+        r3q[i] = r3q[i] + r2q[i, :, zl]
+        q_2(i).start()
+
+    def m3(p, k):
+        other = flip(k)
+        at = pl.multiple_of(p * glob + other * slots, slots)
+        return remote(wus.at[0, pl.ds(at, slots)], rcv3.at[k - 1, p], m3s.at[p, k], m3r.at[p, k], (other, b))
+
+    def q_chunk(p):
+        own = wus[0, pl.ds(pl.multiple_of(p * glob + s * slots, slots), slots), :].astype(F32)
+        for k in peers:
+            m3(p, k).wait_recv()
+        for k in peers:
+            own = own + rcv3[k - 1, p].astype(F32)
+        own = own.astype(BF)
+        for w in range(3):
+            proj[pl.ds(tok, slots), pl.ds(pl.multiple_of(w * width + p * 128, 128), 128)] = own[
+                :, w * 128 : (w + 1) * 128
+            ]
+        right = jnp.concatenate(
+            [proj[pl.ds(0, wide), pl.ds(pl.multiple_of(w * width + p * 128, 128), 128)] for w in range(3)], axis=1
+        )
+        put_chunk(p, dot_nn(n2t[:, pl.ds(0, wide)], right))
+        send_chunk(p)
+
+    def send_chunk(p):
+        @pl.when(lax.rem(p, 2) != c)
+        def _():
+            q_core(p).start()
+
+    def tick(p):
+        for back, act in ((5, do_q_2), (4, do_q_1), (3, do_q_b), (2, do_q_a)):
+            q = p - back
+            if isinstance(p, int) and not 0 <= q < pairs:
+                continue
+            mine = lax.rem(q, 2) == c if isinstance(q, int) else (q >= 0) & (lax.rem(q, 2) == c)
+
+            @pl.when(mine)
+            def _(act=act, q=q):
+                act(q if act is do_q_a else q // 2)
+
+    for yy in range(2):
+        for j in range(2):
+            u_core(yy, j).wait_send()
+    for h in range(2):
+        put_chunk(pairs + h, dot_nn(att_t[:, pl.ds(0, wide)], n2[:, pl.ds(h * 384, 384)]))
+        send_chunk(pairs + h)
 
     minus = jnp.where(lanes_of((rows, 128)) < 32, -1.0, 0.0).astype(BF)
 
@@ -977,117 +1098,62 @@
         grad_q = jnp.concatenate([low, upper], axis=0) * factor
         own = dot_nn(kvt[pl.ds(at, 128), :], probs[p, :, pl.ds(2 * tok, 2 * glob)])
         own = jnp.where(first_head, own[:, :glob], own[:, glob:]) * factor
+        stage = pl.ds(pl.multiple_of(p * glob, glob), glob)
+        wus[0, stage, pl.ds(0, 128)] = jnp.transpose(own).astype(BF)
+        wus[0, stage, pl.ds(128, 128)] = grad_k[tok:].astype(BF)
+        wus[0, stage, pl.ds(256, 128)] = grad_v[tok:].astype(BF)
+        for k in peers:
+            m3(p, k).start()
         proj[pl.ds(0, tok), pl.ds(at, 128)] = jnp.transpose(grad_q).astype(BF)
-        proj[pl.ds(tok, glob), pl.ds(at, 128)] = jnp.transpose(own).astype(BF)
-        proj[:, pl.ds(width + at, 128)] = grad_k.astype(BF)
-        proj[:, pl.ds(2 * width + at, 128)] = grad_v.astype(BF)
-
-        @pl.when(p == 2)
+        proj[pl.ds(0, tok), pl.ds(width + at, 128)] = grad_k[:tok].astype(BF)
+        proj[pl.ds(0, tok), pl.ds(2 * width + at, 128)] = grad_v[:tok].astype(BF)
+
+        @pl.when(p == 0)
         def _():
             do_d_1(0)
             do_d_1(1)
 
+        @pl.when(p == 1)
+        def _():
+            do_u_1()
+            own_out_chunk(do_q_a, lambda: pairs + c)
+
+        @pl.when(p == 2)
+        def _():
+            do_d_2()
+            own_out_chunk(do_q_b, lambda: 3)
+
         @pl.when(p == 3)
         def _():
-            do_u_1()
+            do_u_2()
+            own_out_chunk(do_q_1, lambda: 3)
 
         @pl.when(p == 4)
         def _():
-            do_d_2()
-
-        @pl.when(p == 5)
+            own_out_chunk(do_q_2, lambda: 3)
+
+        @pl.when(p >= 1)
         def _():
-            do_u_2()
-
+            q_chunk(p - 1)
+
+        tick(p)
         return carry
 
+    def own_out_chunk(act, which):
+        act(which())
+
     lax.fori_loop(0, pairs, attention_back, 0)
-
-    sends3 = []
-    for k in peers:
-        other = flip(k)
-        at = pl.multiple_of(tok + other * slots, slots)
-        copy = remote(proj.at[pl.ds(at, slots)], rcv3.at[k - 1], m3s.at[k], m3r.at[k], (other, b))
-        copy.start()
-        sends3.append(copy)
-
-    total3 = proj[pl.ds(pl.multiple_of(tok + my_slots, slots), slots), :].astype(F32)
-    for copy in sends3:
-        copy.wait()
-    for k in peers:
-        total3 = total3 + rcv3[k - 1].astype(F32)
-    proj[pl.ds(tok, slots), :] = total3.astype(BF)
-
-    for yy in range(2):
-        for j in range(2):
-            u_core(yy, j).wait_send()
-
-    def q_block(yy, cc):
-        bb = 2 * yy + cc
-        odd_b = cc == 1
-        at = pl.multiple_of(bb * 576 - 64 * cc, 128)
-        window = proj[pl.ds(0, wide), pl.ds(at, 640)].astype(F32)
-        window = jnp.where(odd_b, pltpu.roll(window, 576, 1), window).astype(BF)
-        at = pl.multiple_of(bb * 192 - 64 * cc, 128)
-        branch = n2[:, pl.ds(at, 256)].astype(F32)
-        branch = jnp.where(odd_b, branch, pltpu.roll(branch, 64, 1)).astype(BF)
-        first = dot_nn(n2t[:, pl.ds(0, wide)], window[:, :384])
-        second = dot_nn(n2t[:, pl.ds(0, wide)], window[:, 384:])
-        third = dot_nn(att_t[:, pl.ds(0, wide)], branch)
-        middle = jnp.where(lanes_of((width, 128)) < 64, second[:, 128:], third[:, :128])
-        return first, jnp.concatenate([second[:, :128], middle, third[:, 128:]], axis=1)
-
-    def q_core(yy, j):
-        return remote(gu.at[yy, 1 - c, j], r0q.at[yy, j], q0s.at[yy * 2 + j], q0r.at[yy * 2 + j], dev_c)
-
-    def q_first(yy, carry):
-        for j, block in enumerate(q_block(yy, 1 - c)):
-            gu[yy, 1 - c, j] = block.astype(BF).reshape(gu.shape[3:])
-            q_core(yy, j).start()
-        return carry
-
-    lax.fori_loop(0, 2, q_first, 0)
-
-    gn2[...] = dot_nt(proj[pl.ds(0, wide), :], wq[...])
-
-    def q_x0(yy):
-        return remote(r0q.at[yy, 0, :, :, 1 - x], r1qx.at[yy], q1s.at[yy], q1r.at[yy], dev_x)
-
-    def q_y0():
-        return remote(r1qx.at[1 - y], r2q.at[0], q2s.at[0], q2r.at[0], dev_y)
-
-    def q_y1():
-        return remote(r0q.at[1 - y, 1], r1qy, q1s.at[2], q1r.at[2], dev_y)
-
-    def q_x1():
-        return remote(r1qy.at[:, :, 1 - x], r2q.at[1], q2s.at[1], q2r.at[1], dev_x)
-
-    def q_1():
-        return remote(r2q.at[:, :, 1 - zl], r3q, q3s.at[0], q3r.at[0], dev_1)
-
-    def q_2():
-        return remote(r3q.at[:, 1 - zh], r4q, q4s.at[0], q4r.at[0], dev_2)
-
-    def q_second(yy, carry):
-        first, second = q_block(yy, c)
-        q_core(yy, 0).wait_recv()
-        r0q[yy, 0] = (r0q[yy, 0].astype(F32) + first.reshape(gu.shape[3:])).astype(BF)
-        q_x0(yy).start()
-        q_core(yy, 1).wait_recv()
-        r0q[yy, 1] = (r0q[yy, 1].astype(F32) + second.reshape(gu.shape[3:])).astype(BF)
-        return carry
-
-    lax.fori_loop(0, 2, q_second, 0)
-    q_y1().start()
 
     def first_pull(first):
         grad, gain_term, shift_term = norm_pull(
-            sec[pl.ds(first, 128), :].astype(F32), attn_gain[...], gn2[pl.ds(first, 128), :]
+            sec[pl.ds(first, 128), :].astype(F32), attn_gain, gn2[pl.ds(first, 128), :]
         )
         n2[pl.ds(first, 128), :] = (grad + x2[pl.ds(first, 128), :]).astype(BF)
         vec[pl.ds(0, 1), :] += gain_term
         vec[pl.ds(1, 1), :] += shift_term
 
+    tick(6)
+    gn2[pl.ds(half, half), :] = dot_nt(proj[pl.ds(half, half), :], wq[...])
     for r in range(half, tok, 128):
         first_pull(r)
     back = remote(
@@ -1095,14 +1161,19 @@
         (lax.rem(s + 1, n_seq), b),
     )
     back.start()
+
+    q_chunk(pairs - 1)
+
+    gn2[pl.ds(0, half), :] = dot_nt(proj[pl.ds(0, half), :], wq[...])
     for r in range(0, half, 128):
         first_pull(r)
     keep = pltpu.make_async_copy(n2.at[pl.ds(0, half)], o_tgrad.at[pl.ds(half, half)], osem.at[2])
     keep.start()
-
+    tick(7)
+    gn2[pl.ds(tok, slots), :] = dot_nt(proj[pl.ds(tok, slots), :], wq[...])
     grad, gain_term, shift_term = norm_pull(
         sec[pl.ds(pl.multiple_of(tok + my_slots, slots), slots), :].astype(F32),
-        glob_gain[...],
+        glob_gain,
         gn2[pl.ds(tok, slots), :],
     )
     vec[pl.ds(2, 1), :] += gain_term
@@ -1121,53 +1192,80 @@
         copy.start()
         sends_g.append(copy)
 
-    def vec_step(k, dev):
-        return remote(vec, rvec.at[k], vs.at[k], vr.at[k], dev)
-
-    def vec_add(k, dev):
-        vec_step(k, dev).wait()
-        vec[...] += rvec[k]
-
-    vec_step(0, dev_c).start()
+    share = vec.shape[1] // n_seq
+    for j in range(n_seq):
+        rolled = vec[pl.ds(0, 8), :]
+        if j:
+            rolled = pltpu.roll(rolled, vec.shape[1] - share * j, 1)
+        vmsg[j, :, pl.ds(0, 128)] = rolled[:, :128]
+        vmsg[j, :, pl.ds(128, chunk)] = jnp.broadcast_to(
+            vec[pl.ds(8 + j // 2, 1), pl.ds((j % 2) * chunk, chunk)], (8, chunk)
+        )
+    sends_v = []
+    for k in peers:
+        copy = remote(vmsg.at[flip(k)], vrcv.at[k - 1], vs.at[k], vr.at[k], (flip(k), b))
+        copy.start()
+        sends_v.append(copy)
+
     d_2().wait_recv()
-    o_down[...] = jnp.transpose(r4d[...].astype(F32) + r3d[zh].astype(F32))
+    o_down[...] = r4d[...].astype(F32) + r3d[zh].astype(F32)
     u_2().wait_recv()
     last = r4u[...].astype(F32) + r3u[:, zh].astype(F32)
-    o_up[:, pl.ds(0, 384)] = last[0]
-    o_up[:, pl.ds(384, 384)] = last[1]
-    vec_add(0, dev_c)
-    vec_step(1, dev_y).start()
-    for yy in range(2):
-        q_x0(yy).wait_recv()
-        r1qx[yy] = r1qx[yy] + r0q[yy, 0, :, :, x]
-    q_y0().start()
-    vec_add(1, dev_y)
-    vec_step(2, dev_x).start()
-    q_y1().wait_recv()
-    r1qy[...] = r1qy[...] + r0q[y, 1]
-    q_x1().start()
-    vec_add(2, dev_x)
-    vec_step(3, dev_1).start()
-    q_y0().wait_recv()
-    r2q[0] = r2q[0] + r1qx[y]
-    q_x1().wait_recv()
-    r2q[1] = r2q[1] + r1qy[:, :, x]
-    q_1().start()
-    vec_add(3, dev_1)
-    vec_step(4, dev_2).start()
-    q_1().wait_recv()
-    r3q[...] = r3q[...] + r2q[:, :, zl]
-    q_2().start()
-    vec_add(4, dev_2)
-    share = vec.shape[1] // n_seq
-    turned = pltpu.roll(vec[pl.ds(0, 8), :], lax.rem(vec.shape[1] - share * s, vec.shape[1]), 1)
-    o_vec[...] = turned[:, :share]
-    o_ub[...] = vec[pl.ds(8 + s // 2, 1), pl.ds(pl.multiple_of((s % 2) * chunk, chunk), chunk)]
-    q_2().wait_recv()
-    last = r4q[...].astype(F32) + r3q[:, zh].astype(F32)
-    o_qkv[:, pl.ds(0, 384)] = last[0]
-    o_qkv[:, pl.ds(384, 192)] = last[1][:, :192]
-    o_wout[...] = last[1][:, 192:]
+    o_up[:, pl.ds(0, 384)] = last[0].reshape(96, 384)
+    o_up[:, pl.ds(384, 384)] = last[1].reshape(96, 384)
+
+    tick(8)
+    for copy in sends_v:
+        copy.wait()
+    vsum[0] = vmsg[s]
+    for k in peers:
+        vsum[0] = vsum[0] + vrcv[k - 1]
+    v_core = remote(vsum.at[0], vsum.at[1], vs.at[0], vr.at[0], dev_c)
+    v_core.start()
+    tick(9)
+    v_core.wait()
+    vsum[2] = vsum[0] + vsum[1]
+    v_y = remote(vsum.at[2], vsum.at[3], vs.at[8], vr.at[8], dev_y)
+    v_y.start()
+    tick(10)
+    v_y.wait()
+    shared = vsum[2] + vsum[3]
+    o_vec[...] = shared[:, :share]
+    o_ub[...] = shared[0:1, 128:]
+
+    for i in range(4):
+        q_2(i).wait_recv()
+        both[c, i] = r4q[i] + r3q[i, zh]
+    f_core = remote(both.at[c], both.at[c], fs.at[0], fr.at[0], dev_c)
+    f_core.start()
+    f_core.wait()
+
+    def columns_of(bb):
+        tiles = []
+        for n in range(5):
+            tile = (bb * 576 - 64 * c) // 128 + n
+            which, pair = tile // 6, lax.rem(tile, 6)
+            tiles.append(both[lax.rem(pair, 2), pair // 2, :, pl.ds(pl.multiple_of(which * 128, 128), 128)])
+        for n in range(2):
+            tile = (bb * 192 - 64 * c) // 128 + n
+            tiles.append(both[tile // 3, 3, :, pl.ds(pl.multiple_of(lax.rem(tile, 3) * 128, 128), 128)])
+        return jnp.concatenate(tiles, axis=1)
+
+    ymsg[...] = columns_of(b + 2 - 4 * y)
+    f_y = remote(ymsg, yrcv, fs.at[1], fr.at[1], dev_y)
+    f_y.start()
+
+    def put_columns(yy, block):
+        block = block.astype(F32)
+        at = pl.multiple_of(yy * 48, 48)
+        main = block[:, :640]
+        o_qkv[pl.ds(at, 48), :] = jnp.where(c == 1, pltpu.roll(main, 576, 1), main)[:, :576]
+        main = block[:, 640:]
+        o_wout[pl.ds(at, 48), :] = jnp.where(c == 1, pltpu.roll(main, 192, 1), main)[:, :192]
+
+    put_columns(y, columns_of(b))
+    f_y.wait()
+    put_columns(1 - y, yrcv[...])
 
     for i in range(8):
         d_core(i).wait_send()
@@ -1180,16 +1278,17 @@
     for yy in range(2):
         for j in range(2):
             u_x(yy, j).wait_send()
-            q_core(yy, j).wait_send()
         u_y(yy).wait_send()
-        q_x0(yy).wait_send()
     u_1().wait_send()
     u_2().wait_send()
-    q_y0().wait_send()
-    q_y1().wait_send()
-    q_x1().wait_send()
-    q_1().wait_send()
-    q_2().wait_send()
+    for i in range(4):
+        q_core(2 * i + 1 - c).wait_send()
+        by_order(i, lambda first, i=i: (q_a(i, first).wait_send(), q_b(i, first).wait_send()))
+        q_1(i).wait_send()
+        q_2(i).wait_send()
+    for p in range(pairs):
+        for k in peers:
+            m3(p, k).wait_send()
     back.wait()
     keep.wait()
     own_grad.wait()
@@ -1208,6 +1307,15 @@
         and w_qkv.shape == (HEADS * HEAD_DIM, 3 * HEADS * HEAD_DIM)
         and w_up.shape == (HEADS * HEAD_DIM, 3072)
     )
+
+
+def finish_kernel(*refs):
+    ins, outs = refs[:10], refs[10:]
+    for i in range(8):
+        outs[i][...] = ins[i][...]
+    for i in range(7):
+        outs[8 + i][...] = ins[8][i, :]
+    outs[15][...] = ins[9][0, :]
 
 
 def fused(
@@ -1242,26 +1350,23 @@
         low(wide, width), low(width, tok + 128), low(wide, width), low(width, tok + 128),
         full(wide, width), full(wide, width), low(wide, width), low(rows, 128), low(rows, 128),
         low(width, 3 * width), low(width, width), low(2, width, chunk), low(2, chunk, width),
-        full(128, glob), full(16, tok), full(width, glob), low(glob, width + 128),
-        low(n_seq, slots, width + 128), full(glob, width), low(glob, width + 128),
-        low(n_seq - 1, slots, 3 * width),
-        full(16, width), full(5, 16, width), full(8, chunk),
+        full(128, glob), full(16, tok), full(glob, width), low(glob, width + 128),
+        low(n_seq, slots, width + 128), low(glob, width + 128),
+        low(n_seq - 1, pairs, slots, chunk),
+        full(16, width), full(n_seq, 8, 128 + chunk), full(n_seq - 1, 8, 128 + chunk), full(4, 8, 128 + chunk), full(8, chunk),
         low(8, 2, 2, side, chunk), low(8, 2, side, chunk), low(8, side, chunk), low(4, side, chunk),
         low(2, side, chunk), low(side, chunk),
-        low(2, 2, 2, 2, 2, 2, part, chunk), low(2, 2, 2, 2, 2, part, chunk), low(2, 2, 2, 2, part, chunk),
-        low(2, 2, 2, part, chunk), low(2, 2, part, chunk), low(2, part, chunk),
-        low(2, 2, 2, 2, 2, part, chunk), low(2, 2, 2, part, chunk), low(2, 2, 2, part, chunk),
-        low(2, 2, 2, part, chunk), low(2, 2, part, chunk), low(2, part, chunk),
+        *[low(*[2] * n, part // 2, chunk) for n in (7, 6, 5, 4, 3, 2)],
+        low(4, 2, 2, 2, 2, part // 2, chunk), low(4, 2, 2, 2, part // 2, chunk), low(4, 2, 2, part // 2, chunk),
+        low(4, 2, part // 2, chunk), low(4, part // 2, chunk), low(2, 4, part // 2, chunk),
+        low(part // 2, 896), low(part // 2, 896),
         dma((8,)), dma((2, 2)), dma((1,)), dma((1,)),
-        *[dma((8,)) for _ in range(10)], dma((5,)), dma((5,)),
+        *[dma((8,)) for _ in range(4)], dma((pairs, 8)), dma((pairs, 8)), *[dma((8,)) for _ in range(4)], dma((9,)), dma((9,)),
         dma((8,)), dma((8,)), dma((8,)), dma((8,)), dma((4,)), dma((4,)), dma((2,)), dma((2,)), dma((1,)), dma((1,)),
         dma((4,)), dma((4,)), dma((4,)), dma((4,)), dma((2,)), dma((2,)), dma((1,)), dma((1,)), dma((1,)), dma((1,)),
-        dma((4,)), dma((4,)), dma((3,)), dma((3,)), dma((2,)), dma((2,)), dma((1,)), dma((1,)), dma((1,)), dma((1,)),
-        dma((1,)), dma((1,)), dma((4,)),
+        *[dma((4,)) for _ in range(10)],
+        dma((2,)), dma((2,)), dma((1,)), dma((1,)), dma((4,)),
     ]
-
-    def row(vector):
-        return vector.reshape(1, -1)
 
     results = pl.pallas_call(
         layer_kernel,
@@ -1273,7 +1378,7 @@
             jax.ShapeDtypeStruct((part, 3 * side), F32),
             jax.ShapeDtypeStruct((part, side), F32),
             jax.ShapeDtypeStruct((part, 2 * chunk), F32),
-            jax.ShapeDtypeStruct((chunk, side), F32),
+            jax.ShapeDtypeStruct((side, chunk), F32),
             jax.ShapeDtypeStruct((8, part), F32),
             jax.ShapeDtypeStruct((1, chunk), F32),
         ],
@@ -1286,14 +1391,24 @@
         ),
         name="layer",
     )(
-        tokens[0], global_states[0], token_seg, global_seg, row(attn_gain), row(attn_shift), row(glob_gain),
-        row(glob_shift), w_qkv, w_out, row(ffn_gain), row(ffn_shift), w_up, row(up_bias), w_down, row(down_bias),
+        tokens[0], global_states[0], token_seg, global_seg, attn_gain, attn_shift, glob_gain,
+        glob_shift, w_qkv, w_out, ffn_gain, ffn_shift, w_up, up_bias, w_down, down_bias,
         out_cotangent[0], global_cotangent[0],
     )
-    out, gout, tgrad, ggrad, g_qkv, g_out, g_up, g_down, g_vec, g_ub = results
+    *large, vectors, ub = results
+    results = pl.pallas_call(
+        finish_kernel,
+        out_shape=[jax.ShapeDtypeStruct(one.shape, one.dtype) for one in large]
+        + [jax.ShapeDtypeStruct((part,), F32)] * 7
+        + [jax.ShapeDtypeStruct((chunk,), F32)],
+        in_specs=[vmem()] * 10,
+        out_specs=[vmem()] * 16,
+        name="results",
+    )(*large, vectors, ub)
+    out, gout, tgrad, ggrad, g_qkv, g_out, g_up, g_down, *g_vec, g_ub = results
     return (
         out[None], gout[None], tgrad[None], ggrad[None], g_vec[0], g_vec[1], g_vec[2], g_vec[3], g_qkv, g_out,
-        g_vec[4], g_vec[5], g_up, g_ub[0], g_down, g_vec[6],
+        g_vec[4], g_vec[5], g_up, g_ub, g_down.T, g_vec[6],
     )
 
 

time: 212 us -> 171 us (0.81)
  local copies, waits for them, and re-layouts: 21.6 us -> 0 us
  Pallas kernels: 187 us -> 167 us
    pallas_call x1, Pallas kernels: 187 us -> 164 us  [fused(): pl.pallas_call(layer_kernel, out_shape=[jax.ShapeDtypeStruct((tok, width)...]
    unnamed x14 -> x0, local copies, waits for them, and re-layouts: 11.3 us -> none
    reshape x7 -> x0, local copies, waits for them, and re-layouts: 8.87 us -> none  [row(): return vector.reshape(1, -1)]
    pallas_call x0 -> x1, Pallas kernels: none -> 3.47 us  [fused(): pl.pallas_call(finish_kernel, out_shape=[jax.ShapeDtypeStruct(one.shape,...]
where the time goes in v2:
time: 171 us; the launch traced here: 168 us
  Pallas kernels  167 us (98%)
    pallas_call x1, Pallas kernels, fused(): pl.pallas_call(layer_kernel, out_shape=[jax.ShapeDtypeStruct((tok, width)...  164 us
    pallas_call x1, Pallas kernels, fused(): pl.pallas_call(finish_kernel, out_shape=[jax.ShapeDtypeStruct(one.shape,...  3.47 us

profile of v2, /device:TPU:2, one launch (start us, length us, event | category | flops | bytes accessed | tf_op | source)
XLA Modules:
  0.0 168.1 jit_solution(10161275220562959931)
XLA Ops:
  0.7 163.8 %layer.1 = (bf16[512,768]{1,0:T(8,128)(2,1)}, bf16[128,768]{1,0:T(8,128)(2,1)}, bf16[512,768]{1,0:T(8,128)(2,1)}, bf16[128,768]{1,0:T(8,128)(2,1)}, f32[96,576]{...) custom-call(bf16[512,768]{1,0:T(8,128)(2,1)} %bitcast.9, ...), custom_call_target="tpu_custom_call" | custom-call | tf_op jit(solution)/shard_map/layer/pallas_call | solution.py:1371
  164.5 3.5 %results.1 = (bf16[512,768]{1,0:T(8,128)(2,1)}, bf16[128,768]{1,0:T(8,128)(2,1)}, bf16[512,768]{1,0:T(8,128)(2,1)}, bf16[128,768]{1,0:T(8,128)(2,1)}, f32[96,576...) custom-call(bf16[512,768]{1,0:T(8,128)(2,1)} %get-tuple-element.42.r, ...), custom_call_target="tpu_custom_call" | custom-call | tf_op jit(solution)/shard_map/results/pallas_call | solution.py:1399

commit v3 on v1

--- a/solution.py
+++ b/solution.py
@@ -499,14 +499,14 @@
     ffn_gain, ffn_shift, w_up, up_bias, w_down, down_bias, cotan, gcotan,
     o_out, o_gout, o_tgrad, o_ggrad, o_qkv, o_wout, o_up, o_down, o_vec, o_ub,
     sec, nrm, proj, kvt, probs, att_t, att, x2, n2, n2t, ct, ct_t, acc, gn2, gatt, qaug, kaug,
-    wq, wo, wus, wds,
-    lse_t, rl_t, og_t, msg1, rcv1, cx, rcv2, rcv3, vec, rvec, rll,
-    gd, r0d, r1d, r2d, r3d, r4d, gu, r0u, r1u, r2u, r3u, r4u, r0q, r1qx, r1qy, r2q, r3q, r4q,
+    wq, wo, wu, wd,
+    lse_t, rl_t, cx, msg1, rcv1, rcv2, rcv3, vec, vmsg, vrcv, vsum, ub,
+    gd, r0d, r1d, r2d, r3d, r4d, gu, r0u, r1u, r2u, r3u, r4u, r0q, r1q, r2q, r3q, r4q, fmsg, frcv,
     loc, wsem, hs, hr, m1s, m1r, m2s, m2r, m3s, m3r, gos, gor, ggs_s, ggs_r, vs, vr,
     d0s, d0r, d1s, d1r, d2s, d2r, d3s, d3r, d4s, d4r,
     u0s, u0r, u1s, u1r, u2s, u2r, u3s, u3r, u4s, u4r,
     q0s, q0r, q1s, q1r, q2s, q2r, q3s, q3r, q4s, q4r,
-    hs2, hr2, osem,
+    qps, qpr, qls, qlr, vbs, vbr, fs, fr, hs2, hr2, osem,
 ):
     tok, width = tokens.shape
     glob = gstates.shape[0]
@@ -516,8 +516,9 @@
     wide = tok + slots
     half = tok // 2
     pairs = HEADS // 2
-    chunk = wus.shape[2]
-    n_chunk = up_bias.shape[1] // chunk
+    chunk = up_bias.shape[0] // n_seq
+    n_chunk = up_bias.shape[0] // width
+    side, part = width // 4, width // n_seq
     tail = 128
 
     s = lax.axis_index("seq")
@@ -525,6 +526,7 @@
     x, zl, zh = s % 2, (s // 2) % 2, s // 4
     c, y = b % 2, b // 2
     dev_c, dev_y = (s, b + 1 - 2 * c), (s, b + 2 - 4 * y)
+    dev_cy, dev_xy = (s, dev_y[1] + 1 - 2 * c), (s + 1 - 2 * x, dev_y[1])
     dev_x, dev_1, dev_2 = (s + 1 - 2 * x, b), (s + 2 - 4 * zl, b), (s + 4 - 8 * zh, b)
 
     def flip(k):
@@ -543,6 +545,13 @@
         )
 
     peers = tuple(range(1, n_seq))
+
+    def as_row(vector):
+        return vector[...].reshape(1, vector.shape[0])
+
+    attn_gain, attn_shift, glob_gain, glob_shift, ffn_gain, ffn_shift, down_bias = (
+        as_row(v) for v in (attn_gain, attn_shift, glob_gain, glob_shift, ffn_gain, ffn_shift, down_bias)
+    )
 
     my_slots = pl.multiple_of(s * slots, slots)
     loads = [
@@ -557,23 +566,29 @@
     for load in loads:
         load.start()
 
-    def stream(i, slot):
-        at = pl.multiple_of(i * chunk, chunk)
-        return (
-            pltpu.make_async_copy(w_up.at[:, pl.ds(at, chunk)], wus.at[slot], wsem.at[0, slot]),
-            pltpu.make_async_copy(w_down.at[pl.ds(at, chunk)], wds.at[slot], wsem.at[1, slot]),
-        )
-
-    for i in range(2):
-        for copy in stream(i, i):
-            copy.start()
+    def piece_of(i, o):
+        return 4 * (i // 2) + 2 * o + i % 2
+
+    def stream(i):
+        copies = []
+        for o in range(2):
+            at = piece_of(i, o) * chunk
+            at = at if isinstance(at, int) else pl.multiple_of(at, chunk)
+            here = pl.ds(o * chunk, chunk)
+            copies.append(pltpu.make_async_copy(w_up.at[:, pl.ds(at, chunk)], wu.at[:, here], wsem.at[0, o]))
+            copies.append(pltpu.make_async_copy(w_down.at[pl.ds(at, chunk)], wd.at[here], wsem.at[1, o]))
+        return copies
+
+    for copy in stream(0):
+        copy.start()
 
     bar = pltpu.get_barrier_semaphore()
     for k in peers:
         pl.semaphore_signal(bar, inc=1, device_id=(flip(k), b), device_id_type=MESH)
     pl.semaphore_signal(bar, inc=1, device_id=dev_c, device_id_type=MESH)
-    pl.semaphore_signal(bar, inc=1, device_id=dev_y, device_id_type=MESH)
-    pl.semaphore_wait(bar, len(peers) + 2)
+    for dev in (dev_y, dev_cy, dev_xy):
+        pl.semaphore_signal(bar, inc=1, device_id=dev, device_id_type=MESH)
+    pl.semaphore_wait(bar, len(peers) + 4)
     halo = remote(
         tokens.at[pl.ds(0, half)], sec.at[pl.ds(half, half)], hs.at[0], hr.at[0],
         (lax.rem(s + n_seq - 1, n_seq), b),
@@ -594,7 +609,7 @@
     def norm_to(first, count, gain, shift):
         for r in range(first, first + count, 128):
             spread, scale = norm_stats(sec[pl.ds(r, 128), :].astype(F32))
-            nrm[pl.ds(r, 128), :] = (spread * scale * gain[...] + shift[...]).astype(BF)
+            nrm[pl.ds(r, 128), :] = (spread * scale * gain + shift).astype(BF)
 
     def project_rows(first, count):
         def step(i, carry):
@@ -620,7 +635,7 @@
     norm_to(half, half, attn_gain, attn_shift)
     project_rows(half, half)
 
-    kvt[...] = jnp.transpose(proj[:, pl.ds(2 * width, width)])
+    kvt[:, pl.ds(0, rows)] = jnp.transpose(proj[:, pl.ds(2 * width, width)])
     lane_p = lanes_of((1, 128))
     even = jnp.where(lane_p < HEAD_DIM, HEAD_DIM ** (-0.5), 0.0).astype(BF)
     odd = jnp.where(lane_p < HEAD_DIM, 0.0, HEAD_DIM ** (-0.5)).astype(BF)
@@ -644,8 +659,8 @@
         total = jnp.sum(raised, axis=0, keepdims=True)
         weights = (raised * (1.0 / total)).astype(BF)
         probs[p, :, pl.ds(2 * tok, 2 * glob)] = weights
-        mixed = dot_nn(kvt[pl.ds(at, 128), :], weights)
-        og_t[pl.ds(at, 128), :] = jnp.where(first_head, mixed[:, :glob], mixed[:, glob:])
+        mixed = dot_nn(kvt[pl.ds(at, 128), pl.ds(0, rows)], weights)
+        cx[:, pl.ds(at, 128)] = jnp.transpose(jnp.where(first_head, mixed[:, :glob], mixed[:, glob:]))
         logsum = top + jnp.log(total)
         lse_t[pl.ds(2 * p, 1), :] = logsum[:, :glob]
         lse_t[pl.ds(2 * p + 1, 1), :] = logsum[:, glob:]
@@ -661,7 +676,7 @@
     part_b = rest.astype(BF)
     part_c = rest - part_b.astype(F32)
     packed = part_a.astype(F32) + pltpu.roll(part_b.astype(F32), 16, 1) + pltpu.roll(part_c, 32, 1)
-    msg1[:, pl.ds(0, width)] = jnp.transpose(og_t[...]).astype(BF)
+    msg1[:, pl.ds(0, width)] = cx[...].astype(BF)
     msg1[:, pl.ds(width, 128)] = packed.astype(BF)
     sends1 = []
     for k in peers:
@@ -686,7 +701,7 @@
             probs[p, :, pl.ds(e * tok, tok)] = weights
             rl_t[pl.ds(2 * p + e, 1), :] = inverse
             here = pl.multiple_of(at + e * HEAD_DIM, HEAD_DIM)
-            mixed = dot_nn(kvt[pl.ds(here, HEAD_DIM), :], weights)
+            mixed = dot_nn(kvt[pl.ds(here, HEAD_DIM), pl.ds(0, rows)], weights)
             att_t[pl.ds(here, HEAD_DIM), pl.ds(0, tok)] = (mixed * inverse).astype(BF)
         return carry
 
@@ -724,7 +739,7 @@
 
     def second_norm(first, count):
         spread, scale = norm_stats(x2[pl.ds(first, count), :])
-        n2[pl.ds(first, count), :] = (spread * scale * ffn_gain[...] + ffn_shift[...]).astype(BF)
+        n2[pl.ds(first, count), :] = (spread * scale * ffn_gain + ffn_shift).astype(BF)
 
     for r in range(0, tok, 128):
         second_norm(r, 128)
@@ -732,134 +747,154 @@
     n2t[:, pl.ds(0, wide)] = jnp.transpose(n2[...])
 
     def d_core(i):
-        return remote(gd.at[i, :, 1 - c], r0d.at[i], d0s.at[i], d0r.at[i], dev_c)
+        return remote(gd.at[i, :, :, 1 - c], r0d.at[i], d0s.at[i], d0r.at[i], dev_c)
 
     def d_y(i):
-        return remote(r0d.at[i, 1 - y], r1d.at[i], d1s.at[i], d1r.at[i], dev_y)
-
-    def d_x(z):
-        return remote(r1d.at[2 * z + 1 - x], r2d.at[z], d2s.at[z], d2r.at[z], dev_x)
+        return remote(r0d.at[i, :, 1 - y], r1d.at[i // 2, i % 2], d1s.at[i], d1r.at[i], dev_y)
+
+    def d_x(h):
+        return remote(r1d.at[h, 1 - x], r2d.at[h], d2s.at[h], d2r.at[h], dev_x)
 
     def d_1(h):
-        return remote(r2d.at[2 * h + 1 - zl], r3d.at[h], d3s.at[h], d3r.at[h], dev_1)
+        return remote(r2d.at[h, 1 - zl], r3d.at[h], d3s.at[h], d3r.at[h], dev_1)
 
     def d_2():
         return remote(r3d.at[1 - zh], r4d, d4s.at[0], d4r.at[0], dev_2)
 
     def do_d_y(i):
         d_core(i).wait_recv()
-        r0d[i] = r0d[i] + gd[i, :, c]
+        r0d[i] = r0d[i] + gd[i, :, :, c]
         d_y(i).start()
 
-    def do_d_x(z):
-        for o in range(2):
-            d_y(2 * z + o).wait_recv()
-            r1d[2 * z + o] = r1d[2 * z + o] + r0d[2 * z + o, y]
-        d_x(z).start()
+    def do_d_x(h):
+        for j in range(2):
+            d_y(2 * h + j).wait_recv()
+            r1d[h, j] = r1d[h, j] + r0d[2 * h + j, :, y]
+        d_x(h).start()
 
     def do_d_1(h):
-        for o in range(2):
-            d_x(2 * h + o).wait_recv()
-            r2d[2 * h + o] = r2d[2 * h + o] + r1d[2 * (2 * h + o) + x]
+        d_x(h).wait_recv()
+        r2d[h] = r2d[h] + r1d[h, x]
         d_1(h).start()
 
     def do_d_2():
         for h in range(2):
             d_1(h).wait_recv()
-            r3d[h] = r3d[h] + r2d[2 * h + zl]
+            r3d[h] = r3d[h] + r2d[h, zl]
         d_2().start()
 
-    def u_core(yy, j):
-        return remote(gu.at[yy, 1 - c, j], r0u.at[yy, j], u0s.at[yy * 2 + j], u0r.at[yy * 2 + j], dev_c)
-
-    def u_x(yy, j):
-        return remote(r0u.at[yy, j, :, :, 1 - x], r1u.at[yy, j], u1s.at[yy * 2 + j], u1r.at[yy * 2 + j], dev_x)
-
-    def u_y(j):
-        return remote(r1u.at[1 - y, j], r2u.at[j], u2s.at[j], u2r.at[j], dev_y)
-
-    def u_1():
-        return remote(r2u.at[:, :, 1 - zl], r3u, u3s.at[0], u3r.at[0], dev_1)
+    def u_core(i):
+        return remote(gu.at[i, 1 - c], r0u.at[i], u0s.at[i], u0r.at[i], dev_c)
+
+    def u_1(i):
+        return remote(r0u.at[i, :, 1 - zl], r1u.at[i], u1s.at[i], u1r.at[i], dev_1)
+
+    def u_x(i):
+        return remote(r1u.at[i, :, 1 - x], r2u.at[i // 2, i % 2], u2s.at[i], u2r.at[i], dev_x)
+
+    def u_y():
+        return remote(r2u.at[1 - y], r3u, u3s.at[0], u3r.at[0], dev_y)
 
     def u_2():
         return remote(r3u.at[:, 1 - zh], r4u, u4s.at[0], u4r.at[0], dev_2)
 
-    def do_u_x(yy, j):
-        u_core(yy, j).wait_recv()
-        r0u[yy, j] = r0u[yy, j] + gu[yy, c, j]
-        u_x(yy, j).start()
-
-    def do_u_y(j):
-        for yy in range(2):
-            u_x(yy, j).wait_recv()
-            r1u[yy, j] = r1u[yy, j] + r0u[yy, j, :, :, x]
-        u_y(j).start()
-
-    def do_u_1():
-        for j in range(2):
-            u_y(j).wait_recv()
-            r2u[j] = r2u[j] + r1u[y, j]
-        u_1().start()
+    def do_u_1(i):
+        u_core(i).wait_recv()
+        r0u[i] = r0u[i] + gu[i, c]
+        u_1(i).start()
+
+    def do_u_x(i):
+        u_1(i).wait_recv()
+        r1u[i] = r1u[i] + r0u[i, :, zl]
+        u_x(i).start()
+
+    def do_u_y():
+        for i in range(4):
+            u_x(i).wait_recv()
+            r2u[i // 2, i % 2] = r2u[i // 2, i % 2] + r1u[i, :, x]
+        u_y().start()
 
     def do_u_2():
-        u_1().wait_recv()
-        r3u[...] = r3u[...] + r2u[:, :, zl]
+        u_y().wait_recv()
+        r3u[...] = r3u[...] + r2u[y]
         u_2().start()
 
+    vec[...] = jnp.zeros_like(vec)
+    for i in range(n_chunk):
+        for o in range(2):
+            ub[pl.ds(i, 1), pl.ds(o * chunk, chunk)] = up_bias[pl.ds(piece_of(i, o) * chunk, chunk)].reshape(1, chunk)
     acc[...] = jnp.zeros_like(acc)
     gn2[...] = jnp.zeros_like(gn2)
 
+    act = gatt
+    gh = kvt
+    cuts = ((0, 256, ((0, 0, 0, 256),)), (256, 256, ((0, 256, 0, 128), (1, 0, 128, 128))), (512, 256, ((1, 128, 0, 256),)))
+
     def ffn_step(i, carry):
-        slot = lax.rem(i, 2)
-        for copy in stream(i, slot):
+        for copy in stream(i):
             copy.wait()
-        at = pl.multiple_of(i * chunk, chunk)
-        hidden = dot_nn(n2[...], wus[slot]) + up_bias[:, pl.ds(at, chunk)]
-        active, slope = gelu_pair(hidden)
-        active = active.astype(BF)
-        gd[i] = dot_nn(ct_t[:, pl.ds(0, wide)], active).astype(BF).reshape(gd.shape[1:])
-        d_core(i).start()
-        grad_hidden = (slope * dot_nt(ct[...], wds[slot])).astype(BF)
-        gu[i // 4, (i // 2) % 2, i % 2] = (
-            dot_nn(n2t[:, pl.ds(0, wide)], grad_hidden).astype(BF).reshape(gu.shape[3:])
-        )
-
-        @pl.when((i // 2) % 2 != c)
+        for first, count, _ in cuts:
+            here = pl.ds(first, count)
+            hidden = dot_nn(n2[...], wu[:, here]) + ub[pl.ds(i, 1), here]
+            active, slope = gelu_pair(hidden)
+            act[:, here] = active.astype(BF)
+            grad_hidden = (slope * dot_nt(ct[...], wd[here, :])).astype(BF)
+            gh[pl.ds(0, wide), here] = grad_hidden
+            ub[pl.ds(i, 1), here] = jnp.sum(grad_hidden.astype(F32), axis=0, keepdims=True)
+
+        @pl.when(i >= 1)
         def _():
-            u_core(i // 4, i % 2).start()
-
-        rll[pl.ds(i, 1), :] = jnp.sum(grad_hidden.astype(F32), axis=0, keepdims=True)
-        acc[...] += dot_nn(active, wds[slot])
-        gn2[...] += dot_nt(grad_hidden, wus[slot])
-
-        @pl.when(i + 2 < n_chunk)
-        def _():
-            for copy in stream(i + 2, slot):
-                copy.start()
+            do_d_y(i - 1)
+            do_u_1(i - 1)
 
         @pl.when(i >= 2)
         def _():
-            do_d_y(i - 2)
-
-        @pl.when((i >= 2) & (((i - 2) // 2) % 2 == c))
+            do_u_x(i - 2)
+
+        @pl.when(i == 3)
         def _():
-            do_u_x((i - 2) // 4, i % 2)
+            do_d_x(0)
+
+        for first, count, _ in cuts:
+            here = pl.ds(first, count)
+            acc[:, here] += dot_nn(act[...], wd[:, here])
+            gn2[:, here] += dot_nt(gh[pl.ds(0, wide), :], wu[here, :])
+
+        @pl.when(i + 1 < n_chunk)
+        def _():
+            for copy in stream(i + 1):
+                copy.start()
+
+        for first, count, parts in cuts:
+            block = dot_nn(ct_t[:, pl.ds(0, wide)], act[:, pl.ds(first, count)]).astype(BF)
+            for o, at, start, size in parts:
+                gd[i, o, :, :, :, pl.ds(at, size)] = block[:, start : start + size].reshape(2, 2, side, size)
+        d_core(i).start()
+        for first, count, parts in cuts:
+            block = dot_nn(n2t[:, pl.ds(0, wide)], gh[pl.ds(0, wide), pl.ds(first, count)]).astype(BF)
+            for o, at, start, size in parts:
+                gu[i, o, :, :, :, :, :, pl.ds(at, size)] = block[:, start : start + size].reshape(
+                    2, 2, 2, 2, part // 2, size
+                )
+        u_core(i).start()
 
         return carry
 
     lax.fori_loop(0, n_chunk, ffn_step, 0)
 
-    vec[...] = jnp.zeros_like(vec)
     for i in range(n_chunk):
-        vec[pl.ds(8 + i // 2, 1), pl.ds((i % 2) * chunk, chunk)] = rll[pl.ds(i, 1), :]
+        for o in range(2):
+            block = piece_of(i, o)
+            vec[pl.ds(8 + block // 2, 1), pl.ds(block % 2 * chunk, chunk)] = ub[pl.ds(i, 1), pl.ds(o * chunk, chunk)]
+
 
     def second_pull(first, count):
         grad, gain_term, shift_term = norm_pull(
-            x2[pl.ds(first, count), :], ffn_gain[...], gn2[pl.ds(first, count), :]
+            x2[pl.ds(first, count), :], ffn_gain, gn2[pl.ds(first, count), :]
         )
         upstream = ct[pl.ds(first, count), :].astype(F32)
         total = upstream + grad
-        acc[pl.ds(first, count), :] += x2[pl.ds(first, count), :] + down_bias[...]
+        acc[pl.ds(first, count), :] += x2[pl.ds(first, count), :] + down_bias
         x2[pl.ds(first, count), :] = total
         n2[pl.ds(first, count), :] = total.astype(BF)
         vec[pl.ds(4, 1), :] += gain_term
@@ -869,14 +904,6 @@
     for r in range(0, tok, 128):
         second_pull(r, 128)
     second_pull(tok, slots)
-    do_d_y(n_chunk - 2)
-    do_d_y(n_chunk - 1)
-
-    @pl.when(c == 1)
-    def _():
-        do_u_x(1, 0)
-        do_u_x(1, 1)
-
     gatt[...] = dot_nt(n2[...], wo[...]).astype(BF)
 
     slot_grad = gatt[pl.ds(tok, slots), :].astype(F32)
@@ -903,12 +930,12 @@
         copy.start()
         sends2.append(copy)
     rcv2[pl.ds(my_slots, slots), :] = msg1[pl.ds(0, slots), :]
+    do_d_y(3)
+    do_u_1(3)
+    do_u_x(2)
 
     n2t[:, pl.ds(0, tok)] = jnp.transpose(nrm[pl.ds(0, tok), :])
-    mine = nrm[pl.ds(pl.multiple_of(tok + my_slots, slots), slots), :].astype(F32)
-    n2t[:, pl.ds(tok, tail)] = jnp.transpose(
-        jnp.concatenate([mine, jnp.zeros((tail - slots, width), F32)], axis=0)
-    ).astype(BF)
+    n2t[:, pl.ds(tok, glob)] = jnp.transpose(nrm[pl.ds(tok, glob), :])
 
     outs = nrm
     outs[pl.ds(0, wide), :] = acc[...].astype(BF)
@@ -918,6 +945,119 @@
         outs.at[pl.ds(tok, slots)], o_gout.at[pl.ds(my_slots, slots)], osem.at[1]
     )
     own_out.start()
+
+    scale_c = jnp.transpose(
+        jnp.concatenate([rl_t[...], jnp.zeros((128 - rl_t.shape[0], tok), F32)], axis=0)
+    )
+    scale_a, scale_b = two_parts(scale_c)
+    for r in range(0, tok, 128):
+        wider = dot_nn(scale_a[r : r + 128], spread_heads) + dot_nn(scale_b[r : r + 128], spread_heads)
+        scaled = (gatt[pl.ds(r, 128), :].astype(F32) * wider).astype(BF)
+        gatt[pl.ds(r, 128), :] = scaled
+        qaug[pl.ds(r, 128), :] = inner_aug(scaled, att[pl.ds(r, 128), :].astype(F32))
+    kvt[:, pl.ds(0, rows)] = jnp.transpose(proj[:, pl.ds(width, width)])
+
+    def chunk_at(p):
+        return gu.at[p // 2, lax.rem(p, 2)]
+
+    def put_chunk(p, value):
+        gu[p // 2, lax.rem(p, 2)] = value.astype(BF).reshape(gu.shape[2:])
+        q_core(p).start()
+
+    def q_core(p):
+        return remote(chunk_at(p).at[:, 1 - c], r0q.at[p], q0s.at[p], q0r.at[p], dev_c)
+
+    def x_first(p):
+        return p % 2 == 1
+
+    def q_a(p):
+        src, dev = (r0q.at[p, :, 1 - x], dev_x) if x_first(p) else (r0q.at[p, :, :, 1 - y], dev_y)
+        return remote(src, r1q.at[p], q1s.at[p], q1r.at[p], dev)
+
+    def q_b(p):
+        src, dev = (r1q.at[p, :, 1 - y], dev_y) if x_first(p) else (r1q.at[p, :, 1 - x], dev_x)
+        return remote(src, r2q.at[p], q2s.at[p], q2r.at[p], dev)
+
+    def q_1(p):
+        return remote(r2q.at[p], r3q.at[p], q3s.at[p], q3r.at[p], dev_1)
+
+    def q_2(p):
+        return remote(r2q.at[p, 1 - zh], r4q.at[p], q4s.at[p], q4r.at[p], dev_2)
+
+    def take_chunk(p):
+        q_core(p).wait_recv()
+        r0q[p] = r0q[p] + gu[p // 2, p % 2, :, c]
+
+    def do_q_a(*which):
+        for p in which:
+            take_chunk(p)
+            q_a(p).start()
+
+    def do_q_b(*which):
+        for p in which:
+            q_a(p).wait_recv()
+            r1q[p] = r1q[p] + (r0q[p, :, x] if x_first(p) else r0q[p, :, :, y])
+            q_b(p).start()
+
+    def do_q_1(*which):
+        for p in which:
+            q_b(p).wait_recv()
+            r2q[p] = r2q[p] + r1q[p, :, y if x_first(p) else x]
+
+            @pl.when(zl != c)
+            def _(p=p):
+                q_1(p).start()
+
+    def do_q_2(*which):
+        @pl.when(zl == c)
+        def _():
+            for p in which:
+                q_1(p).wait_recv()
+                r2q[p] = r2q[p] + r3q[p]
+                q_2(p).start()
+
+    def q_plane(n):
+        src = (r0q.at[5, :, 1 - x, y], r0q.at[5, :, x, 1 - y], r0q.at[5, :, 1 - x, 1 - y])[n]
+        dst = (r1q.at[5, :, 0], r1q.at[5, :, 1], r2q.at[5])[n]
+        return remote(src, dst, qps.at[n], qpr.at[n], (dev_x, dev_y, dev_xy)[n])
+
+    def q_line(n):
+        src = (r0q.at[5, 1 - zh, x, y], r0q.at[5, zh, x, y], r0q.at[5, 1 - zh, x, y])[n]
+        dst = (r3q.at[5, 0], r3q.at[5, 1], r4q.at[5])[n]
+        return remote(src, dst, qls.at[n], qlr.at[n], (dev_2, dev_1, (flip(6), b))[n])
+
+    def do_q_plane():
+        take_chunk(5)
+        for n in range(3):
+            q_plane(n).start()
+
+    def do_q_line():
+        for n in range(3):
+            q_plane(n).wait_recv()
+        total = r0q[5, :, x, y].astype(F32) + r1q[5, :, 0].astype(F32) + r1q[5, :, 1].astype(F32) + r2q[5].astype(F32)
+        r0q[5, :, x, y] = total.astype(BF)
+
+        @pl.when(zl == c)
+        def _():
+            q_line(0).start()
+
+        @pl.when(zl != c)
+        def _():
+            q_line(1).start()
+            q_line(2).start()
+
+    def q_chunk(p):
+        right = jnp.concatenate(
+            [proj[:, pl.ds(pl.multiple_of(w * width + p * 128, 128), 128)] for w in range(3)], axis=1
+        )
+        put_chunk(p, dot_nn(n2t[...], right))
+
+    for i in range(4):
+        u_core(i).wait_send()
+    for h in range(2):
+        put_chunk(pairs + h, dot_nn(att_t[:, pl.ds(0, wide)], n2[:, pl.ds(h * 384, 384)]))
+    for copy in sends2:
+        copy.wait()
     sends_o = []
     for k in peers:
         copy = remote(
@@ -925,23 +1065,6 @@
         )
         copy.start()
         sends_o.append(copy)
-
-    scale_c = jnp.transpose(
-        jnp.concatenate([rl_t[...], jnp.zeros((128 - rl_t.shape[0], tok), F32)], axis=0)
-    )
-    scale_a, scale_b = two_parts(scale_c)
-    for r in range(0, tok, 128):
-        wider = dot_nn(scale_a[r : r + 128], spread_heads) + dot_nn(scale_b[r : r + 128], spread_heads)
-        scaled = (gatt[pl.ds(r, 128), :].astype(F32) * wider).astype(BF)
-        gatt[pl.ds(r, 128), :] = scaled
-        qaug[pl.ds(r, 128), :] = inner_aug(scaled, att[pl.ds(r, 128), :].astype(F32))
-    kvt[...] = jnp.transpose(proj[:, pl.ds(width, width)])
-    for i in range(4):
-        do_d_x(i)
-    do_u_y(0)
-    do_u_y(1)
-    for copy in sends2:
-        copy.wait()
 
     minus = jnp.where(lanes_of((rows, 128)) < 32, -1.0, 0.0).astype(BF)
 
@@ -970,140 +1093,78 @@
             probs[p, :, pl.ds(first, count)] = (here * grad_w).astype(BF)
         grad_k = dot_nn(probs[p], qs)
         factor = HEAD_DIM ** (-0.5)
-        low = dot_nn(kvt[pl.ds(at, HEAD_DIM), :], probs[p, :, pl.ds(0, tok)])
+        low = dot_nn(kvt[pl.ds(at, HEAD_DIM), pl.ds(0, rows)], probs[p, :, pl.ds(0, tok)])
         upper = dot_nn(
-            kvt[pl.ds(pl.multiple_of(at + HEAD_DIM, HEAD_DIM), HEAD_DIM), :], probs[p, :, pl.ds(tok, tok)]
+            kvt[pl.ds(pl.multiple_of(at + HEAD_DIM, HEAD_DIM), HEAD_DIM), pl.ds(0, rows)], probs[p, :, pl.ds(tok, tok)]
         )
         grad_q = jnp.concatenate([low, upper], axis=0) * factor
-        own = dot_nn(kvt[pl.ds(at, 128), :], probs[p, :, pl.ds(2 * tok, 2 * glob)])
+        own = dot_nn(kvt[pl.ds(at, 128), pl.ds(0, rows)], probs[p, :, pl.ds(2 * tok, 2 * glob)])
         own = jnp.where(first_head, own[:, :glob], own[:, glob:]) * factor
+        proj[pl.ds(tok, glob), pl.ds(at, 128)] = jnp.transpose(own).astype(BF)
         proj[pl.ds(0, tok), pl.ds(at, 128)] = jnp.transpose(grad_q).astype(BF)
-        proj[pl.ds(tok, glob), pl.ds(at, 128)] = jnp.transpose(own).astype(BF)
         proj[:, pl.ds(width + at, 128)] = grad_k.astype(BF)
         proj[:, pl.ds(2 * width + at, 128)] = grad_v.astype(BF)
 
-        @pl.when(p == 2)
-        def _():
-            do_d_1(0)
-            do_d_1(1)
-
-        @pl.when(p == 3)
-        def _():
-            do_u_1()
-
-        @pl.when(p == 4)
-        def _():
-            do_d_2()
-
-        @pl.when(p == 5)
-        def _():
-            do_u_2()
+        q_chunk(p)
+        for at_step, act in (
+            (0, lambda: (do_d_x(1), do_u_x(3), do_q_a(6, 7))),
+            (1, lambda: (do_d_1(0), do_d_1(1), do_u_y(), do_q_a(0))),
+            (2, lambda: (do_d_2(), do_q_a(1))),
+            (3, lambda: (do_u_2(), do_q_a(2), do_q_b(6, 7))),
+            (4, lambda: (do_q_a(3), do_q_b(0))),
+            (5, lambda: (do_q_a(4), do_q_b(1), do_q_1(6, 7))),
+        ):
+
+            @pl.when(p == at_step)
+            def _(act=act):
+                act()
 
         return carry
 
     lax.fori_loop(0, pairs, attention_back, 0)
-
-    sends3 = []
-    for k in peers:
-        other = flip(k)
-        at = pl.multiple_of(tok + other * slots, slots)
-        copy = remote(proj.at[pl.ds(at, slots)], rcv3.at[k - 1], m3s.at[k], m3r.at[k], (other, b))
-        copy.start()
-        sends3.append(copy)
-
-    total3 = proj[pl.ds(pl.multiple_of(tok + my_slots, slots), slots), :].astype(F32)
-    for copy in sends3:
-        copy.wait()
-    for k in peers:
-        total3 = total3 + rcv3[k - 1].astype(F32)
-    proj[pl.ds(tok, slots), :] = total3.astype(BF)
-
-    for yy in range(2):
-        for j in range(2):
-            u_core(yy, j).wait_send()
-
-    def q_block(yy, cc):
-        bb = 2 * yy + cc
-        odd_b = cc == 1
-        at = pl.multiple_of(bb * 576 - 64 * cc, 128)
-        window = proj[pl.ds(0, wide), pl.ds(at, 640)].astype(F32)
-        window = jnp.where(odd_b, pltpu.roll(window, 576, 1), window).astype(BF)
-        at = pl.multiple_of(bb * 192 - 64 * cc, 128)
-        branch = n2[:, pl.ds(at, 256)].astype(F32)
-        branch = jnp.where(odd_b, branch, pltpu.roll(branch, 64, 1)).astype(BF)
-        first = dot_nn(n2t[:, pl.ds(0, wide)], window[:, :384])
-        second = dot_nn(n2t[:, pl.ds(0, wide)], window[:, 384:])
-        third = dot_nn(att_t[:, pl.ds(0, wide)], branch)
-        middle = jnp.where(lanes_of((width, 128)) < 64, second[:, 128:], third[:, :128])
-        return first, jnp.concatenate([second[:, :128], middle, third[:, 128:]], axis=1)
-
-    def q_core(yy, j):
-        return remote(gu.at[yy, 1 - c, j], r0q.at[yy, j], q0s.at[yy * 2 + j], q0r.at[yy * 2 + j], dev_c)
-
-    def q_first(yy, carry):
-        for j, block in enumerate(q_block(yy, 1 - c)):
-            gu[yy, 1 - c, j] = block.astype(BF).reshape(gu.shape[3:])
-            q_core(yy, j).start()
-        return carry
-
-    lax.fori_loop(0, 2, q_first, 0)
-
-    gn2[...] = dot_nt(proj[pl.ds(0, wide), :], wq[...])
-
-    def q_x0(yy):
-        return remote(r0q.at[yy, 0, :, :, 1 - x], r1qx.at[yy], q1s.at[yy], q1r.at[yy], dev_x)
-
-    def q_y0():
-        return remote(r1qx.at[1 - y], r2q.at[0], q2s.at[0], q2r.at[0], dev_y)
-
-    def q_y1():
-        return remote(r0q.at[1 - y, 1], r1qy, q1s.at[2], q1r.at[2], dev_y)
-
-    def q_x1():
-        return remote(r1qy.at[:, :, 1 - x], r2q.at[1], q2s.at[1], q2r.at[1], dev_x)
-
-    def q_1():
-        return remote(r2q.at[:, :, 1 - zl], r3q, q3s.at[0], q3r.at[0], dev_1)
-
-    def q_2():
-        return remote(r3q.at[:, 1 - zh], r4q, q4s.at[0], q4r.at[0], dev_2)
-
-    def q_second(yy, carry):
-        first, second = q_block(yy, c)
-        q_core(yy, 0).wait_recv()
-        r0q[yy, 0] = (r0q[yy, 0].astype(F32) + first.reshape(gu.shape[3:])).astype(BF)
-        q_x0(yy).start()
-        q_core(yy, 1).wait_recv()
-        r0q[yy, 1] = (r0q[yy, 1].astype(F32) + second.reshape(gu.shape[3:])).astype(BF)
-        return carry
-
-    lax.fori_loop(0, 2, q_second, 0)
-    q_y1().start()
 
     def first_pull(first):
         grad, gain_term, shift_term = norm_pull(
-            sec[pl.ds(first, 128), :].astype(F32), attn_gain[...], gn2[pl.ds(first, 128), :]
+            sec[pl.ds(first, 128), :].astype(F32), attn_gain, gn2[pl.ds(first, 128), :]
         )
         n2[pl.ds(first, 128), :] = (grad + x2[pl.ds(first, 128), :]).astype(BF)
         vec[pl.ds(0, 1), :] += gain_term
         vec[pl.ds(1, 1), :] += shift_term
 
+    gnm = wu
+    gnm[pl.ds(0, glob), :] = dot_nt(proj[pl.ds(tok, glob), :], wq[...]).astype(BF)
+    sends3 = []
+    for k in peers:
+        other = flip(k)
+        at = pl.multiple_of(other * slots, slots)
+        copy = remote(gnm.at[pl.ds(at, slots)], rcv3.at[k - 1], m3s.at[k], m3r.at[k], (other, b))
+        copy.start()
+        sends3.append(copy)
+    do_q_plane()
+    gn2[pl.ds(half, half), :] = dot_nt(proj[pl.ds(half, half), :], wq[...])
     for r in range(half, tok, 128):
         first_pull(r)
-    back = remote(
-        n2.at[pl.ds(half, half)], o_tgrad.at[pl.ds(0, half)], hs2.at[0], hr2.at[0],
-        (lax.rem(s + 1, n_seq), b),
-    )
-    back.start()
+    do_q_b(2, 3)
+    do_q_1(0, 1)
+    do_q_2(6, 7)
+
+    gn2[pl.ds(0, half), :] = dot_nt(proj[pl.ds(0, half), :], wq[...])
     for r in range(0, half, 128):
         first_pull(r)
     keep = pltpu.make_async_copy(n2.at[pl.ds(0, half)], o_tgrad.at[pl.ds(half, half)], osem.at[2])
     keep.start()
-
+    do_q_b(4)
+    do_q_line()
+
+    grad_slots = gnm[pl.ds(my_slots, slots), :].astype(F32)
+    for copy in sends3:
+        copy.wait()
+    for k in peers:
+        grad_slots = grad_slots + rcv3[k - 1].astype(F32)
     grad, gain_term, shift_term = norm_pull(
         sec[pl.ds(pl.multiple_of(tok + my_slots, slots), slots), :].astype(F32),
-        glob_gain[...],
-        gn2[pl.ds(tok, slots), :],
+        glob_gain,
+        grad_slots,
     )
     vec[pl.ds(2, 1), :] += gain_term
     vec[pl.ds(3, 1), :] += shift_term
@@ -1112,6 +1173,21 @@
         n2.at[pl.ds(tok, slots)], o_ggrad.at[pl.ds(my_slots, slots)], osem.at[3]
     )
     own_grad.start()
+
+    share = vec.shape[1] // n_seq
+    for j in range(n_seq):
+        rolled = vec[pl.ds(0, 8), :]
+        if j:
+            rolled = pltpu.roll(rolled, vec.shape[1] - share * j, 1)
+        vmsg[j, pl.ds(0, 8), :] = rolled[:, :128]
+        for m in range(chunk // 128):
+            vmsg[j, pl.ds(8 + m, 1), :] = vec[pl.ds(8 + j // 2, 1), pl.ds((j % 2) * chunk + m * 128, 128)]
+    sends_v = []
+    for k in peers:
+        copy = remote(vmsg.at[flip(k)], vrcv.at[k - 1], vs.at[k], vr.at[k], (flip(k), b))
+        copy.start()
+        sends_v.append(copy)
+
     sends_g = []
     for k in peers:
         copy = remote(
@@ -1120,76 +1196,129 @@
         )
         copy.start()
         sends_g.append(copy)
-
-    def vec_step(k, dev):
-        return remote(vec, rvec.at[k], vs.at[k], vr.at[k], dev)
-
-    def vec_add(k, dev):
-        vec_step(k, dev).wait()
-        vec[...] += rvec[k]
-
-    vec_step(0, dev_c).start()
+    do_q_1(2, 3)
+    do_q_2(0, 1)
+    back = remote(
+        n2.at[pl.ds(half, half)], o_tgrad.at[pl.ds(0, half)], hs2.at[0], hr2.at[0],
+        (lax.rem(s + 1, n_seq), b),
+    )
+    back.start()
+
     d_2().wait_recv()
-    o_down[...] = jnp.transpose(r4d[...].astype(F32) + r3d[zh].astype(F32))
+    o_down[...] = r4d[...].astype(F32) + r3d[zh].astype(F32)
     u_2().wait_recv()
     last = r4u[...].astype(F32) + r3u[:, zh].astype(F32)
-    o_up[:, pl.ds(0, 384)] = last[0]
-    o_up[:, pl.ds(384, 384)] = last[1]
-    vec_add(0, dev_c)
-    vec_step(1, dev_y).start()
+    o_up[:, pl.ds(0, 384)] = last[0].reshape(96, 384)
+    o_up[:, pl.ds(384, 384)] = last[1].reshape(96, 384)
+
+    do_q_1(4)
+    do_q_2(2, 3)
+
+    for copy in sends_v:
+        copy.wait()
+    vsum[0] = vmsg[s]
+    for k in peers:
+        vsum[0] = vsum[0] + vrcv[k - 1]
+    batch_peers = (dev_c, dev_y, dev_cy)
+    sends_b = []
+    for n, dev in enumerate(batch_peers):
+        copy = remote(vsum.at[0], vsum.at[1 + n], vbs.at[n], vbr.at[n], dev)
+        copy.start()
+        sends_b.append(copy)
+
+    do_q_2(4)
+
+    def final(n, slot):
+        return remote(fmsg.at[n], frcv.at[slot], fs.at[n], fr.at[n], (s, flip_b(n)))
+
+    def flip_b(n):
+        return (b, dev_c[1], dev_y[1], dev_cy[1])[n]
+
+    @pl.when(zl == c)
+    def _():
+        for p in (6, 7, 0, 1, 2, 3, 4):
+            q_2(p).wait_recv()
+            r4q[p] = r4q[p] + r2q[p, zh]
+        for n in range(3):
+            q_line(n).wait_recv()
+        r4q[5] = (
+            r0q[5, zh, x, y].astype(F32) + r3q[5, 0].astype(F32) + r3q[5, 1].astype(F32) + r4q[5].astype(F32)
+        ).astype(BF)
+
+        def columns_of(bb):
+            first = (bb * 576 - 64 * lax.rem(bb, 2)) // 128
+            tiles = []
+            for m in range(5):
+                tile = first + m
+                tiles.append(r4q[lax.rem(tile, 6), :, pl.ds(pl.multiple_of(tile // 6 * 128, 128), 128)])
+            first = (bb * 192 - 64 * lax.rem(bb, 2)) // 128
+            for m in range(2):
+                tile = first + m
+                tiles.append(r4q[pairs + tile // 3, :, pl.ds(pl.multiple_of(lax.rem(tile, 3) * 128, 128), 128)])
+            return jnp.concatenate(tiles, axis=1)
+
+        for n in (3, 2, 1):
+            fmsg[n] = columns_of(flip_b(n))
+            final(n, y).start()
+        frcv[y] = columns_of(b)
+
+    for copy in sends_b:
+        copy.wait()
+    shared = vsum[0] + vsum[1] + (vsum[2] + vsum[3])
+    o_vec[...] = shared[0:8, :share]
+    for m in range(chunk // 128):
+        o_ub[:, pl.ds(m * 128, 128)] = shared[8 + m : 9 + m, :]
+
+    @pl.when(zl == c)
+    def _():
+        final(2, 1 - y).wait_recv()
+
+    @pl.when(zl != c)
+    def _():
+        final(1, y).wait_recv()
+        final(3, 1 - y).wait_recv()
+
     for yy in range(2):
-        q_x0(yy).wait_recv()
-        r1qx[yy] = r1qx[yy] + r0q[yy, 0, :, :, x]
-    q_y0().start()
-    vec_add(1, dev_y)
-    vec_step(2, dev_x).start()
-    q_y1().wait_recv()
-    r1qy[...] = r1qy[...] + r0q[y, 1]
-    q_x1().start()
-    vec_add(2, dev_x)
-    vec_step(3, dev_1).start()
-    q_y0().wait_recv()
-    r2q[0] = r2q[0] + r1qx[y]
-    q_x1().wait_recv()
-    r2q[1] = r2q[1] + r1qy[:, :, x]
-    q_1().start()
-    vec_add(3, dev_1)
-    vec_step(4, dev_2).start()
-    q_1().wait_recv()
-    r3q[...] = r3q[...] + r2q[:, :, zl]
-    q_2().start()
-    vec_add(4, dev_2)
-    share = vec.shape[1] // n_seq
-    turned = pltpu.roll(vec[pl.ds(0, 8), :], lax.rem(vec.shape[1] - share * s, vec.shape[1]), 1)
-    o_vec[...] = turned[:, :share]
-    o_ub[...] = vec[pl.ds(8 + s // 2, 1), pl.ds(pl.multiple_of((s % 2) * chunk, chunk), chunk)]
-    q_2().wait_recv()
-    last = r4q[...].astype(F32) + r3q[:, zh].astype(F32)
-    o_qkv[:, pl.ds(0, 384)] = last[0]
-    o_qkv[:, pl.ds(384, 192)] = last[1][:, :192]
-    o_wout[...] = last[1][:, 192:]
-
-    for i in range(8):
+        block = frcv[yy].astype(F32)
+        main = block[:, :640]
+        o_qkv[pl.ds(yy * 48, 48), :] = jnp.where(c == 1, pltpu.roll(main, 576, 1), main)[:, :576]
+        main = block[:, 640:]
+        o_wout[pl.ds(yy * 48, 48), :] = jnp.where(c == 1, pltpu.roll(main, 192, 1), main)[:, :192]
+
+    for i in range(4):
         d_core(i).wait_send()
         d_y(i).wait_send()
-    for i in range(4):
-        d_x(i).wait_send()
-    for i in range(2):
-        d_1(i).wait_send()
+        u_1(i).wait_send()
+        u_x(i).wait_send()
+    for h in range(2):
+        d_x(h).wait_send()
+        d_1(h).wait_send()
     d_2().wait_send()
-    for yy in range(2):
-        for j in range(2):
-            u_x(yy, j).wait_send()
-            q_core(yy, j).wait_send()
-        u_y(yy).wait_send()
-        q_x0(yy).wait_send()
-    u_1().wait_send()
+    u_y().wait_send()
     u_2().wait_send()
-    q_y0().wait_send()
-    q_y1().wait_send()
-    q_x1().wait_send()
-    q_1().wait_send()
-    q_2().wait_send()
+    for p in range(8):
+        q_core(p).wait_send()
+        if p != 5:
+            q_a(p).wait_send()
+            q_b(p).wait_send()
+    for n in range(3):
+        q_plane(n).wait_send()
+
+    @pl.when(zl == c)
+    def _():
+        q_line(0).wait_send()
+        for n in (1, 2, 3):
+            final(n, y).wait_send()
+        for p in (6, 7, 0, 1, 2, 3, 4):
+            q_2(p).wait_send()
+
+    @pl.when(zl != c)
+    def _():
+        for n in (1, 2):
+            q_line(n).wait_send()
+        for p in (6, 7, 0, 1, 2, 3, 4):
+            q_1(p).wait_send()
+
     back.wait()
     keep.wait()
     own_grad.wait()
@@ -1208,6 +1337,15 @@
         and w_qkv.shape == (HEADS * HEAD_DIM, 3 * HEADS * HEAD_DIM)
         and w_up.shape == (HEADS * HEAD_DIM, 3072)
     )
+
+
+def finish_kernel(*refs):
+    ins, outs = refs[:10], refs[10:]
+    for i in range(8):
+        outs[i][...] = ins[i][...]
+    for i in range(7):
+        outs[8 + i][...] = ins[8][i, :]
+    outs[15][...] = ins[9][0, :]
 
 
 def fused(
@@ -1222,6 +1360,7 @@
     wide = tok + slots
     chunk, part, side = hidden // n_seq, width // n_seq, width // n_batch
     pairs = HEADS // 2
+    eighth = (2, 2, 2)
     dma = pltpu.SemaphoreType.DMA
 
     def any_space():
@@ -1237,31 +1376,27 @@
         return pltpu.VMEM(shape, F32)
 
     scratch = [
-        low(rows, width), low(rows, width), low(rows, 3 * width), low(width, rows),
+        low(rows, width), low(rows, width), low(rows, 3 * width), low(width, width),
         low(pairs, rows, 2 * tok + 2 * glob), low(width, tok + 128), low(wide, width), full(wide, width),
         low(wide, width), low(width, tok + 128), low(wide, width), low(width, tok + 128),
         full(wide, width), full(wide, width), low(wide, width), low(rows, 128), low(rows, 128),
-        low(width, 3 * width), low(width, width), low(2, width, chunk), low(2, chunk, width),
-        full(128, glob), full(16, tok), full(width, glob), low(glob, width + 128),
-        low(n_seq, slots, width + 128), full(glob, width), low(glob, width + 128),
-        low(n_seq - 1, slots, 3 * width),
-        full(16, width), full(5, 16, width), full(8, chunk),
-        low(8, 2, 2, side, chunk), low(8, 2, side, chunk), low(8, side, chunk), low(4, side, chunk),
+        low(width, 3 * width), low(width, width), low(width, width), low(width, width),
+        full(128, glob), full(16, tok), full(glob, width), low(glob, width + 128),
+        low(n_seq, slots, width + 128), low(glob, width + 128),
+        low(n_seq - 1, slots, width),
+        full(16, width), full(n_seq, 16, 128), full(n_seq - 1, 16, 128), full(4, 16, 128), full(4, width),
+        low(4, 2, 2, 2, side, chunk), low(4, 2, 2, side, chunk), low(2, 2, 2, side, chunk), low(2, 2, side, chunk),
         low(2, side, chunk), low(side, chunk),
-        low(2, 2, 2, 2, 2, 2, part, chunk), low(2, 2, 2, 2, 2, part, chunk), low(2, 2, 2, 2, part, chunk),
-        low(2, 2, 2, part, chunk), low(2, 2, part, chunk), low(2, part, chunk),
-        low(2, 2, 2, 2, 2, part, chunk), low(2, 2, 2, part, chunk), low(2, 2, 2, part, chunk),
-        low(2, 2, 2, part, chunk), low(2, 2, part, chunk), low(2, part, chunk),
+        low(4, 2, *eighth, 2, part // 2, chunk), low(4, *eighth, 2, part // 2, chunk), low(4, 2, 2, 2, part // 2, chunk),
+        low(2, 2, 2, 2, part // 2, chunk), low(2, 2, 2, part // 2, chunk), low(2, 2, part // 2, chunk),
+        low(8, 2, 2, 2, part // 2, chunk), low(8, 2, 2, part // 2, chunk), low(8, 2, part // 2, chunk),
+        low(8, 2, part // 2, chunk), low(8, part // 2, chunk),
+        low(4, part // 2, 896), low(2, part // 2, 896),
         dma((8,)), dma((2, 2)), dma((1,)), dma((1,)),
-        *[dma((8,)) for _ in range(10)], dma((5,)), dma((5,)),
-        dma((8,)), dma((8,)), dma((8,)), dma((8,)), dma((4,)), dma((4,)), dma((2,)), dma((2,)), dma((1,)), dma((1,)),
-        dma((4,)), dma((4,)), dma((4,)), dma((4,)), dma((2,)), dma((2,)), dma((1,)), dma((1,)), dma((1,)), dma((1,)),
-        dma((4,)), dma((4,)), dma((3,)), dma((3,)), dma((2,)), dma((2,)), dma((1,)), dma((1,)), dma((1,)), dma((1,)),
-        dma((1,)), dma((1,)), dma((4,)),
+        *[dma((8,)) for _ in range(10)], dma((9,)), dma((9,)),
+        *[dma((4,)) for _ in range(10)], *[dma((4,)) for _ in range(10)], *[dma((8,)) for _ in range(10)],
+        *[dma((3,)) for _ in range(6)], dma((4,)), dma((4,)), dma((1,)), dma((1,)), dma((4,)),
     ]
-
-    def row(vector):
-        return vector.reshape(1, -1)
 
     results = pl.pallas_call(
         layer_kernel,
@@ -1273,7 +1408,7 @@
             jax.ShapeDtypeStruct((part, 3 * side), F32),
             jax.ShapeDtypeStruct((part, side), F32),
             jax.ShapeDtypeStruct((part, 2 * chunk), F32),
-            jax.ShapeDtypeStruct((chunk, side), F32),
+            jax.ShapeDtypeStruct((side, chunk), F32),
             jax.ShapeDtypeStruct((8, part), F32),
             jax.ShapeDtypeStruct((1, chunk), F32),
         ],
@@ -1286,14 +1421,24 @@
         ),
         name="layer",
     )(
-        tokens[0], global_states[0], token_seg, global_seg, row(attn_gain), row(attn_shift), row(glob_gain),
-        row(glob_shift), w_qkv, w_out, row(ffn_gain), row(ffn_shift), w_up, row(up_bias), w_down, row(down_bias),
+        tokens[0], global_states[0], token_seg, global_seg, attn_gain, attn_shift, glob_gain,
+        glob_shift, w_qkv, w_out, ffn_gain, ffn_shift, w_up, up_bias, w_down, down_bias,
         out_cotangent[0], global_cotangent[0],
     )
-    out, gout, tgrad, ggrad, g_qkv, g_out, g_up, g_down, g_vec, g_ub = results
+    *large, vectors, ub = results
+    results = pl.pallas_call(
+        finish_kernel,
+        out_shape=[jax.ShapeDtypeStruct(one.shape, one.dtype) for one in large]
+        + [jax.ShapeDtypeStruct((part,), F32)] * 7
+        + [jax.ShapeDtypeStruct((chunk,), F32)],
+        in_specs=[vmem()] * 10,
+        out_specs=[vmem()] * 16,
+        name="results",
+    )(*large, vectors, ub)
+    out, gout, tgrad, ggrad, g_qkv, g_out, g_up, g_down, *g_vec, g_ub = results
     return (
         out[None], gout[None], tgrad[None], ggrad[None], g_vec[0], g_vec[1], g_vec[2], g_vec[3], g_qkv, g_out,
-        g_vec[4], g_vec[5], g_up, g_ub[0], g_down, g_vec[6],
+        g_vec[4], g_vec[5], g_up, g_ub, g_down.T, g_vec[6],
     )
 
 

time: 212 us -> 145 us (0.68)
  Pallas kernels: 187 us -> 144 us
  local copies, waits for them, and re-layouts: 21.6 us -> 0 us
    pallas_call x1, Pallas kernels: 187 us -> 141 us  [fused(): pl.pallas_call(layer_kernel, out_shape=[jax.ShapeDtypeStruct((tok, width)...]
    unnamed x14 -> x0, local copies, waits for them, and re-layouts: 11.3 us -> none
    reshape x7 -> x0, local copies, waits for them, and re-layouts: 8.87 us -> none  [row(): return vector.reshape(1, -1)]
    pallas_call x0 -> x1, Pallas kernels: none -> 3.47 us  [fused(): pl.pallas_call(finish_kernel, out_shape=[jax.ShapeDtypeStruct(one.shape,...]
where the time goes in v3:
time: 145 us
  Pallas kernels  144 us (99%)
    pallas_call x1, Pallas kernels, fused(): pl.pallas_call(layer_kernel, out_shape=[jax.ShapeDtypeStruct((tok, width)...  141 us
    pallas_call x1, Pallas kernels, fused(): pl.pallas_call(finish_kernel, out_shape=[jax.ShapeDtypeStruct(one.shape,...  3.47 us

profile of v3, /device:TPU:2, one launch (start us, length us, event | category | flops | bytes accessed | tf_op | source)
XLA Modules:
  0.0 144.8 jit_solution(7575135978360210193)
XLA Ops:
  0.7 140.5 %layer.1 = (bf16[512,768]{1,0:T(8,128)(2,1)}, bf16[128,768]{1,0:T(8,128)(2,1)}, bf16[512,768]{1,0:T(8,128)(2,1)}, bf16[128,768]{1,0:T(8,128)(2,1)}, f32[96,576]{...) custom-call(bf16[512,768]{1,0:T(8,128)(2,1)} %bitcast.9, ...), custom_call_target="tpu_custom_call" | custom-call | tf_op jit(solution)/shard_map/layer/pallas_call | solution.py:1401
  141.2 3.5 %results.1 = (bf16[512,768]{1,0:T(8,128)(2,1)}, bf16[128,768]{1,0:T(8,128)(2,1)}, bf16[512,768]{1,0:T(8,128)(2,1)}, bf16[128,768]{1,0:T(8,128)(2,1)}, f32[96,576...) custom-call(bf16[512,768]{1,0:T(8,128)(2,1)} %get-tuple-element.42.r, ...), custom_call_target="tpu_custom_call" | custom-call | tf_op jit(solution)/shard_map/results/pallas_call | solution.py:1429

commit v4 on v3

--- a/solution.py
+++ b/solution.py
@@ -498,15 +498,15 @@
     tokens, gstates, tseg, gseg, attn_gain, attn_shift, glob_gain, glob_shift, w_qkv, w_out,
     ffn_gain, ffn_shift, w_up, up_bias, w_down, down_bias, cotan, gcotan,
     o_out, o_gout, o_tgrad, o_ggrad, o_qkv, o_wout, o_up, o_down, o_vec, o_ub,
-    sec, nrm, proj, kvt, probs, att_t, att, x2, n2, n2t, ct, ct_t, acc, gn2, gatt, qaug, kaug,
+    sec, nrm, proj, kvt, probs, att_t, att, x2, n2, n2t, ct, ct_t, acc_full, gn2_full, gatt, qaug, kaug,
     wq, wo, wu, wd,
-    lse_t, rl_t, cx, msg1, rcv1, rcv2, rcv3, vec, vmsg, vrcv, vsum, ub,
-    gd, r0d, r1d, r2d, r3d, r4d, gu, r0u, r1u, r2u, r3u, r4u, r0q, r1q, r2q, r3q, r4q, fmsg, frcv,
+    lse_t, rl_t, cx, msg1, rcv1, rcv2, rcv3, rcv3b, gsum, gall, vec, vmsg, vrcv, vsum, ub,
+    gd, r0d, r1d, r2d, r3d, r4d, gu, r0u, r1u, r2u, r3u, r4u, r0q, r1q, r2q, r3q, r4q, fmsg, frcv, hid_a, hid_b,
     loc, wsem, hs, hr, m1s, m1r, m2s, m2r, m3s, m3r, gos, gor, ggs_s, ggs_r, vs, vr,
     d0s, d0r, d1s, d1r, d2s, d2r, d3s, d3r, d4s, d4r,
     u0s, u0r, u1s, u1r, u2s, u2r, u3s, u3r, u4s, u4r,
     q0s, q0r, q1s, q1r, q2s, q2r, q3s, q3r, q4s, q4r,
-    qps, qpr, qls, qlr, vbs, vbr, fs, fr, hs2, hr2, osem,
+    qps, qpr, qls, qlr, vbs, vbr, fs, fr, hs2, hr2, osem, gsem,
 ):
     tok, width = tokens.shape
     glob = gstates.shape[0]
@@ -545,6 +545,8 @@
         )
 
     peers = tuple(range(1, n_seq))
+    acc, gn2 = acc_full.at[pl.ds(0, wide)], gn2_full.at[pl.ds(0, wide)]
+    score = (acc_full, gn2_full)
 
     def as_row(vector):
         return vector[...].reshape(1, vector.shape[0])
@@ -569,18 +571,30 @@
     def piece_of(i, o):
         return 4 * (i // 2) + 2 * o + i % 2
 
-    def stream(i):
+    def stream_up(i):
         copies = []
         for o in range(2):
             at = piece_of(i, o) * chunk
             at = at if isinstance(at, int) else pl.multiple_of(at, chunk)
-            here = pl.ds(o * chunk, chunk)
-            copies.append(pltpu.make_async_copy(w_up.at[:, pl.ds(at, chunk)], wu.at[:, here], wsem.at[0, o]))
-            copies.append(pltpu.make_async_copy(w_down.at[pl.ds(at, chunk)], wd.at[here], wsem.at[1, o]))
+            copies.append(
+                pltpu.make_async_copy(w_up.at[:, pl.ds(at, chunk)], wu.at[:, pl.ds(o * chunk, chunk)], wsem.at[0, o])
+            )
         return copies
 
-    for copy in stream(0):
-        copy.start()
+    def stream_down(i, to, which):
+        copies = []
+        for o in range(2):
+            at = piece_of(i, o) * chunk
+            at = at if isinstance(at, int) else pl.multiple_of(at, chunk)
+            copies.append(pltpu.make_async_copy(w_down.at[pl.ds(at, chunk)], to.at[pl.ds(o * chunk, chunk)], wsem.at[which, o]))
+        return copies
+
+    def stream(i):
+        return stream_up(i) + stream_down(i, wd, 1)
+
+    for i, to in ((0, wu), (1, wd)):
+        for copy in stream_down(i, to, i):
+            copy.start()
 
     bar = pltpu.get_barrier_semaphore()
     for k in peers:
@@ -631,6 +645,21 @@
     loads[3].wait()
     loads[4].wait()
     ct_t[:, pl.ds(0, wide)] = jnp.transpose(ct[...])
+    kept_rows = (((0,), 0, 384), ((1, 0, 0), 384, 96), ((1, 0, 1, 0), 480, 48))
+    for i in range(n_chunk):
+        to = (wu, wd)[i % 2]
+        for copy in stream_down(i, to, i % 2):
+            copy.wait()
+        for o in range(2):
+            grad_active = dot_nt(ct[...], to[pl.ds(o * chunk, chunk), :]).astype(BF)
+            for where, first, count in kept_rows:
+                kept = gu.at[(i, o) + where]
+                kept[...] = grad_active[first : first + count].reshape(kept.shape)
+        if i + 2 < n_chunk:
+            for copy in stream_down(i + 2, to, i % 2):
+                copy.start()
+    for copy in stream(0):
+        copy.start()
     halo.wait()
     norm_to(half, half, attn_gain, attn_shift)
     project_rows(half, half)
@@ -666,7 +695,7 @@
         lse_t[pl.ds(2 * p + 1, 1), :] = logsum[:, glob:]
         return carry
 
-    lax.fori_loop(0, pairs, glob_forward, 0)
+    lax.fori_loop(0, pairs, glob_forward, 0, unroll=True)
 
     lse = jnp.transpose(lse_t[...])
     in_heads = lanes_of((glob, 128)) < HEADS
@@ -687,24 +716,31 @@
         sends1.append(copy)
     rcv1[0] = msg1[pl.ds(my_slots, slots), :]
 
-    def local_forward_pair(p, carry):
+    def scores_to(slot, p, mask):
         at = pl.multiple_of(p * 128, 128)
         keys = jnp.concatenate([proj[:, pl.ds(width + at, 128)], kaug[...]], axis=1)
-        qp = proj[pl.ds(0, tok), pl.ds(at, 128)]
-        for e, mask in ((0, even), (1, odd)):
-            queries = jnp.concatenate([qp * mask, qaug[pl.ds(0, tok), :]], axis=1)
-            scores = dot_nt(keys, queries)
-            top = jnp.max(scores, axis=0, keepdims=True)
-            raised = jnp.exp(scores - top)
-            inverse = 1.0 / jnp.sum(raised, axis=0, keepdims=True)
-            weights = raised.astype(BF)
-            probs[p, :, pl.ds(e * tok, tok)] = weights
-            rl_t[pl.ds(2 * p + e, 1), :] = inverse
-            here = pl.multiple_of(at + e * HEAD_DIM, HEAD_DIM)
-            mixed = dot_nn(kvt[pl.ds(here, HEAD_DIM), pl.ds(0, rows)], weights)
-            att_t[pl.ds(here, HEAD_DIM), pl.ds(0, tok)] = (mixed * inverse).astype(BF)
+        queries = jnp.concatenate([proj[pl.ds(0, tok), pl.ds(at, 128)] * mask, qaug[pl.ds(0, tok), :]], axis=1)
+        score[slot][:, pl.ds(0, tok)] = dot_nt(keys, queries)
+
+    def softmax_of(slot, p):
+        values = score[slot][:, pl.ds(0, tok)]
+        raised = jnp.exp(values - jnp.max(values, axis=0, keepdims=True))
+        inverse = 1.0 / jnp.sum(raised, axis=0, keepdims=True)
+        weights = raised.astype(BF)
+        probs[p, :, pl.ds(slot * tok, tok)] = weights
+        rl_t[pl.ds(2 * p + slot, 1), :] = inverse
+        here = pl.multiple_of(p * 128 + slot * HEAD_DIM, HEAD_DIM)
+        mixed = dot_nn(kvt[pl.ds(here, HEAD_DIM), pl.ds(0, rows)], weights)
+        att_t[pl.ds(here, HEAD_DIM), pl.ds(0, tok)] = (mixed * inverse).astype(BF)
+
+    def local_forward_pair(p, carry):
+        scores_to(1, p, odd)
+        softmax_of(0, p)
+        scores_to(0, jnp.minimum(p + 1, pairs - 1), even)
+        softmax_of(1, p)
         return carry
 
+    scores_to(0, 0, even)
     lax.fori_loop(0, pairs, local_forward_pair, 0)
     att[pl.ds(0, tok), :] = jnp.transpose(att_t[:, pl.ds(0, tok)])
 
@@ -733,7 +769,8 @@
     ).astype(BF)
 
     loads[5].wait()
-    x2[...] = dot_nn(att[...], wo[...])
+    for first in range(0, width, 256):
+        x2[:, pl.ds(first, 256)] = dot_nn(att[...], wo[:, pl.ds(first, 256)])
     x2[pl.ds(0, tok), :] += sec[pl.ds(0, tok), :].astype(F32)
     x2[pl.ds(tok, slots), :] += sec[pl.ds(pl.multiple_of(tok + my_slots, slots), slots), :].astype(F32)
 
@@ -750,13 +787,13 @@
         return remote(gd.at[i, :, :, 1 - c], r0d.at[i], d0s.at[i], d0r.at[i], dev_c)
 
     def d_y(i):
-        return remote(r0d.at[i, :, 1 - y], r1d.at[i // 2, i % 2], d1s.at[i], d1r.at[i], dev_y)
+        return remote(r0d.at[i, :, 1 - y], r1d.at[i], d1s.at[i], d1r.at[i], dev_y)
+
+    def d_1(i):
+        return remote(r1d.at[i, 1 - zl], r2d.at[i // 2, i % 2], d2s.at[i], d2r.at[i], dev_1)
 
     def d_x(h):
-        return remote(r1d.at[h, 1 - x], r2d.at[h], d2s.at[h], d2r.at[h], dev_x)
-
-    def d_1(h):
-        return remote(r2d.at[h, 1 - zl], r3d.at[h], d3s.at[h], d3r.at[h], dev_1)
+        return remote(r2d.at[h, 1 - x], r3d.at[h], d3s.at[h], d3r.at[h], dev_x)
 
     def d_2():
         return remote(r3d.at[1 - zh], r4d, d4s.at[0], d4r.at[0], dev_2)
@@ -766,58 +803,71 @@
         r0d[i] = r0d[i] + gd[i, :, :, c]
         d_y(i).start()
 
+    def do_d_1(i):
+        d_y(i).wait_recv()
+        r1d[i] = r1d[i] + r0d[i, :, y]
+        d_1(i).start()
+
     def do_d_x(h):
         for j in range(2):
-            d_y(2 * h + j).wait_recv()
-            r1d[h, j] = r1d[h, j] + r0d[2 * h + j, :, y]
+            d_1(2 * h + j).wait_recv()
+            r2d[h, j] = r2d[h, j] + r1d[2 * h + j, zl]
         d_x(h).start()
-
-    def do_d_1(h):
-        d_x(h).wait_recv()
-        r2d[h] = r2d[h] + r1d[h, x]
-        d_1(h).start()
 
     def do_d_2():
         for h in range(2):
-            d_1(h).wait_recv()
-            r3d[h] = r3d[h] + r2d[h, zl]
+            d_x(h).wait_recv()
+            r3d[h] = r3d[h] + r2d[h, x]
         d_2().start()
 
     def u_core(i):
         return remote(gu.at[i, 1 - c], r0u.at[i], u0s.at[i], u0r.at[i], dev_c)
 
-    def u_1(i):
-        return remote(r0u.at[i, :, 1 - zl], r1u.at[i], u1s.at[i], u1r.at[i], dev_1)
-
-    def u_x(i):
-        return remote(r1u.at[i, :, 1 - x], r2u.at[i // 2, i % 2], u2s.at[i], u2r.at[i], dev_x)
-
-    def u_y():
-        return remote(r2u.at[1 - y], r3u, u3s.at[0], u3r.at[0], dev_y)
-
-    def u_2():
-        return remote(r3u.at[:, 1 - zh], r4u, u4s.at[0], u4r.at[0], dev_2)
-
-    def do_u_1(i):
+    def u_a(i, z_first):
+        src, dev = (r0u.at[i, :, 1 - zl], dev_1) if z_first else (r0u.at[i, :, :, 1 - x], dev_x)
+        return remote(src, r1u.at[i], u1s.at[i], u1r.at[i], dev)
+
+    def u_b(i):
+        src, dev = (r1u.at[i, :, 1 - x], dev_x) if i == 0 else (r1u.at[i, :, 1 - zl], dev_1)
+        return remote(src, r2u.at[i // 2, i % 2], u2s.at[i], u2r.at[i], dev)
+
+    def u_y(j):
+        return remote(r2u.at[1 - y, j], r3u.at[j], u3s.at[j], u3r.at[j], dev_y)
+
+    def u_2(j):
+        return remote(r3u.at[j, 1 - zh], r4u.at[j], u4s.at[j], u4r.at[j], dev_2)
+
+    def do_u_a(i):
         u_core(i).wait_recv()
         r0u[i] = r0u[i] + gu[i, c]
-        u_1(i).start()
-
-    def do_u_x(i):
-        u_1(i).wait_recv()
-        r1u[i] = r1u[i] + r0u[i, :, zl]
-        u_x(i).start()
-
-    def do_u_y():
-        for i in range(4):
-            u_x(i).wait_recv()
-            r2u[i // 2, i % 2] = r2u[i // 2, i % 2] + r1u[i, :, x]
-        u_y().start()
-
-    def do_u_2():
-        u_y().wait_recv()
-        r3u[...] = r3u[...] + r2u[y]
-        u_2().start()
+        if isinstance(i, int):
+            u_a(i, i == 0).start()
+            return
+
+        @pl.when(i == 0)
+        def _():
+            u_a(i, True).start()
+
+        @pl.when(i > 0)
+        def _():
+            u_a(i, False).start()
+
+    def do_u_b(i):
+        u_a(i, i == 0).wait_recv()
+        r1u[i] = r1u[i] + (r0u[i, :, zl] if i == 0 else r0u[i, :, :, x])
+        u_b(i).start()
+
+    def do_u_y(j):
+        for yy in range(2):
+            i = 2 * yy + j
+            u_b(i).wait_recv()
+            r2u[yy, j] = r2u[yy, j] + r1u[i, :, x if i == 0 else zl]
+        u_y(j).start()
+
+    def do_u_2(j):
+        u_y(j).wait_recv()
+        r3u[j] = r3u[j] + r2u[y, j]
+        u_2(j).start()
 
     vec[...] = jnp.zeros_like(vec)
     for i in range(n_chunk):
@@ -830,52 +880,82 @@
     gh = kvt
     cuts = ((0, 256, ((0, 0, 0, 256),)), (256, 256, ((0, 256, 0, 128), (1, 0, 128, 128))), (512, 256, ((1, 128, 0, 256),)))
 
+    def hidden_at(n):
+        return (hid_a, hid_b)[n % 2]
+
     def ffn_step(i, carry):
         for copy in stream(i):
             copy.wait()
-        for first, count, _ in cuts:
-            here = pl.ds(first, count)
-            hidden = dot_nn(n2[...], wu[:, here]) + ub[pl.ds(i, 1), here]
-            active, slope = gelu_pair(hidden)
-            act[:, here] = active.astype(BF)
-            grad_hidden = (slope * dot_nt(ct[...], wd[here, :])).astype(BF)
-            gh[pl.ds(0, wide), here] = grad_hidden
-            ub[pl.ds(i, 1), here] = jnp.sum(grad_hidden.astype(F32), axis=0, keepdims=True)
-
-        @pl.when(i >= 1)
-        def _():
-            do_d_y(i - 1)
-            do_u_1(i - 1)
-
-        @pl.when(i >= 2)
-        def _():
-            do_u_x(i - 2)
-
-        @pl.when(i == 3)
-        def _():
-            do_d_x(0)
-
-        for first, count, _ in cuts:
-            here = pl.ds(first, count)
-            acc[:, here] += dot_nn(act[...], wd[:, here])
-            gn2[:, here] += dot_nt(gh[pl.ds(0, wide), :], wu[here, :])
-
-        @pl.when(i + 1 < n_chunk)
-        def _():
-            for copy in stream(i + 1):
-                copy.start()
-
-        for first, count, parts in cuts:
+
+        def up(n):
+            here = pl.ds(cuts[n][0], 256)
+            hidden_at(n)[...] = dot_nn(n2[...], wu[:, here]) + ub[pl.ds(i, 1), here]
+
+        def activate(n):
+            here = pl.ds(cuts[n][0], 256)
+            total = jnp.zeros((1, 256), F32)
+            for where, first, count in kept_rows:
+                row = pl.ds(first, count)
+                active, slope = gelu_pair(hidden_at(n)[row, :])
+                act[row, here] = active.astype(BF)
+                grad_active = jnp.concatenate(
+                    [
+                        gu[(i, o) + where + (slice(None),) * (5 - len(where)) + (pl.ds(at, size),)].reshape(count, size)
+                        for o, at, _, size in cuts[n][2]
+                    ],
+                    axis=1,
+                )
+                grad_hidden = (slope * grad_active.astype(F32)).astype(BF)
+                gh[row, here] = grad_hidden
+                total = total + jnp.sum(grad_hidden.astype(F32), axis=0, keepdims=True)
+            ub[pl.ds(i, 1), here] = total
+
+        def down_terms(n):
+            first, count, parts = cuts[n]
             block = dot_nn(ct_t[:, pl.ds(0, wide)], act[:, pl.ds(first, count)]).astype(BF)
             for o, at, start, size in parts:
                 gd[i, o, :, :, :, pl.ds(at, size)] = block[:, start : start + size].reshape(2, 2, side, size)
-        d_core(i).start()
-        for first, count, parts in cuts:
+
+        def up_terms(n):
+            first, count, parts = cuts[n]
             block = dot_nn(n2t[:, pl.ds(0, wide)], gh[pl.ds(0, wide), pl.ds(first, count)]).astype(BF)
             for o, at, start, size in parts:
                 gu[i, o, :, :, :, :, :, pl.ds(at, size)] = block[:, start : start + size].reshape(
                     2, 2, 2, 2, part // 2, size
                 )
+
+        up(0)
+        activate(0)
+        up(1)
+        down_terms(0)
+        activate(1)
+        up(2)
+        down_terms(1)
+        activate(2)
+        for first, count, _ in cuts:
+            here = pl.ds(first, count)
+            acc[:, here] += dot_nn(act[...], wd[:, here])
+            gn2[:, here] += dot_nt(gh[pl.ds(0, wide), :], wu[here, :])
+
+        @pl.when(i + 1 < n_chunk)
+        def _():
+            for copy in stream(i + 1):
+                copy.start()
+
+        @pl.when(i >= 1)
+        def _():
+            do_d_y(i - 1)
+            do_u_a(i - 1)
+
+        @pl.when(i == 3)
+        def _():
+            do_u_b(0)
+            do_d_1(0)
+
+        down_terms(2)
+        for n in range(3):
+            up_terms(n)
+        d_core(i).start()
         u_core(i).start()
 
         return carry
@@ -931,8 +1011,9 @@
         sends2.append(copy)
     rcv2[pl.ds(my_slots, slots), :] = msg1[pl.ds(0, slots), :]
     do_d_y(3)
-    do_u_1(3)
-    do_u_x(2)
+    do_u_a(3)
+    do_d_1(1)
+    do_u_b(1)
 
     n2t[:, pl.ds(0, tok)] = jnp.transpose(nrm[pl.ds(0, tok), :])
     n2t[:, pl.ds(tok, glob)] = jnp.transpose(nrm[pl.ds(tok, glob), :])
@@ -968,7 +1049,7 @@
         return remote(chunk_at(p).at[:, 1 - c], r0q.at[p], q0s.at[p], q0r.at[p], dev_c)
 
     def x_first(p):
-        return p % 2 == 1
+        return p in (1, 7)
 
     def q_a(p):
         src, dev = (r0q.at[p, :, 1 - x], dev_x) if x_first(p) else (r0q.at[p, :, :, 1 - y], dev_y)
@@ -1056,6 +1137,95 @@
         u_core(i).wait_send()
     for h in range(2):
         put_chunk(pairs + h, dot_nn(att_t[:, pl.ds(0, wide)], n2[:, pl.ds(h * 384, 384)]))
+
+    minus = jnp.where(lanes_of((rows, 128)) < 32, -1.0, 0.0).astype(BF)
+    factor = HEAD_DIM ** (-0.5)
+
+    def chosen(head):
+        lane = lanes_of((1, 128))
+        return jnp.where((lane == head) | (lane == head + 16), 1.0, 0.0).astype(BF)
+
+    def values_of(at):
+        return jnp.concatenate([proj[:, pl.ds(2 * width + at, 128)], minus], axis=1)
+
+    def parts_at(p):
+        return acc_full.at[:, pl.ds(pl.multiple_of(lax.rem(p, 3) * 256, 256), 256)]
+
+    def token_queries(p):
+        at = pl.multiple_of(p * 128, 128)
+        values = values_of(at)
+        qp = proj[pl.ds(0, tok), pl.ds(at, 128)]
+        gp = gatt[pl.ds(0, tok), pl.ds(at, 128)]
+        ups = jnp.concatenate([gp * even_one, gp * odd_one], axis=0)
+        dd = qaug[pl.ds(0, tok), :]
+        inner = jnp.concatenate([dd * chosen(2 * p), dd * chosen(2 * p + 1)], axis=0)
+        own = pl.ds(0, 2 * tok)
+        parts_at(p)[:, 128:] = dot_nn(probs[p, :, own], ups)
+        for first in range(0, 2 * tok, 256):
+            right = jnp.concatenate([ups[first : first + 256], inner[first : first + 256]], axis=1)
+            grad_w = dot_nt(values, right)
+            here = probs[p, :, pl.ds(first, 256)].astype(F32)
+            probs[p, :, pl.ds(first, 256)] = (here * grad_w).astype(BF)
+        parts_at(p)[:, :128] = dot_nn(probs[p, :, own], jnp.concatenate([qp * even, qp * odd], axis=0))
+        low = dot_nn(kvt[pl.ds(at, HEAD_DIM), pl.ds(0, rows)], probs[p, :, pl.ds(0, tok)])
+        upper = dot_nn(
+            kvt[pl.ds(pl.multiple_of(at + HEAD_DIM, HEAD_DIM), HEAD_DIM), pl.ds(0, rows)],
+            probs[p, :, pl.ds(tok, tok)],
+        )
+        grad_q = jnp.concatenate([low, upper], axis=0) * factor
+        proj[pl.ds(0, tok), pl.ds(at, 128)] = jnp.transpose(grad_q).astype(BF)
+
+    def glob_queries(p):
+        at = pl.multiple_of(p * 128, 128)
+        qg = proj[pl.ds(tok, glob), pl.ds(at, 128)]
+        gg = rcv2[:, pl.ds(at, 128)]
+        dg = rcv2[:, pl.ds(width, 128)]
+        ups = jnp.concatenate([gg * even_one, gg * odd_one], axis=0)
+        inner = jnp.concatenate([dg * chosen(2 * p), dg * chosen(2 * p + 1)], axis=0)
+        weights = probs[p, :, pl.ds(2 * tok, 2 * glob)]
+        grad_v = parts_at(p)[:, 128:] + dot_nn(weights, ups)
+        grad_w = dot_nt(values_of(at), jnp.concatenate([ups, inner], axis=1))
+        grad_s = (weights.astype(F32) * grad_w).astype(BF)
+        grad_k = parts_at(p)[:, :128] + dot_nn(grad_s, jnp.concatenate([qg * even, qg * odd], axis=0))
+        own = dot_nn(kvt[pl.ds(at, 128), pl.ds(0, rows)], grad_s)
+        own = jnp.where(first_head, own[:, :glob], own[:, glob:]) * factor
+        proj[pl.ds(tok, glob), pl.ds(at, 128)] = jnp.transpose(own).astype(BF)
+        proj[:, pl.ds(width + at, 128)] = grad_k.astype(BF)
+        proj[:, pl.ds(2 * width + at, 128)] = grad_v.astype(BF)
+
+    def at_steps(p, steps):
+        for step, act in steps:
+
+            @pl.when(p == step)
+            def _(act=act):
+                act()
+
+    def first_pairs(p, carry):
+        token_queries(p)
+        return carry
+
+    def middle_pairs(p, carry):
+        token_queries(p)
+        glob_queries(p - 2)
+        q_chunk(p - 2)
+        at_steps(p, (
+            (2, lambda: (do_d_1(3), do_u_b(3), do_d_x(0))),
+            (3, lambda: (do_q_a(0), do_u_y(0), do_q_b(6, 7))),
+            (4, lambda: (do_q_a(1), do_d_x(1), do_u_y(1))),
+            (5, lambda: (do_q_a(2), do_q_b(0), do_u_2(0), do_q_1(6, 7))),
+        ))
+        return carry
+
+    def last_pairs(p, carry):
+        glob_queries(p)
+        q_chunk(p)
+        at_steps(p, ((4, lambda: (do_q_a(3), do_q_b(1), do_d_2())), (5, lambda: (do_q_a(4), do_u_2(1), do_q_2(6, 7), do_q_1(0)))))
+        return carry
+
+    lax.fori_loop(0, 2, first_pairs, 0)
+    do_d_1(2)
+    do_u_b(2)
+    do_q_a(6, 7)
     for copy in sends2:
         copy.wait()
     sends_o = []
@@ -1066,62 +1236,8 @@
         copy.start()
         sends_o.append(copy)
 
-    minus = jnp.where(lanes_of((rows, 128)) < 32, -1.0, 0.0).astype(BF)
-
-    def chosen(head):
-        lane = lanes_of((1, 128))
-        return jnp.where((lane == head) | (lane == head + 16), 1.0, 0.0).astype(BF)
-
-    def attention_back(p, carry):
-        at = pl.multiple_of(p * 128, 128)
-        qp = proj[pl.ds(0, tok), pl.ds(at, 128)]
-        qg = proj[pl.ds(tok, glob), pl.ds(at, 128)]
-        gp = gatt[pl.ds(0, tok), pl.ds(at, 128)]
-        gg = rcv2[:, pl.ds(at, 128)]
-        dg = rcv2[:, pl.ds(width, 128)]
-        values = jnp.concatenate([proj[:, pl.ds(2 * width + at, 128)], minus], axis=1)
-        ups = jnp.concatenate([gp * even_one, gp * odd_one, gg * even_one, gg * odd_one], axis=0)
-        dd = qaug[pl.ds(0, tok), :]
-        sel_e, sel_o = chosen(2 * p), chosen(2 * p + 1)
-        inner = jnp.concatenate([dd * sel_e, dd * sel_o, dg * sel_e, dg * sel_o], axis=0)
-        qs = jnp.concatenate([qp * even, qp * odd, qg * even, qg * odd], axis=0)
-        grad_v = dot_nn(probs[p], ups)
-        for first, count in ((0, tok), (tok, tok), (2 * tok, 2 * glob)):
-            right = jnp.concatenate([ups[first : first + count], inner[first : first + count]], axis=1)
-            grad_w = dot_nt(values, right)
-            here = probs[p, :, pl.ds(first, count)].astype(F32)
-            probs[p, :, pl.ds(first, count)] = (here * grad_w).astype(BF)
-        grad_k = dot_nn(probs[p], qs)
-        factor = HEAD_DIM ** (-0.5)
-        low = dot_nn(kvt[pl.ds(at, HEAD_DIM), pl.ds(0, rows)], probs[p, :, pl.ds(0, tok)])
-        upper = dot_nn(
-            kvt[pl.ds(pl.multiple_of(at + HEAD_DIM, HEAD_DIM), HEAD_DIM), pl.ds(0, rows)], probs[p, :, pl.ds(tok, tok)]
-        )
-        grad_q = jnp.concatenate([low, upper], axis=0) * factor
-        own = dot_nn(kvt[pl.ds(at, 128), pl.ds(0, rows)], probs[p, :, pl.ds(2 * tok, 2 * glob)])
-        own = jnp.where(first_head, own[:, :glob], own[:, glob:]) * factor
-        proj[pl.ds(tok, glob), pl.ds(at, 128)] = jnp.transpose(own).astype(BF)
-        proj[pl.ds(0, tok), pl.ds(at, 128)] = jnp.transpose(grad_q).astype(BF)
-        proj[:, pl.ds(width + at, 128)] = grad_k.astype(BF)
-        proj[:, pl.ds(2 * width + at, 128)] = grad_v.astype(BF)
-
-        q_chunk(p)
-        for at_step, act in (
-            (0, lambda: (do_d_x(1), do_u_x(3), do_q_a(6, 7))),
-            (1, lambda: (do_d_1(0), do_d_1(1), do_u_y(), do_q_a(0))),
-            (2, lambda: (do_d_2(), do_q_a(1))),
-            (3, lambda: (do_u_2(), do_q_a(2), do_q_b(6, 7))),
-            (4, lambda: (do_q_a(3), do_q_b(0))),
-            (5, lambda: (do_q_a(4), do_q_b(1), do_q_1(6, 7))),
-        ):
-
-            @pl.when(p == at_step)
-            def _(act=act):
-                act()
-
-        return carry
-
-    lax.fori_loop(0, pairs, attention_back, 0)
+    lax.fori_loop(2, pairs, middle_pairs, 0)
+    lax.fori_loop(pairs - 2, pairs, last_pairs, 0)
 
     def first_pull(first):
         grad, gain_term, shift_term = norm_pull(
@@ -1134,45 +1250,56 @@
     gnm = wu
     gnm[pl.ds(0, glob), :] = dot_nt(proj[pl.ds(tok, glob), :], wq[...]).astype(BF)
     sends3 = []
-    for k in peers:
+    for k in (1, 2, 3):
         other = flip(k)
-        at = pl.multiple_of(other * slots, slots)
-        copy = remote(gnm.at[pl.ds(at, slots)], rcv3.at[k - 1], m3s.at[k], m3r.at[k], (other, b))
-        copy.start()
-        sends3.append(copy)
+        for h in range(2):
+            at = pl.multiple_of((4 * h + lax.rem(other, 4)) * slots, slots)
+            copy = remote(
+                gnm.at[pl.ds(at, slots)], rcv3.at[k - 1, h], m3s.at[2 * k - 2 + h], m3r.at[2 * k - 2 + h], (other, b)
+            )
+            copy.start()
+            sends3.append(copy)
     do_q_plane()
     gn2[pl.ds(half, half), :] = dot_nt(proj[pl.ds(half, half), :], wq[...])
     for r in range(half, tok, 128):
         first_pull(r)
     do_q_b(2, 3)
-    do_q_1(0, 1)
-    do_q_2(6, 7)
+    do_q_1(1)
+    do_q_2(0)
+    for copy in sends3:
+        copy.wait()
+
+    def slots_of(h):
+        mine = gnm[pl.ds(pl.multiple_of((4 * h + lax.rem(s, 4)) * slots, slots), slots), :].astype(F32)
+        for k in (1, 2, 3):
+            mine = mine + rcv3[k - 1, h].astype(F32)
+        return mine
+
+    gsum[...] = slots_of(1 - zh).astype(BF)
+    line3 = remote(gsum, rcv3b, m3s.at[6], m3r.at[6], dev_2)
+    line3.start()
 
     gn2[pl.ds(0, half), :] = dot_nt(proj[pl.ds(0, half), :], wq[...])
     for r in range(0, half, 128):
         first_pull(r)
     keep = pltpu.make_async_copy(n2.at[pl.ds(0, half)], o_tgrad.at[pl.ds(half, half)], osem.at[2])
     keep.start()
+    do_q_line()
     do_q_b(4)
-    do_q_line()
-
-    grad_slots = gnm[pl.ds(my_slots, slots), :].astype(F32)
-    for copy in sends3:
-        copy.wait()
-    for k in peers:
-        grad_slots = grad_slots + rcv3[k - 1].astype(F32)
+    do_q_1(2, 3)
+    do_q_2(1)
+
+    line3.wait()
     grad, gain_term, shift_term = norm_pull(
         sec[pl.ds(pl.multiple_of(tok + my_slots, slots), slots), :].astype(F32),
         glob_gain,
-        grad_slots,
+        slots_of(zh) + rcv3b[...].astype(F32),
     )
     vec[pl.ds(2, 1), :] += gain_term
     vec[pl.ds(3, 1), :] += shift_term
     n2[pl.ds(tok, slots), :] = (grad + x2[pl.ds(tok, slots), :]).astype(BF)
-    own_grad = pltpu.make_async_copy(
-        n2.at[pl.ds(tok, slots)], o_ggrad.at[pl.ds(my_slots, slots)], osem.at[3]
-    )
-    own_grad.start()
+    line_g = remote(n2.at[pl.ds(tok, slots)], gall, ggs_s.at[0], ggs_r.at[0], dev_2)
+    line_g.start()
 
     share = vec.shape[1] // n_seq
     for j in range(n_seq):
@@ -1188,16 +1315,8 @@
         copy.start()
         sends_v.append(copy)
 
-    sends_g = []
-    for k in peers:
-        copy = remote(
-            n2.at[pl.ds(tok, slots)], o_ggrad.at[pl.ds(my_slots, slots)], ggs_s.at[k], ggs_r.at[k],
-            (flip(k), b),
-        )
-        copy.start()
-        sends_g.append(copy)
-    do_q_1(2, 3)
-    do_q_2(0, 1)
+    do_q_1(4)
+    do_q_2(2, 3)
     back = remote(
         n2.at[pl.ds(half, half)], o_tgrad.at[pl.ds(0, half)], hs2.at[0], hr2.at[0],
         (lax.rem(s + 1, n_seq), b),
@@ -1205,14 +1324,32 @@
     back.start()
 
     d_2().wait_recv()
-    o_down[...] = r4d[...].astype(F32) + r3d[zh].astype(F32)
-    u_2().wait_recv()
+    acc[pl.ds(96, 192), pl.ds(0, 384)] = r4d[...].astype(F32) + r3d[zh].astype(F32)
+    for j in range(2):
+        u_2(j).wait_recv()
     last = r4u[...].astype(F32) + r3u[:, zh].astype(F32)
-    o_up[:, pl.ds(0, 384)] = last[0].reshape(96, 384)
-    o_up[:, pl.ds(384, 384)] = last[1].reshape(96, 384)
-
-    do_q_1(4)
-    do_q_2(2, 3)
+    acc[pl.ds(0, 96), pl.ds(0, 384)] = last[0].reshape(96, 384)
+    acc[pl.ds(0, 96), pl.ds(384, 384)] = last[1].reshape(96, 384)
+    results = [
+        pltpu.make_async_copy(acc.at[pl.ds(0, 96)], o_up, osem.at[4]),
+        pltpu.make_async_copy(acc.at[pl.ds(96, 192), pl.ds(0, 384)], o_down, osem.at[5]),
+    ]
+    for copy in results:
+        copy.start()
+
+    line_g.wait()
+    far_slots = pl.multiple_of(flip(4) * slots, slots)
+    sends_g = []
+    for n, (src, at) in enumerate(((n2.at[pl.ds(tok, slots)], my_slots), (gall, far_slots))):
+        copy = pltpu.make_async_copy(src, o_ggrad.at[pl.ds(at, slots)], gsem.at[n])
+        copy.start()
+        sends_g.append(copy)
+        for k in (1, 2, 3):
+            copy = remote(
+                src, o_ggrad.at[pl.ds(at, slots)], ggs_s.at[2 * k + n - 1], ggs_r.at[2 * k + n - 1], (flip(k), b)
+            )
+            copy.start()
+            sends_g.append(copy)
 
     for copy in sends_v:
         copy.wait()
@@ -1229,7 +1366,7 @@
     do_q_2(4)
 
     def final(n, slot):
-        return remote(fmsg.at[n], frcv.at[slot], fs.at[n], fr.at[n], (s, flip_b(n)))
+        return remote(fmsg.at[n - 1], frcv.at[slot], fs.at[n], fr.at[n], (s, flip_b(n)))
 
     def flip_b(n):
         return (b, dev_c[1], dev_y[1], dev_cy[1])[n]
@@ -1258,7 +1395,7 @@
             return jnp.concatenate(tiles, axis=1)
 
         for n in (3, 2, 1):
-            fmsg[n] = columns_of(flip_b(n))
+            fmsg[n - 1] = columns_of(flip_b(n))
             final(n, y).start()
         frcv[y] = columns_of(b)
 
@@ -1281,21 +1418,28 @@
     for yy in range(2):
         block = frcv[yy].astype(F32)
         main = block[:, :640]
-        o_qkv[pl.ds(yy * 48, 48), :] = jnp.where(c == 1, pltpu.roll(main, 576, 1), main)[:, :576]
+        acc[pl.ds(288 + yy * 48, 48), pl.ds(0, 640)] = jnp.where(c == 1, pltpu.roll(main, 576, 1), main)
         main = block[:, 640:]
-        o_wout[pl.ds(yy * 48, 48), :] = jnp.where(c == 1, pltpu.roll(main, 192, 1), main)[:, :192]
+        acc[pl.ds(384 + yy * 48, 48), pl.ds(0, 256)] = jnp.where(c == 1, pltpu.roll(main, 192, 1), main)
+    for copy in (
+        pltpu.make_async_copy(acc.at[pl.ds(288, 96), pl.ds(0, 640)], o_qkv, osem.at[6]),
+        pltpu.make_async_copy(acc.at[pl.ds(384, 96), pl.ds(0, 256)], o_wout, osem.at[7]),
+    ):
+        copy.start()
+        results.append(copy)
 
     for i in range(4):
         d_core(i).wait_send()
         d_y(i).wait_send()
-        u_1(i).wait_send()
-        u_x(i).wait_send()
+        d_1(i).wait_send()
+        u_a(i, i == 0).wait_send()
+        u_b(i).wait_send()
     for h in range(2):
         d_x(h).wait_send()
-        d_1(h).wait_send()
     d_2().wait_send()
-    u_y().wait_send()
-    u_2().wait_send()
+    for j in range(2):
+        u_y(j).wait_send()
+        u_2(j).wait_send()
     for p in range(8):
         q_core(p).wait_send()
         if p != 5:
@@ -1321,9 +1465,10 @@
 
     back.wait()
     keep.wait()
-    own_grad.wait()
     out_copy.wait()
     own_out.wait()
+    for copy in results:
+        copy.wait()
     for copy in sends_o + sends_g:
         copy.wait()
 
@@ -1342,7 +1487,7 @@
 def finish_kernel(*refs):
     ins, outs = refs[:10], refs[10:]
     for i in range(8):
-        outs[i][...] = ins[i][...]
+        outs[i][...] = ins[i][:, : outs[i].shape[1]]
     for i in range(7):
         outs[8 + i][...] = ins[8][i, :]
     outs[15][...] = ins[9][0, :]
@@ -1379,23 +1524,24 @@
         low(rows, width), low(rows, width), low(rows, 3 * width), low(width, width),
         low(pairs, rows, 2 * tok + 2 * glob), low(width, tok + 128), low(wide, width), full(wide, width),
         low(wide, width), low(width, tok + 128), low(wide, width), low(width, tok + 128),
-        full(wide, width), full(wide, width), low(wide, width), low(rows, 128), low(rows, 128),
+        full(rows, width), full(rows, width), low(wide, width), low(rows, 128), low(rows, 128),
         low(width, 3 * width), low(width, width), low(width, width), low(width, width),
         full(128, glob), full(16, tok), full(glob, width), low(glob, width + 128),
         low(n_seq, slots, width + 128), low(glob, width + 128),
-        low(n_seq - 1, slots, width),
+        low(3, 2, slots, width), low(slots, width), low(slots, width), low(slots, width),
         full(16, width), full(n_seq, 16, 128), full(n_seq - 1, 16, 128), full(4, 16, 128), full(4, width),
-        low(4, 2, 2, 2, side, chunk), low(4, 2, 2, side, chunk), low(2, 2, 2, side, chunk), low(2, 2, side, chunk),
+        low(4, 2, 2, 2, side, chunk), low(4, 2, 2, side, chunk), low(4, 2, side, chunk), low(2, 2, side, chunk),
         low(2, side, chunk), low(side, chunk),
         low(4, 2, *eighth, 2, part // 2, chunk), low(4, *eighth, 2, part // 2, chunk), low(4, 2, 2, 2, part // 2, chunk),
         low(2, 2, 2, 2, part // 2, chunk), low(2, 2, 2, part // 2, chunk), low(2, 2, part // 2, chunk),
         low(8, 2, 2, 2, part // 2, chunk), low(8, 2, 2, part // 2, chunk), low(8, 2, part // 2, chunk),
         low(8, 2, part // 2, chunk), low(8, part // 2, chunk),
-        low(4, part // 2, 896), low(2, part // 2, 896),
+        low(3, part // 2, 896), low(2, part // 2, 896),
+        full(wide, 256), full(wide, 256),
         dma((8,)), dma((2, 2)), dma((1,)), dma((1,)),
         *[dma((8,)) for _ in range(10)], dma((9,)), dma((9,)),
         *[dma((4,)) for _ in range(10)], *[dma((4,)) for _ in range(10)], *[dma((8,)) for _ in range(10)],
-        *[dma((3,)) for _ in range(6)], dma((4,)), dma((4,)), dma((1,)), dma((1,)), dma((4,)),
+        *[dma((3,)) for _ in range(6)], dma((4,)), dma((4,)), dma((1,)), dma((1,)), dma((8,)), dma((2,)),
     ]
 
     results = pl.pallas_call(
@@ -1405,8 +1551,8 @@
             jax.ShapeDtypeStruct((glob, width), BF),
             jax.ShapeDtypeStruct((tok, width), BF),
             jax.ShapeDtypeStruct((glob, width), BF),
-            jax.ShapeDtypeStruct((part, 3 * side), F32),
-            jax.ShapeDtypeStruct((part, side), F32),
+            jax.ShapeDtypeStruct((part, 640), F32),
+            jax.ShapeDtypeStruct((part, 256), F32),
             jax.ShapeDtypeStruct((part, 2 * chunk), F32),
             jax.ShapeDtypeStruct((side, chunk), F32),
             jax.ShapeDtypeStruct((8, part), F32),
@@ -1414,7 +1560,7 @@
         ],
         in_specs=[any_space(), any_space(), vmem(), vmem(), vmem(), vmem(), vmem(), vmem(), any_space(), any_space(),
                   vmem(), vmem(), any_space(), vmem(), any_space(), vmem(), any_space(), any_space()],
-        out_specs=[any_space()] * 4 + [vmem()] * 6,
+        out_specs=[any_space()] * 8 + [vmem()] * 2,
         scratch_shapes=scratch,
         compiler_params=pltpu.CompilerParams(
             collective_id=0, has_side_effects=True, vmem_limit_bytes=64 * 1024 * 1024
@@ -1426,9 +1572,12 @@
         out_cotangent[0], global_cotangent[0],
     )
     *large, vectors, ub = results
+    columns = {4: 3 * side, 5: side}
     results = pl.pallas_call(
         finish_kernel,
-        out_shape=[jax.ShapeDtypeStruct(one.shape, one.dtype) for one in large]
+        out_shape=[
+            jax.ShapeDtypeStruct((one.shape[0], columns.get(i, one.shape[1])), one.dtype) for i, one in enumerate(large)
+        ]
         + [jax.ShapeDtypeStruct((part,), F32)] * 7
         + [jax.ShapeDtypeStruct((chunk,), F32)],
         in_specs=[vmem()] * 10,

time: 145 us -> 134 us (0.924); the launches traced: 145 us -> 132 us
  Pallas kernels: 144 us -> 131 us
    pallas_call x1, Pallas kernels: 141 us -> 127 us  [fused(): pl.pallas_call(layer_kernel, out_shape=[jax.ShapeDtypeStruct((tok, width)...]
where the time goes in v4:
time: 134 us; the launch traced here: 132 us
  Pallas kernels  131 us (98%)
    pallas_call x1, Pallas kernels, fused(): pl.pallas_call(layer_kernel, out_shape=[jax.ShapeDtypeStruct((tok, width)...  127 us
    pallas_call x1, Pallas kernels, fused(): pl.pallas_call(finish_kernel, out_shape=[jax.ShapeDtypeStruct((one.shape[...  3.47 us

profile of v4, /device:TPU:2, one launch (start us, length us, event | category | flops | bytes accessed | tf_op | source)
XLA Modules:
  0.0 131.5 jit_solution(1884044298906142228)
XLA Ops:
  0.7 127.2 %layer.1 = (bf16[512,768]{1,0:T(8,128)(2,1)}, bf16[128,768]{1,0:T(8,128)(2,1)}, bf16[512,768]{1,0:T(8,128)(2,1)}, bf16[128,768]{1,0:T(8,128)(2,1)}, f32[96,640]{...) custom-call(bf16[512,768]{1,0:T(8,128)(2,1)} %bitcast.9, ...), custom_call_target="tpu_custom_call" | custom-call | tf_op jit(solution)/shard_map/layer/pallas_call | solution.py:1547
  127.9 3.5 %results.1 = (bf16[512,768]{1,0:T(8,128)(2,1)}, bf16[128,768]{1,0:T(8,128)(2,1)}, bf16[512,768]{1,0:T(8,128)(2,1)}, bf16[128,768]{1,0:T(8,128)(2,1)}, f32[96,576...) custom-call(bf16[512,768]{1,0:T(8,128)(2,1)} %get-tuple-element.42.r, ...), custom_call_target="tpu_custom_call" | custom-call | tf_op jit(solution)/shard_map/results/pallas_call | solution.py:1576

commit v5 on v4

--- a/solution.py
+++ b/solution.py
@@ -744,6 +744,18 @@
     lax.fori_loop(0, pairs, local_forward_pair, 0)
     att[pl.ds(0, tok), :] = jnp.transpose(att_t[:, pl.ds(0, tok)])
 
+    loads[5].wait()
+
+    def second_norm(first, count):
+        spread, scale = norm_stats(x2[pl.ds(first, count), :])
+        n2[pl.ds(first, count), :] = (spread * scale * ffn_gain + ffn_shift).astype(BF)
+
+    for first in range(0, width, 256):
+        here = pl.ds(first, 256)
+        x2[pl.ds(0, tok), here] = dot_nn(att[pl.ds(0, tok), :], wo[:, here]) + sec[pl.ds(0, tok), here].astype(F32)
+    for r in range(0, tok, 128):
+        second_norm(r, 128)
+
     head_of = lanes_of((128, width)) // HEAD_DIM
     spread_heads = jnp.where(head_of == lax.broadcasted_iota(jnp.int32, (128, width), 0), 1.0, 0.0).astype(BF)
     for copy in sends1:
@@ -768,18 +780,9 @@
         jnp.concatenate([mixed, jnp.zeros((tail - slots, width), F32)], axis=0)
     ).astype(BF)
 
-    loads[5].wait()
-    for first in range(0, width, 256):
-        x2[:, pl.ds(first, 256)] = dot_nn(att[...], wo[:, pl.ds(first, 256)])
-    x2[pl.ds(0, tok), :] += sec[pl.ds(0, tok), :].astype(F32)
-    x2[pl.ds(tok, slots), :] += sec[pl.ds(pl.multiple_of(tok + my_slots, slots), slots), :].astype(F32)
-
-    def second_norm(first, count):
-        spread, scale = norm_stats(x2[pl.ds(first, count), :])
-        n2[pl.ds(first, count), :] = (spread * scale * ffn_gain + ffn_shift).astype(BF)
-
-    for r in range(0, tok, 128):
-        second_norm(r, 128)
+    x2[pl.ds(tok, slots), :] = dot_nn(att[pl.ds(tok, slots), :], wo[...]) + sec[
+        pl.ds(pl.multiple_of(tok + my_slots, slots), slots), :
+    ].astype(F32)
     second_norm(tok, slots)
     n2t[:, pl.ds(0, wide)] = jnp.transpose(n2[...])
 
@@ -1269,6 +1272,37 @@
     for copy in sends3:
         copy.wait()
 
+    quarter = half // 2
+    after, after_relay = (lax.rem(s + 1, n_seq), b), (lax.rem(s + 2, n_seq), b)
+    relay = ct.at[pl.ds(0, quarter)]
+
+    def back(n):
+        part_n = pl.ds(n * quarter, quarter)
+        return remote(n2.at[pl.ds(half + n * quarter, quarter)], o_tgrad.at[part_n], hs2.at[n], hr2.at[n], after)
+
+    def back_to_relay():
+        return remote(n2.at[pl.ds(half + quarter, quarter)], relay, hs2.at[1], hr2.at[2], dev_x)
+
+    def back_from_relay():
+        return remote(relay, o_tgrad.at[pl.ds(quarter, quarter)], hs2.at[2], hr2.at[1], after_relay)
+
+    def start_back():
+        back(0).start()
+
+        @pl.when(x == 0)
+        def _():
+            back(1).start()
+
+        @pl.when(x == 1)
+        def _():
+            back_to_relay().start()
+
+    def pass_back_on():
+        @pl.when(x == 0)
+        def _():
+            back_to_relay().wait_recv()
+            back_from_relay().start()
+
     def slots_of(h):
         mine = gnm[pl.ds(pl.multiple_of((4 * h + lax.rem(s, 4)) * slots, slots), slots), :].astype(F32)
         for k in (1, 2, 3):
@@ -1288,6 +1322,11 @@
     do_q_b(4)
     do_q_1(2, 3)
     do_q_2(1)
+
+    @pl.when(s == n_seq - 1)
+    def _():
+        start_back()
+
 
     line3.wait()
     grad, gain_term, shift_term = norm_pull(
@@ -1317,11 +1356,6 @@
 
     do_q_1(4)
     do_q_2(2, 3)
-    back = remote(
-        n2.at[pl.ds(half, half)], o_tgrad.at[pl.ds(0, half)], hs2.at[0], hr2.at[0],
-        (lax.rem(s + 1, n_seq), b),
-    )
-    back.start()
 
     d_2().wait_recv()
     acc[pl.ds(96, 192), pl.ds(0, 384)] = r4d[...].astype(F32) + r3d[zh].astype(F32)
@@ -1365,6 +1399,15 @@
 
     do_q_2(4)
 
+    @pl.when(s != n_seq - 1)
+    def _():
+        start_back()
+
+    @pl.when(s == n_seq - 2)
+    def _():
+        pass_back_on()
+
+
     def final(n, slot):
         return remote(fmsg.at[n - 1], frcv.at[slot], fs.at[n], fr.at[n], (s, flip_b(n)))
 
@@ -1398,6 +1441,10 @@
             fmsg[n - 1] = columns_of(flip_b(n))
             final(n, y).start()
         frcv[y] = columns_of(b)
+
+    @pl.when(s != n_seq - 2)
+    def _():
+        pass_back_on()
 
     for copy in sends_b:
         copy.wait()
@@ -1463,7 +1510,13 @@
         for p in (6, 7, 0, 1, 2, 3, 4):
             q_1(p).wait_send()
 
-    back.wait()
+    back(0).wait()
+    back(1).wait()
+
+    @pl.when(x == 0)
+    def _():
+        back_from_relay().wait_send()
+
     keep.wait()
     out_copy.wait()
     own_out.wait()
@@ -1541,7 +1594,7 @@
         dma((8,)), dma((2, 2)), dma((1,)), dma((1,)),
         *[dma((8,)) for _ in range(10)], dma((9,)), dma((9,)),
         *[dma((4,)) for _ in range(10)], *[dma((4,)) for _ in range(10)], *[dma((8,)) for _ in range(10)],
-        *[dma((3,)) for _ in range(6)], dma((4,)), dma((4,)), dma((1,)), dma((1,)), dma((8,)), dma((2,)),
+        *[dma((3,)) for _ in range(6)], *[dma((4,)) for _ in range(4)], dma((8,)), dma((2,)),
     ]
 
     results = pl.pallas_call(

time: 134 us -> 132 us (0.985)
  Pallas kernels: 131 us -> 129 us
    pallas_call x1, Pallas kernels: 127 us -> 126 us  [fused(): pl.pallas_call(layer_kernel, out_shape=[jax.ShapeDtypeStruct((tok, width)...]
where the time goes in v5:
time: 132 us; the launch traced here: 130 us
  Pallas kernels  129 us (98%)
    pallas_call x1, Pallas kernels, fused(): pl.pallas_call(layer_kernel, out_shape=[jax.ShapeDtypeStruct((tok, width)...  126 us
    pallas_call x1, Pallas kernels, fused(): pl.pallas_call(finish_kernel, out_shape=[jax.ShapeDtypeStruct((one.shape[...  3.47 us

profile of v5, /device:TPU:2, one launch (start us, length us, event | category | flops | bytes accessed | tf_op | source)
XLA Modules:
  0.0 130.2 jit_solution(2143092127673229508)
XLA Ops:
  0.7 125.8 %layer.1 = (bf16[512,768]{1,0:T(8,128)(2,1)}, bf16[128,768]{1,0:T(8,128)(2,1)}, bf16[512,768]{1,0:T(8,128)(2,1)}, bf16[128,768]{1,0:T(8,128)(2,1)}, f32[96,640]{...) custom-call(bf16[512,768]{1,0:T(8,128)(2,1)} %bitcast.9, ...), custom_call_target="tpu_custom_call" | custom-call | tf_op jit(solution)/shard_map/layer/pallas_call | solution.py:1600
  126.5 3.5 %results.1 = (bf16[512,768]{1,0:T(8,128)(2,1)}, bf16[128,768]{1,0:T(8,128)(2,1)}, bf16[512,768]{1,0:T(8,128)(2,1)}, bf16[128,768]{1,0:T(8,128)(2,1)}, f32[96,576...) custom-call(bf16[512,768]{1,0:T(8,128)(2,1)} %get-tuple-element.42.r, ...), custom_call_target="tpu_custom_call" | custom-call | tf_op jit(solution)/shard_map/results/pallas_call | solution.py:1629

commit v6 on v5

--- a/solution.py
+++ b/solution.py
@@ -1052,7 +1052,7 @@
         return remote(chunk_at(p).at[:, 1 - c], r0q.at[p], q0s.at[p], q0r.at[p], dev_c)
 
     def x_first(p):
-        return p in (1, 7)
+        return p in (1, 3, 7)
 
     def q_a(p):
         src, dev = (r0q.at[p, :, 1 - x], dev_x) if x_first(p) else (r0q.at[p, :, :, 1 - y], dev_y)

time: 132 us -> 132 us (level)
  the two profiles are of different devices: /device:TPU:2 before, /device:TPU:0 now
where the time goes in v6:
time: 132 us
  Pallas kernels  131 us (99%)
    pallas_call x1, Pallas kernels, fused(): pl.pallas_call(layer_kernel, out_shape=[jax.ShapeDtypeStruct((tok, width)...  127 us
    pallas_call x1, Pallas kernels, fused(): pl.pallas_call(finish_kernel, out_shape=[jax.ShapeDtypeStruct((one.shape[...  3.47 us

profile of v6, /device:TPU:0, one launch (start us, length us, event | category | flops | bytes accessed | tf_op | source)
XLA Modules:
  0.0 131.7 jit_solution(8474506542903881573)
XLA Ops:
  0.7 127.4 %layer.1 = (bf16[512,768]{1,0:T(8,128)(2,1)}, bf16[128,768]{1,0:T(8,128)(2,1)}, bf16[512,768]{1,0:T(8,128)(2,1)}, bf16[128,768]{1,0:T(8,128)(2,1)}, f32[96,640]{...) custom-call(bf16[512,768]{1,0:T(8,128)(2,1)} %bitcast.9, ...), custom_call_target="tpu_custom_call" | custom-call | tf_op jit(solution)/shard_map/layer/pallas_call | solution.py:1600
  128.0 3.5 %results.1 = (bf16[512,768]{1,0:T(8,128)(2,1)}, bf16[128,768]{1,0:T(8,128)(2,1)}, bf16[512,768]{1,0:T(8,128)(2,1)}, bf16[128,768]{1,0:T(8,128)(2,1)}, f32[96,576...) custom-call(bf16[512,768]{1,0:T(8,128)(2,1)} %get-tuple-element.42.r, ...), custom_call_target="tpu_custom_call" | custom-call | tf_op jit(solution)/shard_map/results/pallas_call | solution.py:1629
